TPU v7x, 256 devices: a whole 4x4x8 slice. The times are simulated.
256 devices in a mesh: dp: 32 (over y, x, core), mp: 8 (over z).
Axes of the slice: x: 4, y: 4, z: 8, core: 2. Of those that a mesh axis runs over, the one named last changes fastest.
Arguments:
- gradient: bfloat16 [96, 1024, 1024], P(None, 'dp', 'mp'), may hold values from -0.19921875 to 0.19921875
- slot_block: int32 [96], replicated, may hold values from 0 to 95, each once
- first_moment: float32 [96, 1024, 1024], P(None, 'dp', 'mp')
- second_moment: float32 [96, 1024, 1024], P(None, 'dp', 'mp'), may hold values from 0.0001 to 0.01
- left_stat: float32 [96, 1024, 1024], P('dp', 'mp')
- right_stat: float32 [96, 1024, 1024], P('dp', 'mp')
- left_root: bfloat16 [96, 1024, 1024], P('dp', 'mp')
- right_root: bfloat16 [96, 1024, 1024], P('dp', 'mp')
Outputs:
- update: bfloat16 [96, 1024, 1024], P(None, 'dp', 'mp')
- left_new: float32 [96, 1024, 1024], P('dp', 'mp')
- right_new: float32 [96, 1024, 1024], P('dp', 'mp')
Inputs may be any that keep to these rules, and one draw needn't show every extreme that they name: `slot_block`: every block number appears exactly once.
All inputs are finite; a program needn't handle non-finite values. Where the computation divides by a largest or mean magnitude, that divisor is 1e-20 or more.
Results may differ from a plain program's by a relative error of at most 0.0061.
Values may be sent and summed in bfloat16 or wider, within the bound.
No kernel may reach another device: no remote copies, remote signals or barrier semaphores. Data moves between devices by JAX's collectives and lax.ppermute only.
A program may use at most 128 MiB of HBM per device.

v0:
```python
import jax
import jax.numpy as jnp
from jax import lax
from jax.sharding import PartitionSpec as P

BETA_ONE = 0.9
BETA_TWO = 0.999
ADAM_EPS = 1e-08
STAT_DECAY = 0.9
CLIP_LIMIT = 1.0
NORM_EPS = 1e-06


def shards(
    gradient, slot_block, first_moment, second_moment, left_stat, right_stat, left_root, right_root
):
    block_total = gradient.shape[0]
    owned_count = left_stat.shape[0]
    factor_rows = left_stat.shape[1]
    grad_wide = gradient.astype(jnp.float32)
    moment_one = BETA_ONE * first_moment + (1.0 - BETA_ONE) * grad_wide
    moment_two = BETA_TWO * second_moment + (1.0 - BETA_TWO) * grad_wide * grad_wide
    adam = moment_one / (jnp.sqrt(moment_two) + ADAM_EPS)
    adam_sq = lax.psum(jnp.sum(adam * adam, axis=(1, 2)), ("dp", "mp"))
    ordered = jnp.take(gradient, slot_block, axis=0)
    widened = lax.all_gather(ordered, "mp", axis=2, tiled=True)
    blocks = lax.all_to_all(widened, "dp", split_axis=0, concat_axis=1, tiled=True)
    offset = lax.axis_index("mp") * factor_rows
    owned_rows = lax.dynamic_slice_in_dim(blocks, offset, factor_rows, 1)
    owned_cols = lax.dynamic_slice_in_dim(blocks, offset, factor_rows, 2)
    left_part = jnp.einsum("sik,sjk->sij", owned_rows, blocks, preferred_element_type=jnp.float32)
    right_part = jnp.einsum("ski,skj->sij", owned_cols, blocks, preferred_element_type=jnp.float32)
    left_new = STAT_DECAY * left_stat + (1.0 - STAT_DECAY) * left_part
    right_new = STAT_DECAY * right_stat + (1.0 - STAT_DECAY) * right_part
    half_done = jnp.einsum(
        "sik,skj->sij", left_root, blocks, preferred_element_type=jnp.float32
    ).astype(jnp.bfloat16)
    precond = jnp.einsum(
        "sik,skj->sij",
        half_done,
        lax.all_gather(right_root, "mp", axis=1, tiled=True),
        preferred_element_type=jnp.float32,
    )
    pre_sq = lax.psum(jnp.sum(precond * precond, axis=(1, 2)), "mp")
    counter = jnp.arange(block_total, dtype=jnp.int32)
    owned_ids = lax.dynamic_slice_in_dim(
        slot_block, lax.axis_index("dp") * owned_count, owned_count
    )
    matches = owned_ids[:, None] == counter[None, :]
    adam_slot = jnp.sum(jnp.where(matches, adam_sq[None, :], 0.0), axis=1)
    graft = precond * (jnp.sqrt(adam_slot) / jnp.sqrt(pre_sq + NORM_EPS))[:, None, None]
    inverse = jnp.sum(
        jnp.where(slot_block[:, None] == counter[None, :], counter[:, None], 0), axis=0
    )
    by_rows = lax.all_to_all(
        lax.all_to_all(graft, "mp", split_axis=2, concat_axis=1, tiled=True),
        "dp",
        split_axis=1,
        concat_axis=0,
        tiled=True,
    )
    largest = lax.pmax(jnp.max(jnp.abs(by_rows)), ("dp", "mp"))
    restored = jnp.take(by_rows, inverse, axis=0)
    update = (restored * jnp.minimum(1.0, CLIP_LIMIT / largest)).astype(jnp.bfloat16)
    return (update, left_new, right_new)


def solution(mesh):
    return jax.shard_map(
        shards,
        mesh=mesh,
        in_specs=(
            P(None, "dp", "mp"),
            P(),
            P(None, "dp", "mp"),
            P(None, "dp", "mp"),
            P("dp", "mp", None),
            P("dp", "mp", None),
            P("dp", "mp", None),
            P("dp", "mp", None),
        ),
        out_specs=(P(None, "dp", "mp"), P("dp", "mp", None), P("dp", "mp", None)),
        check_vma=False,
    )
```

profile of v0, /device:TPU:1, one launch (start us, length us, event | category | flops | bytes accessed | tf_op | source)
XLA Modules:
  0.0 459.7 jit_solution(8323807380268230275)
XLA Ops:
  8.6 1.8 gather_fusion
  10.5 1.1 broadcast_select_fusion
  12.3 81.2 %all-gather.3.cloned.1.call-done = bf16[96,32,1024]{2,1,0:T(8,128)(2,1)} async-done(((bf16[96,32,128]{2,1,0:T(8,128)(2,1)}), bf16[96,32,1024]{2,1,0:T(8,128)(2,1)}) %all-gather.3.cloned.1.call-update) | async-done | bytes 6291472 | tf_op jit(solution)/shard_map/all_gather | solution.py:26
  93.5 10.8 %all-to-all-start = ((bf16[96,32,1024]{2,1,0:T(8,128)(2,1)}), bf16[96,32,1024]{2,1,0:T(8,128)(2,1)}, u32[]{:S(2)}, u32[]{:S(2)}) async-start(bf16[96,32,1024]{2,1,0:T(8,128)(2,1)} %all-gather.3.cloned.1.call-done), calls=%async_computation | async-start | bytes 12582912 | tf_op jit(solution)/shard_map/all_to_all | solution.py:27
  104.4 2.7 fusion.6
  107.2 138.3 %psum.14 = f32[96]{0:T(128)S(1)} all-reduce(f32[96]{0:T(128)S(1)} %fusion.6), channel_id=1, replica_groups=mesh['dp'=32,'mp'=8] {'dp','mp'}, use_global_device_ids=true, to_apply=%region_2.3 | all-reduce | flops 96 | bytes 768 | tf_op jit(solution)/shard_map/psum | solution.py:24
  245.7 6.8 %copy.43 = bf16[3,32,32,1024]{3,2,1,0:T(8,128)(2,1)} copy(bf16[3,32,32,1024]{3,2,0,1:T(8,128)(2,1)} %bitcast.1) | data formatting | bytes 12582912 | tf_op jit(solution)/shard_map/all_to_all | solution.py:27
  252.4 7.9 %multiply_reduce_fusion = (f32[3]{0:T(128)S(1)}, f32[3,128,1024]{2,1,0:T(8,128)S(1)}) fusion(bf16[3,1024,1024]{2,1,0:T(8,128)(2,1)} %all-gather.5.cloned.1.call-done, bf16[3,1024,1024]{2,1,0:T(8,128)(2,1)} %bitcast.21, bf16[3,128,1024]{2,1,0:T(8,128)(2,1)S(1)} %copy-done), kind=kOutput, calls=%fused_computation.14 | convolution fusion | flops 1611792384 | bytes 14942220 | tf_op jit(solution)/shard_map/sik,skj->sij/dot_general | solution.py:38
  260.3 12.4 %psum.15 = f32[3]{0:T(128)S(1)} all-reduce(f32[3]{0:T(128)S(1)} %get-tuple-element.3), channel_id=1, replica_groups=mesh['dp'=32,'mp'=8] {'mp'}, use_global_device_ids=true, to_apply=%region_5.6 | all-reduce | flops 3 | bytes 24 | tf_op jit(solution)/shard_map/psum | solution.py:44
  272.7 1.4 broadcast_multiply_fusion
  274.1 2.8 copy.46
  276.9 3.7 all-to-all-start.1
  280.7 47.6 %all-to-all-done.1 = f32[3,128,1024]{1,0,2:T(4,128)S(1)} async-done(((f32[3,128,1024]{1,0,2:T(4,128)}), f32[3,128,1024]{1,0,2:T(4,128)S(1)}, u32[]{:S(2)}, u32[]{:S(2)}) %all-to-all-start.1) | async-done | bytes 1572896 | tf_op jit(solution)/shard_map/all_to_all | solution.py:56
  328.4 1.2 copy.47
  329.6 1.9 copy.48
  331.5 2.5 copy.49
  334.0 8.9 %all-to-all-start.2 = ((f32[3,1024,128]{2,0,1:T(4,128)}), f32[3,1024,128]{2,0,1:T(4,128)}, u32[]{:S(2)}, u32[]{:S(2)}) async-start(f32[3,1024,128]{2,0,1:T(4,128)} %copy.49), calls=%async_computation.2 | async-start | bytes 4194304 | tf_op jit(solution)/shard_map/all_to_all | solution.py:55
  342.9 6.0 %multiply_add_fusion = f32[3,128,1024]{2,1,0:T(8,128)} fusion(f32[3,128,1024]{2,1,0:T(8,128)} %param.13, bf16[3,1024,1024]{2,1,0:T(8,128)(2,1)} %bitcast.22, s32[]{:T(128)S(6)} %select_n.51), kind=kOutput, calls=%fused_computation.10 | convolution fusion | flops 806486016 | bytes 10223620 | tf_op jit(solution)/shard_map/ski,skj->sij/dot_general | solution.py:32
  349.0 3.4 multiply_add_fusion.1
  352.4 18.3 %all-to-all-done.2 = f32[3,1024,128]{2,0,1:T(4,128)} async-done(((f32[3,1024,128]{2,0,1:T(4,128)}), f32[3,1024,128]{2,0,1:T(4,128)}, u32[]{:S(2)}, u32[]{:S(2)}) %all-to-all-start.2) | async-done | bytes 1572896 | tf_op jit(solution)/shard_map/all_to_all | solution.py:55
  370.7 1.7 copy.50
  373.3 74.5 %pmax.7 = f32[]{:T(128)} all-reduce(f32[]{:T(128)} %abs_reduce_fusion), channel_id=1, replica_groups=mesh['dp'=32,'mp'=8] {'dp','mp'}, use_global_device_ids=true, to_apply=%region_7.8 | all-reduce | flops 1 | bytes 8 | tf_op jit(solution)/shard_map/pmax | solution.py:62
  448.4 1.9 gather_fusion.1
  450.3 2.5 multiply_convert_fusion
  (33 shorter events, 3.5 us)
Async XLA Ops:
  7.2 245.3 %copy-start = (bf16[3,128,1024]{2,1,0:T(8,128)(2,1)S(1)}, bf16[3,128,1024]{2,1,0:T(8,128)(2,1)}, u32[]{:S(2)}) copy-start(bf16[3,128,1024]{2,1,0:T(8,128)(2,1)} %param.14) | copy-start | bytes 2359300
  7.2 86.3 %all-gather.3.cloned.1.call-start = ((), (), s32[]{:S(2)}) async-start(), calls=%async_computation.3 | async-start | bytes 7077888 | tf_op jit(solution)/shard_map/all_gather | solution.py:26
  11.6 240.9 %all-gather.5.cloned.1.call-start = ((), (), s32[]{:S(2)}) async-start(), calls=%async_computation.4 | async-start | bytes 7077888 | tf_op jit(solution)/shard_map/all_gather | solution.py:41
  12.3 92.0 %copy-start.4 = (s32[96]{0:T(128)S(1)}, s32[96]{0:T(128)}, u32[]{:S(2)}) copy-start(s32[96]{0:T(128)} %param.9) | copy-start | bytes 1156
  12.3 92.1 %copy-start.1 = (bf16[96,32,128]{2,1,0:T(8,128)(2,1)S(1)}, bf16[96,32,128]{2,1,0:T(8,128)(2,1)}, u32[]{:S(2)}) copy-start(bf16[96,32,128]{2,1,0:T(8,128)(2,1)} %param.8) | copy-start | bytes 2359300
  12.3 92.1 %copy-start.3 = (f32[96,32,128]{2,1,0:T(8,128)S(1)}, f32[96,32,128]{2,1,0:T(8,128)}, u32[]{:S(2)}) copy-start(f32[96,32,128]{2,1,0:T(8,128)} %param.11) | copy-start | bytes 4718596
  93.5 152.2 %all-to-all-start = ((bf16[96,32,1024]{2,1,0:T(8,128)(2,1)}), bf16[96,32,1024]{2,1,0:T(8,128)(2,1)}, u32[]{:S(2)}, u32[]{:S(2)}) async-start(bf16[96,32,1024]{2,1,0:T(8,128)(2,1)} %all-gather.3.cloned.1.call-done), calls=%async_computation | async-start | bytes 12582912 | tf_op jit(solution)/shard_map/all_to_all | solution.py:27
  276.9 51.5 %all-to-all-start.1 = ((f32[3,128,1024]{1,0,2:T(4,128)}), f32[3,128,1024]{1,0,2:T(4,128)S(1)}, u32[]{:S(2)}, u32[]{:S(2)}) async-start(f32[3,128,1024]{1,0,2:T(4,128)} %copy.46), calls=%async_computation.1 | async-start | bytes 4194304 | tf_op jit(solution)/shard_map/all_to_all | solution.py:56
  334.0 15.0 %slice-start = ((s8[6291456]{0:T(1024)(128)(4,1)}), s8[2097152]{0:T(1024)(128)(4,1)S(1)}, s32[]{:S(2)}) async-start(s8[6291456]{0:T(1024)(128)(4,1)} %bitcast.23), calls=%async_computation.5 | async-start | bytes 4194304
  334.0 36.7 %all-to-all-start.2 = ((f32[3,1024,128]{2,0,1:T(4,128)}), f32[3,1024,128]{2,0,1:T(4,128)}, u32[]{:S(2)}, u32[]{:S(2)}) async-start(f32[3,1024,128]{2,0,1:T(4,128)} %copy.49), calls=%async_computation.2 | async-start | bytes 4194304 | tf_op jit(solution)/shard_map/all_to_all | solution.py:55
  342.9 6.1 %slice-start.1 = ((s8[6291456]{0:T(1024)(128)(4,1)}), s8[4194304]{0:T(1024)(128)(4,1)S(1)}, s32[]{:S(2)}) async-start(s8[6291456]{0:T(1024)(128)(4,1)} %bitcast.23), calls=%async_computation.6 | async-start | bytes 8388608
  342.9 6.1 %copy-start.2 = (f32[3,128,1024]{2,1,0:T(8,128)S(1)}, f32[3,128,1024]{2,1,0:T(8,128)}, u32[]{:S(2)}) copy-start(f32[3,128,1024]{2,1,0:T(8,128)} %param.12) | copy-start | bytes 4718596
Sparse Core Ops, SparseCore 0:
  11.7 81.7 all-gather.2
  95.3 76.1 all-gather.4
where the time goes:
time: 460 us
  blocking collectives  225 us (49%)
  waiting for transfers between devices  148 us (32%)
  starting transfers between devices  23.6 us (5%)
  local copies, waits for them, and re-layouts  20.8 us (5%)
  matrix products  17.3 us (4%)
  between operations  14.9 us (3%)
  other arithmetic  10.1 us (2%)
    psum x1, blocking collectives, shards(): adam_sq = lax.psum(jnp.sum(adam * adam, axis=(1, 2)), ('dp', 'mp'))  138 us
    all_gather x1, waiting for transfers between devices, shards(): widened = lax.all_gather(ordered, 'mp', axis=2, tiled=True)  81.2 us
    pmax x1, blocking collectives, shards(): largest = lax.pmax(jnp.max(jnp.abs(by_rows)), ('dp', 'mp'))  74.5 us
    all_to_all x1, waiting for transfers between devices, shards(): lax.all_to_all(graft, 'mp', split_axis=2, concat_axis=1, tiled=True)  47.6 us
    all_to_all x1, waiting for transfers between devices, shards(): lax.all_to_all(lax.all_to_all(graft, 'mp', split_axis=2, concat_axis=1, t...  18.3 us
    psum x1, blocking collectives, shards(): pre_sq = lax.psum(jnp.sum(precond * precond, axis=(1, 2)), 'mp')  12.4 us
    all_to_all x1, starting transfers between devices, shards(): lax.all_to_all(widened, 'dp', split_axis=0, concat_axis=1, tiled=True)  10.8 us
  transfers between devices with their start and end apart: 5, of which 3 were waited for; matrix products, arithmetic and copies ran while one was open for 4% of the time, Pallas kernels for 0%

commit v1 on v0

v1 whole, which is shorter than its diff:
```python
import functools

import jax
import jax.numpy as jnp
from jax import lax
from jax.experimental import pallas as pl
from jax.experimental.pallas import tpu as pltpu
from jax.sharding import PartitionSpec as P

BETA_ONE = 0.9
BETA_TWO = 0.999
ADAM_EPS = 1e-08
STAT_DECAY = 0.9
CLIP_LIMIT = 1.0
NORM_EPS = 1e-06
PAD = 16
F32 = jnp.float32
BF16 = jnp.bfloat16
SMEM = pltpu.SMEM


def params():
    return pltpu.CompilerParams(vmem_limit_bytes=60 * 1024 * 1024)


def scalars():
    return pl.BlockSpec(memory_space=SMEM)


def whole(shape):
    return pl.BlockSpec(tuple(shape), lambda g: (0,) * len(shape))


def slot_of(shape):
    return pl.BlockSpec((None,) + tuple(shape[1:]), lambda g: (g,) + (0,) * (len(shape) - 1))


def cost(flops, nbytes):
    return pl.CostEstimate(flops=int(flops), bytes_accessed=int(nbytes), transcendentals=0)


def split_rows(values):
    row = lax.broadcasted_iota(jnp.int32, (PAD, 128), 0)
    tile = jnp.zeros((PAD, 128), F32)
    for k, value in enumerate(values):
        high = value.astype(BF16).astype(F32)
        rest = value - high
        middle = rest.astype(BF16).astype(F32)
        low = rest - middle
        for at, piece in enumerate((high, middle, low)):
            tile = jnp.where(row == 3 * k + at, jnp.broadcast_to(piece, (PAD, 128)), tile)
    return tile.astype(BF16)


def joined(tile, k):
    return tile[3 * k : 3 * k + 1] + tile[3 * k + 1 : 3 * k + 2] + tile[3 * k + 2 : 3 * k + 3]


def prepare_kernel(count, slot_ref, grad_ref, one_ref, two_ref, out_ref):
    rows = grad_ref.shape[1]

    def body(owner, _):
        parts = []
        for i in range(count):
            block = slot_ref[owner * count + i]
            grad = grad_ref[block]
            out_ref[owner, i * rows : (i + 1) * rows, :] = grad
            wide = grad.astype(F32)
            moment_one = BETA_ONE * one_ref[block] + (1.0 - BETA_ONE) * wide
            moment_two = BETA_TWO * two_ref[block] + (1.0 - BETA_TWO) * wide * wide
            adam = moment_one / (jnp.sqrt(moment_two) + ADAM_EPS)
            parts.append(jnp.sum(adam * adam, axis=0, keepdims=True))
        out_ref[owner, count * rows :, :] = split_rows(parts)
        return 0

    lax.fori_loop(0, out_ref.shape[0], body, 0)


def prepare(count, owners, slot_block, gradient, first_moment, second_moment):
    rows = gradient.shape[1]
    return pl.pallas_call(
        functools.partial(prepare_kernel, count),
        out_shape=jax.ShapeDtypeStruct((owners, count * rows + PAD, 128), BF16),
        grid=(1,),
        in_specs=[scalars()] + [whole(gradient.shape)] * 3,
        out_specs=whole((owners, count * rows + PAD, 128)),
        compiler_params=params(),
        cost_estimate=cost(20 * gradient.size, 12 * gradient.size),
        name="prepare",
    )(slot_block, gradient, first_moment, second_moment)


def unpack_kernel(got_ref, ring_ref, adam_ref):
    count, order = ring_ref.shape[:2]
    rows = order // got_ref.shape[0]
    for i in range(count):
        ring_ref[i] = got_ref[:, i * rows : (i + 1) * rows, :].reshape(order, 128)
    at = count * rows
    total = got_ref[0, at:, :].astype(F32)
    for d in range(1, got_ref.shape[0]):
        total = total + got_ref[d, at:, :].astype(F32)
    adam_ref[...] = total


def unpack(count, got):
    order = (got.shape[1] - PAD) // count * got.shape[0]
    shape = (count, order, 128)
    return pl.pallas_call(
        unpack_kernel,
        out_shape=[
            jax.ShapeDtypeStruct(shape, BF16),
            jax.ShapeDtypeStruct((PAD, 128), F32),
        ],
        grid=(1,),
        in_specs=[whole(got.shape)],
        out_specs=[whole(shape), whole((PAD, 128))],
        compiler_params=params(),
        cost_estimate=cost(0, 4 * got.size),
        name="unpack",
    )(got)


class RingPanels:
    def __init__(self, place, refs):
        self.place = place
        self.refs = refs

    def place_of(self, k):
        return lax.rem(self.place + k, 8)

    def rows(self, k, low, high):
        if k != 4:
            return self.refs[k if k < 4 else k + 1][low:high, :]
        upper, lower = self.refs[4:6]
        half = upper.shape[0]
        if high <= half:
            return upper[low:high, :]
        if low >= half:
            return lower[low - half : high - half, :]
        return jnp.concatenate([upper[low:, :], lower[: high - half, :]], axis=0)

    def rows_at(self, k, at):
        if k != 4:
            return self.refs[k if k < 4 else k + 1][pl.ds(at, 128), :]
        upper, lower = self.refs[4:6]
        half = upper.shape[0]
        inside = pl.ds(pl.multiple_of(lax.rem(at, half), 128), 128)
        return jnp.where(at < half, upper[inside, :], lower[inside, :])

    def mine(self):
        return self.refs[0][...]


def pair_of(grads, k, order):
    return jnp.concatenate([grads.rows(2 * k + e, 0, order) for e in range(2)], axis=1)


def precondition_kernel(place_ref, left_ref, adam_ref, *refs):
    out_ref = refs[-1]
    grads, roots = RingPanels(place_ref[0], refs[:9]), refs[9:18]
    order = left_ref.shape[1]
    step = pl.program_id(0)
    base = pl.multiple_of(step * (128 + PAD), PAD)
    left = left_ref[...]
    half = []
    for k in range(4):
        pair = pair_of(grads, k, order)
        half.append(jnp.dot(left, pair, preferred_element_type=F32).astype(BF16))
    half = jnp.concatenate(half, axis=1)
    square = jnp.zeros((1, 128), F32)
    largest = jnp.zeros((1, 128), F32)
    for c in range(4):
        parts = [ref[:, 256 * c : 256 * (c + 1)] for ref in roots]
        pre = jnp.dot(half, jnp.concatenate(parts, axis=0), preferred_element_type=F32)
        for e in range(2):
            piece = pre[:, 128 * e : 128 * (e + 1)]
            out_ref[2 * c + e, pl.ds(base, 128), :] = piece.astype(BF16)
            square = square + jnp.sum(piece * piece, axis=0, keepdims=True)
            largest = jnp.maximum(largest, jnp.max(jnp.abs(piece), axis=0, keepdims=True))
    low = 3 * step
    row = lax.broadcasted_iota(jnp.int32, (PAD, 128), 0)
    inside = (row >= low) & (row < low + 3)
    adam = jnp.sum(jnp.where(inside, adam_ref[...], 0.0), axis=0, keepdims=True)
    tile = split_rows([adam, square, largest])
    tail = pl.multiple_of(base + 128, PAD)
    for k in range(8):
        out_ref[k, pl.ds(tail, PAD), :] = tile


def precondition(place, left_root, adam, grads, roots):
    count, _, order = left_root.shape
    out = (8, count * (128 + PAD), 128)
    return pl.pallas_call(
        precondition_kernel,
        out_shape=jax.ShapeDtypeStruct(out, BF16),
        grid=(count,),
        in_specs=[scalars(), slot_of(left_root.shape), whole(adam.shape)]
        + [slot_of(panel.shape) for panel in (*grads, *roots)],
        out_specs=whole(out),
        compiler_params=params(),
        cost_estimate=cost(count * 4 * 128 * order * order, count * 5 * order * order),
        name="precondition",
    )(place, left_root, adam, *grads, *roots)


def scale_kernel(count, got_ref, out_ref):
    rows = (out_ref.shape[1] - PAD) // count
    step = min(rows, 128)
    scales = []
    peak = jnp.zeros((1, 128), F32)
    for i in range(count):
        base = i * (128 + PAD)
        adam = square = largest = None
        for k in range(8):
            tile = got_ref[k, base + 128 : base + 128 + PAD, :].astype(F32)
            a, s, m = joined(tile, 0), joined(tile, 1), joined(tile, 2)
            adam = a if adam is None else adam + a
            square = s if square is None else square + s
            largest = m if largest is None else jnp.maximum(largest, m)
        adam = jnp.sum(adam, axis=1, keepdims=True)
        square = jnp.sum(square, axis=1, keepdims=True)
        largest = jnp.max(largest, axis=1, keepdims=True)
        scale = jnp.broadcast_to(jnp.sqrt(adam) / jnp.sqrt(square + NORM_EPS), (1, 128))
        scales.append(scale)
        peak = jnp.maximum(peak, scale * jnp.broadcast_to(largest, (1, 128)))
    tile = split_rows(scales + [peak])
    for d in range(out_ref.shape[0]):
        for i in range(count):
            for at in range(0, rows, step):
                row = d * rows + at
                low = i * (128 + PAD) + row % 128
                to = i * rows + at
                out_ref[d, to : to + step, :] = got_ref[row // 128, low : low + step, :]
        out_ref[d, count * rows :, :] = tile


def scale_up(owners, count, order, got):
    out = (owners, count * (order // owners) + PAD, 128)
    return pl.pallas_call(
        functools.partial(scale_kernel, count),
        out_shape=jax.ShapeDtypeStruct(out, BF16),
        grid=(1,),
        in_specs=[whole(got.shape)],
        out_specs=whole(out),
        compiler_params=params(),
        cost_estimate=cost(0, 4 * got.size),
        name="scale",
    )(got)


def finish_kernel(count, slot_ref, got_ref, out_ref):
    rows = out_ref.shape[1]
    owners = got_ref.shape[0]

    def carried(owner, k):
        return joined(got_ref[owner, count * rows :, :].astype(F32), k)

    def find(owner, peak):
        return jnp.maximum(peak, carried(owner, count))

    peak = lax.fori_loop(0, owners, find, jnp.zeros((1, 128), F32))
    clip = jnp.minimum(1.0, CLIP_LIMIT / peak)

    def body(owner, _):
        for i in range(count):
            graft = got_ref[owner, i * rows : (i + 1) * rows, :].astype(F32) * carried(owner, i)
            out_ref[slot_ref[owner * count + i]] = (graft * clip).astype(BF16)
        return 0

    lax.fori_loop(0, owners, body, 0)


def finish(count, slot_block, got):
    out = (slot_block.shape[0], (got.shape[1] - PAD) // count, 128)
    return pl.pallas_call(
        functools.partial(finish_kernel, count),
        out_shape=jax.ShapeDtypeStruct(out, BF16),
        grid=(1,),
        in_specs=[scalars(), whole(got.shape)],
        out_specs=whole(out),
        compiler_params=params(),
        cost_estimate=cost(0, 4 * got.size),
        name="finish",
    )(slot_block, got)


def factors_kernel(place_ref, left_ref, right_ref, *refs):
    left_out, right_out = refs[-2:]
    order = left_ref.shape[1]
    place = place_ref[0]
    grads = RingPanels(place, refs[:9])
    at = pl.multiple_of(place * 128, 128)
    mine = jnp.concatenate([grads.rows_at(k, at) for k in range(8)], axis=1)
    for c in range(4):
        low = 256 * c
        rows = jnp.concatenate([grads.rows(k, low, low + 256) for k in range(8)], axis=1)
        part = lax.dot_general(
            mine, rows, (((1,), (1,)), ((), ())), preferred_element_type=F32
        )
        old = left_ref[:, low : low + 256]
        left_out[:, low : low + 256] = STAT_DECAY * old + (1.0 - STAT_DECAY) * part
    turned = grads.mine().T
    for k in range(4):
        part = jnp.dot(turned, pair_of(grads, k, order), preferred_element_type=F32)
        for e in range(2):
            to = grads.place_of(2 * k + e) * 128
            column = pl.ds(to if isinstance(to, int) else pl.multiple_of(to, 128), 128)
            old = right_ref[:, column]
            new = STAT_DECAY * old + (1.0 - STAT_DECAY) * part[:, 128 * e : 128 * (e + 1)]
            right_out[:, column] = new


def factors(place, left_stat, right_stat, grads):
    count, _, order = left_stat.shape
    return pl.pallas_call(
        factors_kernel,
        out_shape=[jax.ShapeDtypeStruct(left_stat.shape, F32)] * 2,
        grid=(count,),
        in_specs=[scalars(), slot_of(left_stat.shape), slot_of(right_stat.shape)]
        + [slot_of(grad.shape) for grad in grads],
        out_specs=[slot_of(left_stat.shape)] * 2,
        compiler_params=params(),
        cost_estimate=cost(count * 4 * 128 * order * order, count * 4 * order * order),
        name="factors",
    )(place, left_stat, right_stat, *grads)


def ring(own, axis):
    up = [(i, (i + 1) % 8) for i in range(8)]
    down = [(i, (i - 1) % 8) for i in range(8)]
    from_below, from_above = [own], [own]
    for _ in range(3):
        from_below.append(lax.ppermute(from_below[-1], "mp", up))
        from_above.append(lax.ppermute(from_above[-1], "mp", down))
    size = own.shape[axis]
    first = lax.slice_in_dim(from_below[3], 0, size // 2, axis=axis)
    second = lax.slice_in_dim(from_above[3], size // 2, size, axis=axis)
    first = lax.ppermute(first, "mp", up)
    second = lax.ppermute(second, "mp", down)
    return from_above + [first, second] + from_below[:0:-1]


def shards(
    gradient, slot_block, first_moment, second_moment, left_stat, right_stat, left_root, right_root
):
    count, _, order = left_stat.shape
    owners = gradient.shape[0] // count
    place = lax.axis_index("mp").astype(jnp.int32).reshape(1)
    roots = ring(right_root, 1)
    sent = prepare(count, owners, slot_block, gradient, first_moment, second_moment)
    got = lax.all_to_all(sent, "dp", split_axis=0, concat_axis=0, tiled=True)
    own, adam = unpack(count, got)
    own, _ = lax.optimization_barrier((own, (roots[3], roots[6])))
    grads = ring(own, 1)
    sent = precondition(place, left_root, adam, grads, roots)
    got = lax.all_to_all(sent, "mp", split_axis=0, concat_axis=0, tiled=True)
    sent = scale_up(owners, count, order, got)
    got = lax.all_to_all(sent, "dp", split_axis=0, concat_axis=0, tiled=True)
    left_new, right_new = factors(place, left_stat, right_stat, grads)
    update = finish(count, slot_block, got)
    return (update, left_new, right_new)


def solution(mesh):
    return jax.shard_map(
        shards,
        mesh=mesh,
        in_specs=(
            P(None, "dp", "mp"),
            P(),
            P(None, "dp", "mp"),
            P(None, "dp", "mp"),
            P("dp", "mp", None),
            P("dp", "mp", None),
            P("dp", "mp", None),
            P("dp", "mp", None),
        ),
        out_specs=(P(None, "dp", "mp"), P("dp", "mp", None), P("dp", "mp", None)),
        check_vma=False,
    )
```

time: 460 us -> 197 us (0.43)
  blocking collectives: 225 us -> 22.5 us
  waiting for transfers between devices: 148 us -> 91.2 us
  Pallas kernels: 0 us -> 26.7 us
  starting transfers between devices: 23.6 us -> 49.3 us
  matrix products: 17.3 us -> 0 us
  local copies, waits for them, and re-layouts: 20.8 us -> 5.81 us
  between operations: 14.9 us -> 0.74 us
  other arithmetic: 10.1 us -> 0 us
    psum x2 -> x0, blocking collectives: 151 us -> none  [the longest x1 138 us: shards(): adam_sq = lax.psum(jnp.sum(adam * adam, axis=(1, 2)), ('dp', 'mp'))]
    all_gather x2 -> x0, waiting for transfers between devices: 81.2 us -> none  [the longest x1 81.2 us: shards(): widened = lax.all_gather(ordered, 'mp', axis=2, tiled=True)]
    pmax x1 -> x0, blocking collectives: 74.5 us -> none  [shards(): largest = lax.pmax(jnp.max(jnp.abs(by_rows)), ('dp', 'mp'))]
    ppermute x0 -> x16, waiting for transfers between devices: none -> 71.5 us  [the longest x6 40.7 us: ring(): from_below.append(lax.ppermute(from_below[-1], 'mp', up))]
    all_to_all x3 -> x2, waiting for transfers between devices: 65.9 us -> 19.7 us  [shards(): got = lax.all_to_all(sent, 'dp', split_axis=0, concat_axis=0, tiled=True)]
    pallas_call x0 -> x6, Pallas kernels: none -> 26.7 us  [the longest x1 7.21 us: factors(): pl.pallas_call(factors_kernel, out_shape=[jax.ShapeDtypeStruct(left_stat....]
    ppermute x0 -> x16, starting transfers between devices: none -> 25.4 us  [the longest x6 21.3 us: ring(): from_above.append(lax.ppermute(from_above[-1], 'mp', down))]
    all_to_all x0 -> x1, blocking collectives: none -> 22.5 us  [shards(): got = lax.all_to_all(sent, 'mp', split_axis=0, concat_axis=0, tiled=True)]
  transfers between devices with their start and end apart: 5 -> 18, of which waited for: 3 -> 12; matrix products, arithmetic and copies ran while one was open for 4% -> 2% of each run, Pallas kernels for 0% -> 7%
where the time goes in v1:
time: 197 us; the launch traced here: 196 us
  waiting for transfers between devices  91.2 us (46%)
  starting transfers between devices  49.3 us (25%)
  Pallas kernels  26.7 us (14%)
  blocking collectives  22.5 us (11%)
  local copies, waits for them, and re-layouts  5.81 us (3%)
    ppermute x6, waiting for transfers between devices, ring(): from_below.append(lax.ppermute(from_below[-1], 'mp', up))  40.7 us
    all_to_all x2, starting transfers between devices, shards(): got = lax.all_to_all(sent, 'dp', split_axis=0, concat_axis=0, tiled=True)  23.9 us
    all_to_all x1, blocking collectives, shards(): got = lax.all_to_all(sent, 'mp', split_axis=0, concat_axis=0, tiled=True)  22.5 us
    ppermute x6, starting transfers between devices, ring(): from_above.append(lax.ppermute(from_above[-1], 'mp', down))  21.3 us
    all_to_all x2, waiting for transfers between devices, shards(): got = lax.all_to_all(sent, 'dp', split_axis=0, concat_axis=0, tiled=True)  19.7 us
    ppermute x6, waiting for transfers between devices, ring(): from_above.append(lax.ppermute(from_above[-1], 'mp', down))  18.2 us
    ppermute x2, waiting for transfers between devices, ring(): first = lax.ppermute(first, 'mp', up)  9.44 us
    pallas_call x1, Pallas kernels, factors(): pl.pallas_call(factors_kernel, out_shape=[jax.ShapeDtypeStruct(left_stat....  7.21 us
  transfers between devices with their start and end apart: 18, of which 12 were waited for; matrix products, arithmetic and copies ran while one was open for 2% of the time, Pallas kernels for 7%

profile of v1, /device:TPU:1, one launch (start us, length us, event | category | flops | bytes accessed | tf_op | source)
XLA Modules:
  0.0 196.3 jit_solution(7684869962818482962)
XLA Ops:
  0.6 6.5 %collective-permute-start = (bf16[3,128,1024]{2,1,0:T(8,128)(2,1)}, bf16[3,128,1024]{2,1,0:T(8,128)(2,1)S(1)}, u32[]{:S(2)}, u32[]{:S(2)}) collective-permute-start(bf16[3,128,1024]{2,1,0:T(8,128)(2,1)} %refs_9_.1), channel_id=1, source_target_pairs={{0,7},{1,0},{2,1},{3,2},{4,3},{5,4},{6,5},{7,6},{8,15},{9,8},{10,9... | collective-permute-start | bytes 2359304 | tf_op jit(solution)/shard_map/ppermute | solution.py:334
  7.1 16.5 %collective-permute-done.refs_10_ = bf16[3,128,1024]{2,1,0:T(8,128)(2,1)S(1)} collective-permute-done((bf16[3,128,1024]{2,1,0:T(8,128)(2,1)}, bf16[3,128,1024]{2,1,0:T(8,128)(2,1)S(1)}, u32[]{:S(2)}, u32[]{:S(2)}) %collective-permute-start) | collective-permute-done | bytes 786464 | tf_op jit(solution)/shard_map/ppermute | solution.py:334
  23.6 3.3 %collective-permute-start.1 = (bf16[3,128,1024]{2,1,0:T(8,128)(2,1)S(1)}, bf16[3,128,1024]{2,1,0:T(8,128)(2,1)}, u32[]{:S(2)}, u32[]{:S(2)}) collective-permute-start(bf16[3,128,1024]{2,1,0:T(8,128)(2,1)S(1)} %collective-permute-done.refs_10_), channel_id=1, source_target_pairs={{0,7},{1,0},{2,1},{3,2},{4,3},{5,4},{6,5},{7,6},{8,15},{9,8},{10,9... | collective-permute-start | bytes 2359304 | tf_op jit(solution)/shard_map/ppermute | solution.py:334
  27.0 5.2 %prepare.1 = bf16[32,112,128]{2,1,0:T(8,128)(2,1)} custom-call(s32[96]{0:T(128)} %slot_ref.3, bf16[96,32,128]{2,1,0:T(8,128)(2,1)} %grad_ref.1, f32[96,32,128]{2,1,0:T(8,128)} %one_ref.1, f32[96,32,128]{2,1,0:T(8,128)} %two_ref.1), custom_call_target="tpu_custom_call" | custom-call | flops 7864320 | bytes 4718592 | tf_op jit(solution)/shard_map/prepare/pallas_call | solution.py:81
  32.2 8.9 %all-to-all-start = ((bf16[32,112,128]{2,1,0:T(8,128)(2,1)}), bf16[32,112,128]{2,1,0:T(8,128)(2,1)S(1)}, u32[]{:S(2)}, u32[]{:S(2)}) async-start(bf16[32,112,128]{2,1,0:T(8,128)(2,1)} %prepare.1), calls=%async_computation | async-start | bytes 1835008 | tf_op jit(solution)/shard_map/all_to_all | solution.py:351
  42.2 3.5 %collective-permute-start.2 = (bf16[3,128,1024]{2,1,0:T(8,128)(2,1)}, bf16[3,128,1024]{2,1,0:T(8,128)(2,1)S(1)}, u32[]{:S(2)}, u32[]{:S(2)}) collective-permute-start(bf16[3,128,1024]{2,1,0:T(8,128)(2,1)} %collective-permute-done.1.refs_11_), channel_id=1, source_target_pairs={{0,7},{1,0},{2,1},{3,2},{4,3},{5,4},{6,5},{7,6},{8,15},{9,8},{10,9... | collective-permute-start | bytes 2359304 | tf_op jit(solution)/shard_map/ppermute | solution.py:334
  45.8 11.1 %all-to-all-done.got_ref = bf16[32,112,128]{2,1,0:T(8,128)(2,1)S(1)} async-done(((bf16[32,112,128]{2,1,0:T(8,128)(2,1)}), bf16[32,112,128]{2,1,0:T(8,128)(2,1)S(1)}, u32[]{:S(2)}, u32[]{:S(2)}) %all-to-all-start) | async-done | bytes 917536 | tf_op jit(solution)/shard_map/all_to_all | solution.py:351
  60.4 3.0 %collective-permute-done.5.refs_15_ = bf16[3,128,1024]{2,1,0:T(8,128)(2,1)S(1)} collective-permute-done((bf16[3,128,1024]{2,1,0:T(8,128)(2,1)}, bf16[3,128,1024]{2,1,0:T(8,128)(2,1)S(1)}, u32[]{:S(2)}, u32[]{:S(2)}) %collective-permute-start.5) | collective-permute-done | bytes 786464 | tf_op jit(solution)/shard_map/ppermute | solution.py:333
  63.5 2.7 %collective-permute-start.6 = (bf16[3,1024,128]{2,1,0:T(8,128)(2,1)}, bf16[3,1024,128]{2,1,0:T(8,128)(2,1)S(1)}, u32[]{:S(2)}, u32[]{:S(2)}) collective-permute-start(bf16[3,1024,128]{2,1,0:T(8,128)(2,1)} %get-tuple-element.10.refs_0_), channel_id=1, source_target_pairs={{0,7},{1,0},{2,1},{3,2},{4,3},{5,4},{6,5},{7,6},{8,15},{9,8},{10,9... | collective-permute-start | bytes 2359304 | tf_op jit(solution)/shard_map/ppermute | solution.py:334
  66.1 14.1 %collective-permute-done.9.refs_8_ = bf16[3,1024,128]{2,1,0:T(8,128)(2,1)S(1)} collective-permute-done((bf16[3,1024,128]{2,1,0:T(8,128)(2,1)}, bf16[3,1024,128]{2,1,0:T(8,128)(2,1)S(1)}, u32[]{:S(2)}, u32[]{:S(2)}) %collective-permute-start.9) | collective-permute-done | bytes 786464 | tf_op jit(solution)/shard_map/ppermute | solution.py:333
  80.3 2.7 %collective-permute-start.7 = (bf16[3,1024,128]{2,1,0:T(8,128)(2,1)S(1)}, bf16[3,1024,128]{2,1,0:T(8,128)(2,1)S(1)}, u32[]{:S(2)}, u32[]{:S(2)}) collective-permute-start(bf16[3,1024,128]{2,1,0:T(8,128)(2,1)S(1)} %collective-permute-done.6.refs_1_), channel_id=1, source_target_pairs={{0,7},{1,0},{2,1},{3,2},{4,3},{5,4},{6,5},{7,6},{8,15},{9,8},{10,9... | collective-permute-start | bytes 2359304 | tf_op jit(solution)/shard_map/ppermute | solution.py:334
  82.9 13.3 %collective-permute-done.10.refs_7_ = bf16[3,1024,128]{2,1,0:T(8,128)(2,1)S(1)} collective-permute-done((bf16[3,1024,128]{2,1,0:T(8,128)(2,1)S(1)}, bf16[3,1024,128]{2,1,0:T(8,128)(2,1)S(1)}, u32[]{:S(2)}, u32[]{:S(2)}) %collective-permute-start.10) | collective-permute-done | bytes 786464 | tf_op jit(solution)/shard_map/ppermute | solution.py:333
  96.3 2.7 %collective-permute-start.8 = (bf16[3,1024,128]{2,1,0:T(8,128)(2,1)S(1)}, bf16[3,1024,128]{2,1,0:T(8,128)(2,1)S(1)}, u32[]{:S(2)}, u32[]{:S(2)}) collective-permute-start(bf16[3,1024,128]{2,1,0:T(8,128)(2,1)S(1)} %collective-permute-done.7.refs_2_), channel_id=1, source_target_pairs={{0,7},{1,0},{2,1},{3,2},{4,3},{5,4},{6,5},{7,6},{8,15},{9,8},{10,9... | collective-permute-start | bytes 2359304 | tf_op jit(solution)/shard_map/ppermute | solution.py:334
  102.0 10.3 %collective-permute-done.11.refs_6_ = bf16[3,1024,128]{2,1,0:T(8,128)(2,1)S(1)} collective-permute-done((bf16[3,1024,128]{2,1,0:T(8,128)(2,1)S(1)}, bf16[3,1024,128]{2,1,0:T(8,128)(2,1)S(1)}, u32[]{:S(2)}, u32[]{:S(2)}) %collective-permute-start.11) | collective-permute-done | bytes 786464 | tf_op jit(solution)/shard_map/ppermute | solution.py:333
  113.9 2.7 %collective-permute-start.13 = (bf16[3,512,128]{2,1,0:T(8,128)(2,1)}, bf16[3,512,128]{2,1,0:T(8,128)(2,1)}, u32[]{:S(2)}, u32[]{:S(2)}) collective-permute-start(bf16[3,512,128]{2,1,0:T(8,128)(2,1)} %slice.17), channel_id=1, source_target_pairs={{0,7},{1,0},{2,1},{3,2},{4,3},{5,4},{6,5},{7,6},{8,15},{9,8},{10,9... | collective-permute-start | bytes 1179656 | tf_op jit(solution)/shard_map/ppermute | solution.py:339
  116.6 3.2 %collective-permute-done.15.refs_14_ = bf16[3,64,1024]{2,1,0:T(8,128)(2,1)} collective-permute-done((bf16[3,64,1024]{2,1,0:T(8,128)(2,1)}, bf16[3,64,1024]{2,1,0:T(8,128)(2,1)}, u32[]{:S(2)}, u32[]{:S(2)}) %collective-permute-start.15) | collective-permute-done | bytes 393248 | tf_op jit(solution)/shard_map/ppermute | solution.py:339
  120.7 8.5 %collective-permute-done.12.refs_4_ = bf16[3,512,128]{2,1,0:T(8,128)(2,1)S(1)} collective-permute-done((bf16[3,512,128]{2,1,0:T(8,128)(2,1)}, bf16[3,512,128]{2,1,0:T(8,128)(2,1)S(1)}, u32[]{:S(2)}, u32[]{:S(2)}) %collective-permute-start.12) | collective-permute-done | bytes 393248 | tf_op jit(solution)/shard_map/ppermute | solution.py:338
  130.0 7.0 %precondition.1 = bf16[8,432,128]{2,1,0:T(8,128)(2,1)} custom-call(s32[1]{0:T(128)} %bitcast.place_ref, bf16[3,128,1024]{2,1,0:T(8,128)(2,1)} %left_ref.2, f32[16,128]{1,0:T(8,128)} %get-tuple-element.8.adam_ref, bf16[3,1024,128]{2,1,0:T(8,128)(2,1)} %get-tuple-element.10.refs_0_, bf16[3,1024,128]{2,1,0:T(8,128)(2,1)} %copy-done.5, ...), custom_call_target="tpu_custom_call" | custom-call | flops 1610612736 | bytes 15728640 | tf_op jit(solution)/shard_map/precondition/pallas_call | solution.py:193
  137.0 22.5 %all_to_all.15.got_ref = bf16[8,432,128]{2,1,0:T(8,128)(2,1)} all-to-all(bf16[8,432,128]{2,1,0:T(8,128)(2,1)} %precondition.1), channel_id=1, replica_groups=mesh['dp'=32,'mp'=8] {'mp'}, dimensions={0} | all-to-all | bytes 1769472 | tf_op jit(solution)/shard_map/all_to_all | solution.py:356
  159.5 2.3 %scale.1 = bf16[32,112,128]{2,1,0:T(8,128)(2,1)} custom-call(bf16[8,432,128]{2,1,0:T(8,128)(2,1)} %all_to_all.15.got_ref), custom_call_target="tpu_custom_call" | custom-call | bytes 1769472 | tf_op jit(solution)/shard_map/scale/pallas_call | solution.py:239
  161.8 15.0 %all-to-all-start.2 = ((bf16[32,112,128]{2,1,0:T(8,128)(2,1)}), bf16[32,112,128]{2,1,0:T(8,128)(2,1)S(1)}, u32[]{:S(2)}, u32[]{:S(2)}) async-start(bf16[32,112,128]{2,1,0:T(8,128)(2,1)} %scale.1), calls=%async_computation.2 | async-start | bytes 1835008 | tf_op jit(solution)/shard_map/all_to_all | solution.py:358
  176.8 7.2 %factors.1 = (f32[3,128,1024]{2,1,0:T(8,128)}, f32[3,128,1024]{2,1,0:T(8,128)}) custom-call(s32[1]{0:T(128)} %bitcast.place_ref, f32[3,128,1024]{2,1,0:T(8,128)} %left_ref.3, f32[3,128,1024]{2,1,0:T(8,128)} %right_ref.1, bf16[3,1024,128]{2,1,0:T(8,128)(2,1)} %get-tuple-element.10.refs_0_, bf16[3,1024,128]{2,1,0:T(8,128)(2,1)} %copy-done.5, ...), custom_call_target="tpu_custom_call" | custom-call | flops 1610612736 | bytes 12582912 | tf_op jit(solution)/shard_map/factors/pallas_call | solution.py:315
  184.0 8.5 %all-to-all-done.2.got_ref = bf16[32,112,128]{2,1,0:T(8,128)(2,1)S(1)} async-done(((bf16[32,112,128]{2,1,0:T(8,128)(2,1)}), bf16[32,112,128]{2,1,0:T(8,128)(2,1)S(1)}, u32[]{:S(2)}, u32[]{:S(2)}) %all-to-all-start.2) | async-done | bytes 917536 | tf_op jit(solution)/shard_map/all_to_all | solution.py:358
  193.5 2.7 %finish.1 = bf16[96,32,128]{2,1,0:T(8,128)(2,1)} custom-call(s32[96]{0:T(128)} %slot_ref.3, bf16[32,112,128]{2,1,0:T(8,128)(2,1)} %copy-done.3), custom_call_target="tpu_custom_call" | custom-call | bytes 1835008 | tf_op jit(solution)/shard_map/finish/pallas_call | solution.py:275
  (49 shorter events, 12.0 us)
Async XLA Ops:
  0.6 23.0 %collective-permute-start = (bf16[3,128,1024]{2,1,0:T(8,128)(2,1)}, bf16[3,128,1024]{2,1,0:T(8,128)(2,1)S(1)}, u32[]{:S(2)}, u32[]{:S(2)}) collective-permute-start(bf16[3,128,1024]{2,1,0:T(8,128)(2,1)} %refs_9_.1), channel_id=1, source_target_pairs={{0,7},{1,0},{2,1},{3,2},{4,3},{5,4},{6,5},{7,6},{8,15},{9,8},{10,9... | collective-permute-start | bytes 2359304 | tf_op jit(solution)/shard_map/ppermute | solution.py:334
  7.1 19.8 %collective-permute-start.3 = (bf16[3,128,1024]{2,1,0:T(8,128)(2,1)}, bf16[3,128,1024]{2,1,0:T(8,128)(2,1)S(1)}, u32[]{:S(2)}, u32[]{:S(2)}) collective-permute-start(bf16[3,128,1024]{2,1,0:T(8,128)(2,1)} %refs_9_.1), channel_id=1, source_target_pairs={{0,1},{1,2},{2,3},{3,4},{4,5},{5,6},{6,7},{7,0},{8,9},{9,10},{10,1... | collective-permute-start | bytes 2359304 | tf_op jit(solution)/shard_map/ppermute | solution.py:333
  23.6 18.6 %collective-permute-start.1 = (bf16[3,128,1024]{2,1,0:T(8,128)(2,1)S(1)}, bf16[3,128,1024]{2,1,0:T(8,128)(2,1)}, u32[]{:S(2)}, u32[]{:S(2)}) collective-permute-start(bf16[3,128,1024]{2,1,0:T(8,128)(2,1)S(1)} %collective-permute-done.refs_10_), channel_id=1, source_target_pairs={{0,7},{1,0},{2,1},{3,2},{4,3},{5,4},{6,5},{7,6},{8,15},{9,8},{10,9... | collective-permute-start | bytes 2359304 | tf_op jit(solution)/shard_map/ppermute | solution.py:334
  27.0 18.8 %collective-permute-start.4 = (bf16[3,128,1024]{2,1,0:T(8,128)(2,1)S(1)}, bf16[3,128,1024]{2,1,0:T(8,128)(2,1)}, u32[]{:S(2)}, u32[]{:S(2)}) collective-permute-start(bf16[3,128,1024]{2,1,0:T(8,128)(2,1)S(1)} %collective-permute-done.3.refs_17_), channel_id=1, source_target_pairs={{0,1},{1,2},{2,3},{3,4},{4,5},{5,6},{6,7},{7,0},{8,9},{9,10},{10,1... | collective-permute-start | bytes 2359304 | tf_op jit(solution)/shard_map/ppermute | solution.py:333
  32.2 24.7 %all-to-all-start = ((bf16[32,112,128]{2,1,0:T(8,128)(2,1)}), bf16[32,112,128]{2,1,0:T(8,128)(2,1)S(1)}, u32[]{:S(2)}, u32[]{:S(2)}) async-start(bf16[32,112,128]{2,1,0:T(8,128)(2,1)} %prepare.1), calls=%async_computation | async-start | bytes 1835008 | tf_op jit(solution)/shard_map/all_to_all | solution.py:351
  42.2 18.2 %collective-permute-start.2 = (bf16[3,128,1024]{2,1,0:T(8,128)(2,1)}, bf16[3,128,1024]{2,1,0:T(8,128)(2,1)S(1)}, u32[]{:S(2)}, u32[]{:S(2)}) collective-permute-start(bf16[3,128,1024]{2,1,0:T(8,128)(2,1)} %collective-permute-done.1.refs_11_), channel_id=1, source_target_pairs={{0,7},{1,0},{2,1},{3,2},{4,3},{5,4},{6,5},{7,6},{8,15},{9,8},{10,9... | collective-permute-start | bytes 2359304 | tf_op jit(solution)/shard_map/ppermute | solution.py:334
  45.8 17.7 %collective-permute-start.5 = (bf16[3,128,1024]{2,1,0:T(8,128)(2,1)}, bf16[3,128,1024]{2,1,0:T(8,128)(2,1)S(1)}, u32[]{:S(2)}, u32[]{:S(2)}) collective-permute-start(bf16[3,128,1024]{2,1,0:T(8,128)(2,1)} %collective-permute-done.4.refs_16_), channel_id=1, source_target_pairs={{0,1},{1,2},{2,3},{3,4},{4,5},{5,6},{6,7},{7,0},{8,9},{9,10},{10,1... | collective-permute-start | bytes 2359304 | tf_op jit(solution)/shard_map/ppermute | solution.py:333
  60.4 68.8 %copy-start.8 = (bf16[3,128,1024]{2,1,0:T(8,128)(2,1)}, bf16[3,128,1024]{2,1,0:T(8,128)(2,1)S(1)}, u32[]{:S(2)}) copy-start(bf16[3,128,1024]{2,1,0:T(8,128)(2,1)S(1)} %collective-permute-done.2.refs_12_) | copy-start | bytes 2359300
  63.5 65.8 %copy-start.9 = (bf16[3,128,1024]{2,1,0:T(8,128)(2,1)}, bf16[3,128,1024]{2,1,0:T(8,128)(2,1)S(1)}, u32[]{:S(2)}) copy-start(bf16[3,128,1024]{2,1,0:T(8,128)(2,1)S(1)} %collective-permute-done.5.refs_15_) | copy-start | bytes 2359300
  63.5 16.8 %collective-permute-start.9 = (bf16[3,1024,128]{2,1,0:T(8,128)(2,1)}, bf16[3,1024,128]{2,1,0:T(8,128)(2,1)S(1)}, u32[]{:S(2)}, u32[]{:S(2)}) collective-permute-start(bf16[3,1024,128]{2,1,0:T(8,128)(2,1)} %get-tuple-element.10.refs_0_), channel_id=1, source_target_pairs={{0,1},{1,2},{2,3},{3,4},{4,5},{5,6},{6,7},{7,0},{8,9},{9,10},{10,1... | collective-permute-start | bytes 2359304 | tf_op jit(solution)/shard_map/ppermute | solution.py:333
  63.5 16.8 %collective-permute-start.6 = (bf16[3,1024,128]{2,1,0:T(8,128)(2,1)}, bf16[3,1024,128]{2,1,0:T(8,128)(2,1)S(1)}, u32[]{:S(2)}, u32[]{:S(2)}) collective-permute-start(bf16[3,1024,128]{2,1,0:T(8,128)(2,1)} %get-tuple-element.10.refs_0_), channel_id=1, source_target_pairs={{0,7},{1,0},{2,1},{3,2},{4,3},{5,4},{6,5},{7,6},{8,15},{9,8},{10,9... | collective-permute-start | bytes 2359304 | tf_op jit(solution)/shard_map/ppermute | solution.py:334
  80.3 33.7 %copy-start.4 = (bf16[3,1024,128]{2,1,0:T(8,128)(2,1)}, bf16[3,1024,128]{2,1,0:T(8,128)(2,1)S(1)}, u32[]{:S(2)}) copy-start(bf16[3,1024,128]{2,1,0:T(8,128)(2,1)S(1)} %collective-permute-done.9.refs_8_) | copy-start | bytes 2359300
  80.3 16.0 %collective-permute-start.10 = (bf16[3,1024,128]{2,1,0:T(8,128)(2,1)S(1)}, bf16[3,1024,128]{2,1,0:T(8,128)(2,1)S(1)}, u32[]{:S(2)}, u32[]{:S(2)}) collective-permute-start(bf16[3,1024,128]{2,1,0:T(8,128)(2,1)S(1)} %collective-permute-done.9.refs_8_), channel_id=1, source_target_pairs={{0,1},{1,2},{2,3},{3,4},{4,5},{5,6},{6,7},{7,0},{8,9},{9,10},{10,1... | collective-permute-start | bytes 2359304 | tf_op jit(solution)/shard_map/ppermute | solution.py:333
  80.3 33.7 %copy-start.5 = (bf16[3,1024,128]{2,1,0:T(8,128)(2,1)}, bf16[3,1024,128]{2,1,0:T(8,128)(2,1)S(1)}, u32[]{:S(2)}) copy-start(bf16[3,1024,128]{2,1,0:T(8,128)(2,1)S(1)} %collective-permute-done.6.refs_1_) | copy-start | bytes 2359300
  80.3 16.0 %collective-permute-start.7 = (bf16[3,1024,128]{2,1,0:T(8,128)(2,1)S(1)}, bf16[3,1024,128]{2,1,0:T(8,128)(2,1)S(1)}, u32[]{:S(2)}, u32[]{:S(2)}) collective-permute-start(bf16[3,1024,128]{2,1,0:T(8,128)(2,1)S(1)} %collective-permute-done.6.refs_1_), channel_id=1, source_target_pairs={{0,7},{1,0},{2,1},{3,2},{4,3},{5,4},{6,5},{7,6},{8,15},{9,8},{10,9... | collective-permute-start | bytes 2359304 | tf_op jit(solution)/shard_map/ppermute | solution.py:334
  96.2 20.3 %copy-start.6 = (bf16[3,1024,128]{2,1,0:T(8,128)(2,1)}, bf16[3,1024,128]{2,1,0:T(8,128)(2,1)S(1)}, u32[]{:S(2)}) copy-start(bf16[3,1024,128]{2,1,0:T(8,128)(2,1)S(1)} %collective-permute-done.10.refs_7_) | copy-start | bytes 2359300
  96.2 16.0 %collective-permute-start.11 = (bf16[3,1024,128]{2,1,0:T(8,128)(2,1)S(1)}, bf16[3,1024,128]{2,1,0:T(8,128)(2,1)S(1)}, u32[]{:S(2)}, u32[]{:S(2)}) collective-permute-start(bf16[3,1024,128]{2,1,0:T(8,128)(2,1)S(1)} %collective-permute-done.10.refs_7_), channel_id=1, source_target_pairs={{0,1},{1,2},{2,3},{3,4},{4,5},{5,6},{6,7},{7,0},{8,9},{9,10},{10,1... | collective-permute-start | bytes 2359304 | tf_op jit(solution)/shard_map/ppermute | solution.py:333
  96.3 20.3 %copy-start.7 = (bf16[3,1024,128]{2,1,0:T(8,128)(2,1)}, bf16[3,1024,128]{2,1,0:T(8,128)(2,1)S(1)}, u32[]{:S(2)}) copy-start(bf16[3,1024,128]{2,1,0:T(8,128)(2,1)S(1)} %collective-permute-done.7.refs_2_) | copy-start | bytes 2359300
  96.3 16.8 %collective-permute-start.8 = (bf16[3,1024,128]{2,1,0:T(8,128)(2,1)S(1)}, bf16[3,1024,128]{2,1,0:T(8,128)(2,1)S(1)}, u32[]{:S(2)}, u32[]{:S(2)}) collective-permute-start(bf16[3,1024,128]{2,1,0:T(8,128)(2,1)S(1)} %collective-permute-done.7.refs_2_), channel_id=1, source_target_pairs={{0,7},{1,0},{2,1},{3,2},{4,3},{5,4},{6,5},{7,6},{8,15},{9,8},{10,9... | collective-permute-start | bytes 2359304 | tf_op jit(solution)/shard_map/ppermute | solution.py:334
  99.7 20.1 %collective-permute-start.15 = (bf16[3,64,1024]{2,1,0:T(8,128)(2,1)}, bf16[3,64,1024]{2,1,0:T(8,128)(2,1)}, u32[]{:S(2)}, u32[]{:S(2)}) collective-permute-start(bf16[3,64,1024]{2,1,0:T(8,128)(2,1)} %slice.19), channel_id=1, source_target_pairs={{0,7},{1,0},{2,1},{3,2},{4,3},{5,4},{6,5},{7,6},{8,15},{9,8},{10,9... | collective-permute-start | bytes 1179656 | tf_op jit(solution)/shard_map/ppermute | solution.py:339
  100.5 20.1 %collective-permute-start.14 = (bf16[3,64,1024]{2,1,0:T(8,128)(2,1)}, bf16[3,64,1024]{2,1,0:T(8,128)(2,1)}, u32[]{:S(2)}, u32[]{:S(2)}) collective-permute-start(bf16[3,64,1024]{2,1,0:T(8,128)(2,1)} %slice.18), channel_id=1, source_target_pairs={{0,1},{1,2},{2,3},{3,4},{4,5},{5,6},{6,7},{7,0},{8,9},{9,10},{10,1... | collective-permute-start | bytes 1179656 | tf_op jit(solution)/shard_map/ppermute | solution.py:338
  113.1 16.1 %collective-permute-start.12 = (bf16[3,512,128]{2,1,0:T(8,128)(2,1)}, bf16[3,512,128]{2,1,0:T(8,128)(2,1)S(1)}, u32[]{:S(2)}, u32[]{:S(2)}) collective-permute-start(bf16[3,512,128]{2,1,0:T(8,128)(2,1)} %slice.16), channel_id=1, source_target_pairs={{0,1},{1,2},{2,3},{3,4},{4,5},{5,6},{6,7},{7,0},{8,9},{9,10},{10,1... | collective-permute-start | bytes 1179656 | tf_op jit(solution)/shard_map/ppermute | solution.py:338
  113.9 15.3 %collective-permute-start.13 = (bf16[3,512,128]{2,1,0:T(8,128)(2,1)}, bf16[3,512,128]{2,1,0:T(8,128)(2,1)}, u32[]{:S(2)}, u32[]{:S(2)}) collective-permute-start(bf16[3,512,128]{2,1,0:T(8,128)(2,1)} %slice.17), channel_id=1, source_target_pairs={{0,7},{1,0},{2,1},{3,2},{4,3},{5,4},{6,5},{7,6},{8,15},{9,8},{10,9... | collective-permute-start | bytes 1179656 | tf_op jit(solution)/shard_map/ppermute | solution.py:339
  161.8 30.7 %all-to-all-start.2 = ((bf16[32,112,128]{2,1,0:T(8,128)(2,1)}), bf16[32,112,128]{2,1,0:T(8,128)(2,1)S(1)}, u32[]{:S(2)}, u32[]{:S(2)}) async-start(bf16[32,112,128]{2,1,0:T(8,128)(2,1)} %scale.1), calls=%async_computation.2 | async-start | bytes 1835008 | tf_op jit(solution)/shard_map/all_to_all | solution.py:358
  (7 other events, 49.5 us)

commit v2 on v1

--- a/solution.py
+++ b/solution.py
@@ -20,7 +20,7 @@
 
 
 def params():
-    return pltpu.CompilerParams(vmem_limit_bytes=60 * 1024 * 1024)
+    return pltpu.CompilerParams(vmem_limit_bytes=62 * 1024 * 1024)
 
 
 def scalars():
@@ -155,97 +155,140 @@
     return jnp.concatenate([grads.rows(2 * k + e, 0, order) for e in range(2)], axis=1)
 
 
-def precondition_kernel(place_ref, left_ref, adam_ref, *refs):
-    out_ref = refs[-1]
-    grads, roots = RingPanels(place_ref[0], refs[:9]), refs[9:18]
-    order = left_ref.shape[1]
-    step = pl.program_id(0)
-    base = pl.multiple_of(step * (128 + PAD), PAD)
+def bulk_kernel(left_ref, *refs):
+    grads, roots, out_ref = refs[:7], refs[7:14], refs[14]
     left = left_ref[...]
     half = []
-    for k in range(4):
-        pair = pair_of(grads, k, order)
+    for k in (0, 2, 4, 6):
+        pair = [ref[...] for ref in grads[k : k + 2]]
+        pair = jnp.concatenate(pair, axis=1) if len(pair) > 1 else pair[0]
         half.append(jnp.dot(left, pair, preferred_element_type=F32).astype(BF16))
     half = jnp.concatenate(half, axis=1)
+    for c in range(4):
+        column = slice(256 * c, 256 * (c + 1))
+        part = jnp.concatenate([ref[:, column] for ref in roots], axis=0)
+        out_ref[:, column] = jnp.dot(half, part, preferred_element_type=F32)
+
+
+def bulk(left_root, grads, roots):
+    count, rows, order = left_root.shape
+    early = [*grads[:4], *grads[6:], *roots[:4], *roots[6:]]
+    return pl.pallas_call(
+        bulk_kernel,
+        out_shape=jax.ShapeDtypeStruct(left_root.shape, F32),
+        grid=(count,),
+        in_specs=[slot_of(left_root.shape)] + [slot_of(panel.shape) for panel in early],
+        out_specs=slot_of(left_root.shape),
+        compiler_params=params(),
+        cost_estimate=cost(count * 4 * rows * order * order, count * 5 * order * order),
+        name="bulk",
+    )(left_root, *early)
+
+
+def precondition_kernel(place_ref, left_ref, adam_ref, part_ref, *refs):
+    out_refs, sums_ref = refs[4:12], refs[12]
+    count = pl.num_programs(0)
+    step = pl.program_id(0)
+    rows = pl.ds(pl.multiple_of(step * 128, 128), 128)
+    panel = jnp.concatenate([refs[0][...], refs[1][...]], axis=0)
+    half = jnp.dot(left_ref[...], panel, preferred_element_type=F32).astype(BF16)
     square = jnp.zeros((1, 128), F32)
     largest = jnp.zeros((1, 128), F32)
-    for c in range(4):
-        parts = [ref[:, 256 * c : 256 * (c + 1)] for ref in roots]
-        pre = jnp.dot(half, jnp.concatenate(parts, axis=0), preferred_element_type=F32)
-        for e in range(2):
-            piece = pre[:, 128 * e : 128 * (e + 1)]
-            out_ref[2 * c + e, pl.ds(base, 128), :] = piece.astype(BF16)
-            square = square + jnp.sum(piece * piece, axis=0, keepdims=True)
-            largest = jnp.maximum(largest, jnp.max(jnp.abs(piece), axis=0, keepdims=True))
+    for k in range(8):
+        column = pl.ds(pl.multiple_of(lax.rem(place_ref[0] + k, 8) * 128, 128), 128)
+        root = jnp.concatenate([refs[2][:, column], refs[3][:, column]], axis=0)
+        pre = part_ref[:, column] + jnp.dot(half, root, preferred_element_type=F32)
+        out_refs[k][rows, :] = pre.astype(BF16)
+        square = square + jnp.sum(pre * pre, axis=0, keepdims=True)
+        largest = jnp.maximum(largest, jnp.max(jnp.abs(pre), axis=0, keepdims=True))
     low = 3 * step
     row = lax.broadcasted_iota(jnp.int32, (PAD, 128), 0)
     inside = (row >= low) & (row < low + 3)
     adam = jnp.sum(jnp.where(inside, adam_ref[...], 0.0), axis=0, keepdims=True)
-    tile = split_rows([adam, square, largest])
-    tail = pl.multiple_of(base + 128, PAD)
-    for k in range(8):
-        out_ref[k, pl.ds(tail, PAD), :] = tile
-
-
-def precondition(place, left_root, adam, grads, roots):
-    count, _, order = left_root.shape
-    out = (8, count * (128 + PAD), 128)
+    lane = lax.broadcasted_iota(jnp.int32, (1, 128), 1)
+
+    @pl.when(step == 0)
+    def _():
+        sums_ref[...] = jnp.zeros((1, 128), F32)
+
+    sums = sums_ref[...]
+    for at, value in (
+        (step, jnp.sum(adam, axis=1, keepdims=True)),
+        (count + step, jnp.sum(square, axis=1, keepdims=True)),
+        (2 * count + step, jnp.max(largest, axis=1, keepdims=True)),
+    ):
+        sums = jnp.where(lane == at, jnp.broadcast_to(value, (1, 128)), sums)
+    sums_ref[...] = sums
+
+    @pl.when(step == count - 1)
+    def _():
+        tile = split_rows([sums])
+        for out_ref in out_refs:
+            out_ref[out_ref.shape[0] - PAD :, :] = tile
+
+
+def precondition(place, left_root, adam, part, grads, roots):
+    count, rows, order = left_root.shape
+    out = (count * rows + PAD, 128)
+    late = [*grads[4:6], *roots[4:6]]
     return pl.pallas_call(
         precondition_kernel,
-        out_shape=jax.ShapeDtypeStruct(out, BF16),
+        out_shape=[jax.ShapeDtypeStruct(out, BF16)] * 8,
         grid=(count,),
-        in_specs=[scalars(), slot_of(left_root.shape), whole(adam.shape)]
-        + [slot_of(panel.shape) for panel in (*grads, *roots)],
-        out_specs=whole(out),
-        compiler_params=params(),
-        cost_estimate=cost(count * 4 * 128 * order * order, count * 5 * order * order),
+        in_specs=[scalars(), slot_of(left_root.shape), whole(adam.shape), slot_of(part.shape)]
+        + [slot_of(panel.shape) for panel in late],
+        out_specs=[whole(out)] * 8,
+        scratch_shapes=[pltpu.VMEM((1, 128), F32)],
+        compiler_params=params(),
+        cost_estimate=cost(count * 4 * rows * 128 * order, count * 4 * rows * order),
         name="precondition",
-    )(place, left_root, adam, *grads, *roots)
-
-
-def scale_kernel(count, got_ref, out_ref):
+    )(place, left_root, adam, part, *late)
+
+
+def scale_kernel(count, place_ref, *refs):
+    got_refs, out_ref = refs[:-1], refs[-1]
     rows = (out_ref.shape[1] - PAD) // count
-    step = min(rows, 128)
+    each = 128 // rows
+    lane = lax.broadcasted_iota(jnp.int32, (1, 128), 1)
+    total = largest = jnp.zeros((1, 128), F32)
+    for ref in got_refs:
+        values = joined(ref[count * 128 :, :].astype(F32), 0)
+        total = total + values
+        largest = jnp.maximum(largest, values)
+
+    def only(values, at):
+        one = jnp.sum(jnp.where(lane == at, values, 0.0), axis=1, keepdims=True)
+        return jnp.broadcast_to(one, (1, 128))
+
     scales = []
     peak = jnp.zeros((1, 128), F32)
     for i in range(count):
-        base = i * (128 + PAD)
-        adam = square = largest = None
-        for k in range(8):
-            tile = got_ref[k, base + 128 : base + 128 + PAD, :].astype(F32)
-            a, s, m = joined(tile, 0), joined(tile, 1), joined(tile, 2)
-            adam = a if adam is None else adam + a
-            square = s if square is None else square + s
-            largest = m if largest is None else jnp.maximum(largest, m)
-        adam = jnp.sum(adam, axis=1, keepdims=True)
-        square = jnp.sum(square, axis=1, keepdims=True)
-        largest = jnp.max(largest, axis=1, keepdims=True)
-        scale = jnp.broadcast_to(jnp.sqrt(adam) / jnp.sqrt(square + NORM_EPS), (1, 128))
+        adam, square = only(total, i), only(total, count + i)
+        scale = jnp.sqrt(adam) / jnp.sqrt(square + NORM_EPS)
         scales.append(scale)
-        peak = jnp.maximum(peak, scale * jnp.broadcast_to(largest, (1, 128)))
+        peak = jnp.maximum(peak, scale * only(largest, 2 * count + i))
     tile = split_rows(scales + [peak])
-    for d in range(out_ref.shape[0]):
-        for i in range(count):
-            for at in range(0, rows, step):
-                row = d * rows + at
-                low = i * (128 + PAD) + row % 128
-                to = i * rows + at
-                out_ref[d, to : to + step, :] = got_ref[row // 128, low : low + step, :]
-        out_ref[d, count * rows :, :] = tile
-
-
-def scale_up(owners, count, order, got):
-    out = (owners, count * (order // owners) + PAD, 128)
+    for k, ref in enumerate(got_refs):
+        first = lax.rem(place_ref[0] + 8 - k, 8) * each
+        for e in range(each):
+            for i in range(count):
+                low = i * 128 + e * rows
+                out_ref[first + e, i * rows : (i + 1) * rows, :] = ref[low : low + rows, :]
+            out_ref[first + e, count * rows :, :] = tile
+
+
+def scale_up(owners, count, place, gots):
+    out = (owners, count * (1024 // owners) + PAD, 128)
     return pl.pallas_call(
         functools.partial(scale_kernel, count),
         out_shape=jax.ShapeDtypeStruct(out, BF16),
         grid=(1,),
-        in_specs=[whole(got.shape)],
+        in_specs=[scalars()] + [whole(got.shape) for got in gots],
         out_specs=whole(out),
         compiler_params=params(),
-        cost_estimate=cost(0, 4 * got.size),
+        cost_estimate=cost(0, 32 * gots[0].size),
         name="scale",
-    )(got)
+    )(place, *gots)
 
 
 def finish_kernel(count, slot_ref, got_ref, out_ref):
@@ -343,7 +386,7 @@
 def shards(
     gradient, slot_block, first_moment, second_moment, left_stat, right_stat, left_root, right_root
 ):
-    count, _, order = left_stat.shape
+    count = left_stat.shape[0]
     owners = gradient.shape[0] // count
     place = lax.axis_index("mp").astype(jnp.int32).reshape(1)
     roots = ring(right_root, 1)
@@ -352,9 +395,12 @@
     own, adam = unpack(count, got)
     own, _ = lax.optimization_barrier((own, (roots[3], roots[6])))
     grads = ring(own, 1)
-    sent = precondition(place, left_root, adam, grads, roots)
-    got = lax.all_to_all(sent, "mp", split_axis=0, concat_axis=0, tiled=True)
-    sent = scale_up(owners, count, order, got)
+    part = bulk(left_root, grads, roots)
+    sents = precondition(place, left_root, adam, part, grads, roots)
+    gots = list(sents)
+    for k in (4, 3, 5, 2, 6, 1, 7):
+        gots[k] = lax.ppermute(sents[k], "mp", [(i, (i + k) % 8) for i in range(8)])
+    sent = scale_up(owners, count, place, gots)
     got = lax.all_to_all(sent, "dp", split_axis=0, concat_axis=0, tiled=True)
     left_new, right_new = factors(place, left_stat, right_stat, grads)
     update = finish(count, slot_block, got)

time: 197 us -> 192 us (0.975)
  blocking collectives: 22.5 us -> 0 us
  starting transfers between devices: 49.3 us -> 62.9 us
  Pallas kernels: 26.7 us -> 30.8 us
  local copies, waits for them, and re-layouts: 5.81 us -> 8.45 us
  waiting for transfers between devices: 91.2 us -> 88.6 us
    all_to_all x1 -> x0, blocking collectives: 22.5 us -> none  [shards(): got = lax.all_to_all(sent, 'mp', split_axis=0, concat_axis=0, tiled=True)]
    ppermute x0 -> x7, starting transfers between devices: none -> 11.7 us  [shards(): gots[k] = lax.ppermute(sents[k], 'mp', [(i, (i + k) % 8) for i in range(8)])]
    ppermute x0 -> x7, waiting for transfers between devices: none -> 7.21 us  [shards(): gots[k] = lax.ppermute(sents[k], 'mp', [(i, (i + k) % 8) for i in range(8)])]
    pallas_call x1 -> x2, Pallas kernels: 7.05 us -> 11.4 us  [the longest x1 6.92 us: bulk(): pl.pallas_call(bulk_kernel, out_shape=jax.ShapeDtypeStruct(left_root.shap...]
    ppermute x2, waiting for transfers between devices: 9.44 us -> 5.7 us  [ring(): first = lax.ppermute(first, 'mp', up)]
    ppermute x6, waiting for transfers between devices: 40.7 us -> 37.5 us  [ring(): from_below.append(lax.ppermute(from_below[-1], 'mp', up))]
    ppermute x2, waiting for transfers between devices: 3.18 us -> 0.01 us  [ring(): second = lax.ppermute(second, 'mp', down)]
    ppermute x2, starting transfers between devices: 2.71 us -> 5.34 us  [ring(): second = lax.ppermute(second, 'mp', down)]
  transfers between devices with their start and end apart: 18 -> 25, of which waited for: 12 -> 14; matrix products, arithmetic and copies ran while one was open for 2% -> 3% of each run, Pallas kernels for 7% -> 11%
where the time goes in v2:
time: 192 us
  waiting for transfers between devices  88.6 us (46%)
  starting transfers between devices  62.9 us (33%)
  Pallas kernels  30.8 us (16%)
  local copies, waits for them, and re-layouts  8.45 us (4%)
    ppermute x6, waiting for transfers between devices, ring(): from_below.append(lax.ppermute(from_below[-1], 'mp', up))  37.5 us
    all_to_all x2, starting transfers between devices, shards(): got = lax.all_to_all(sent, 'dp', split_axis=0, concat_axis=0, tiled=True)  24.5 us
    ppermute x6, starting transfers between devices, ring(): from_above.append(lax.ppermute(from_above[-1], 'mp', down))  21.4 us
    all_to_all x2, waiting for transfers between devices, shards(): got = lax.all_to_all(sent, 'dp', split_axis=0, concat_axis=0, tiled=True)  19.4 us
    ppermute x6, waiting for transfers between devices, ring(): from_above.append(lax.ppermute(from_above[-1], 'mp', down))  18.8 us
    ppermute x7, starting transfers between devices, shards(): gots[k] = lax.ppermute(sents[k], 'mp', [(i, (i + k) % 8) for i in range(8)])  11.7 us
    pallas_call x1, Pallas kernels, factors(): pl.pallas_call(factors_kernel, out_shape=[jax.ShapeDtypeStruct(left_stat....  7.21 us
    ppermute x7, waiting for transfers between devices, shards(): gots[k] = lax.ppermute(sents[k], 'mp', [(i, (i + k) % 8) for i in range(8)])  7.21 us
  transfers between devices with their start and end apart: 25, of which 14 were waited for; matrix products, arithmetic and copies ran while one was open for 3% of the time, Pallas kernels for 11%

profile of v2, /device:TPU:1, one launch (start us, length us, event | category | flops | bytes accessed | tf_op | source)
XLA Modules:
  0.0 191.6 jit_solution(6636048152036513723)
XLA Ops:
  0.6 6.5 %collective-permute-start = (bf16[3,128,1024]{2,1,0:T(8,128)(2,1)}, bf16[3,128,1024]{2,1,0:T(8,128)(2,1)S(1)}, u32[]{:S(2)}, u32[]{:S(2)}) collective-permute-start(bf16[3,128,1024]{2,1,0:T(8,128)(2,1)} %refs_7_.1), channel_id=1, source_target_pairs={{0,7},{1,0},{2,1},{3,2},{4,3},{5,4},{6,5},{7,6},{8,15},{9,8},{10,9... | collective-permute-start | bytes 2359304 | tf_op jit(solution)/shard_map/ppermute | solution.py:377
  7.1 16.5 %collective-permute-done.refs_8_ = bf16[3,128,1024]{2,1,0:T(8,128)(2,1)S(1)} collective-permute-done((bf16[3,128,1024]{2,1,0:T(8,128)(2,1)}, bf16[3,128,1024]{2,1,0:T(8,128)(2,1)S(1)}, u32[]{:S(2)}, u32[]{:S(2)}) %collective-permute-start) | collective-permute-done | bytes 786464 | tf_op jit(solution)/shard_map/ppermute | solution.py:377
  23.6 3.3 %collective-permute-start.1 = (bf16[3,128,1024]{2,1,0:T(8,128)(2,1)S(1)}, bf16[3,128,1024]{2,1,0:T(8,128)(2,1)}, u32[]{:S(2)}, u32[]{:S(2)}) collective-permute-start(bf16[3,128,1024]{2,1,0:T(8,128)(2,1)S(1)} %collective-permute-done.refs_8_), channel_id=1, source_target_pairs={{0,7},{1,0},{2,1},{3,2},{4,3},{5,4},{6,5},{7,6},{8,15},{9,8},{10,9... | collective-permute-start | bytes 2359304 | tf_op jit(solution)/shard_map/ppermute | solution.py:377
  27.0 4.9 %prepare.1 = bf16[32,112,128]{2,1,0:T(8,128)(2,1)} custom-call(s32[96]{0:T(128)} %slot_ref.3, bf16[96,32,128]{2,1,0:T(8,128)(2,1)} %grad_ref.1, f32[96,32,128]{2,1,0:T(8,128)} %one_ref.1, f32[96,32,128]{2,1,0:T(8,128)} %two_ref.1), custom_call_target="tpu_custom_call" | custom-call | flops 7864320 | bytes 4718592 | tf_op jit(solution)/shard_map/prepare/pallas_call | solution.py:81
  31.9 8.9 %all-to-all-start = ((bf16[32,112,128]{2,1,0:T(8,128)(2,1)}), bf16[32,112,128]{2,1,0:T(8,128)(2,1)S(1)}, u32[]{:S(2)}, u32[]{:S(2)}) async-start(bf16[32,112,128]{2,1,0:T(8,128)(2,1)} %prepare.1), calls=%async_computation | async-start | bytes 1835008 | tf_op jit(solution)/shard_map/all_to_all | solution.py:394
  42.2 3.5 %collective-permute-start.2 = (bf16[3,128,1024]{2,1,0:T(8,128)(2,1)}, bf16[3,128,1024]{2,1,0:T(8,128)(2,1)S(1)}, u32[]{:S(2)}, u32[]{:S(2)}) collective-permute-start(bf16[3,128,1024]{2,1,0:T(8,128)(2,1)} %collective-permute-done.1.refs_9_), channel_id=1, source_target_pairs={{0,7},{1,0},{2,1},{3,2},{4,3},{5,4},{6,5},{7,6},{8,15},{9,8},{10,9... | collective-permute-start | bytes 2359304 | tf_op jit(solution)/shard_map/ppermute | solution.py:377
  45.8 10.8 %all-to-all-done.got_ref = bf16[32,112,128]{2,1,0:T(8,128)(2,1)S(1)} async-done(((bf16[32,112,128]{2,1,0:T(8,128)(2,1)}), bf16[32,112,128]{2,1,0:T(8,128)(2,1)S(1)}, u32[]{:S(2)}, u32[]{:S(2)}) %all-to-all-start) | async-done | bytes 917536 | tf_op jit(solution)/shard_map/all_to_all | solution.py:394
  60.4 3.1 %collective-permute-done.5.refs_11_ = bf16[3,128,1024]{2,1,0:T(8,128)(2,1)} collective-permute-done((bf16[3,128,1024]{2,1,0:T(8,128)(2,1)}, bf16[3,128,1024]{2,1,0:T(8,128)(2,1)}, u32[]{:S(2)}, u32[]{:S(2)}) %collective-permute-start.5) | collective-permute-done | bytes 786464 | tf_op jit(solution)/shard_map/ppermute | solution.py:376
  63.6 2.7 %collective-permute-start.6 = (bf16[3,1024,128]{2,1,0:T(8,128)(2,1)}, bf16[3,1024,128]{2,1,0:T(8,128)(2,1)S(1)}, u32[]{:S(2)}, u32[]{:S(2)}) collective-permute-start(bf16[3,1024,128]{2,1,0:T(8,128)(2,1)} %get-tuple-element.18.refs_0_), channel_id=1, source_target_pairs={{0,7},{1,0},{2,1},{3,2},{4,3},{5,4},{6,5},{7,6},{8,15},{9,8},{10,9... | collective-permute-start | bytes 2359304 | tf_op jit(solution)/shard_map/ppermute | solution.py:377
  66.2 14.1 %collective-permute-done.9.refs_6_.refs_8_ = bf16[3,1024,128]{2,1,0:T(8,128)(2,1)S(1)} collective-permute-done((bf16[3,1024,128]{2,1,0:T(8,128)(2,1)}, bf16[3,1024,128]{2,1,0:T(8,128)(2,1)S(1)}, u32[]{:S(2)}, u32[]{:S(2)}) %collective-permute-start.9) | collective-permute-done | bytes 786464 | tf_op jit(solution)/shard_map/ppermute | solution.py:376
  83.0 13.3 %collective-permute-done.10.refs_5_.refs_7_ = bf16[3,1024,128]{2,1,0:T(8,128)(2,1)S(1)} collective-permute-done((bf16[3,1024,128]{2,1,0:T(8,128)(2,1)S(1)}, bf16[3,1024,128]{2,1,0:T(8,128)(2,1)S(1)}, u32[]{:S(2)}, u32[]{:S(2)}) %collective-permute-start.10) | collective-permute-done | bytes 786464 | tf_op jit(solution)/shard_map/ppermute | solution.py:376
  96.4 2.7 %collective-permute-start.8 = (bf16[3,1024,128]{2,1,0:T(8,128)(2,1)S(1)}, bf16[3,1024,128]{2,1,0:T(8,128)(2,1)S(1)}, u32[]{:S(2)}, u32[]{:S(2)}) collective-permute-start(bf16[3,1024,128]{2,1,0:T(8,128)(2,1)S(1)} %collective-permute-done.7.refs_2_), channel_id=1, source_target_pairs={{0,7},{1,0},{2,1},{3,2},{4,3},{5,4},{6,5},{7,6},{8,15},{9,8},{10,9... | collective-permute-start | bytes 2359304 | tf_op jit(solution)/shard_map/ppermute | solution.py:377
  102.7 2.7 %collective-permute-start.15 = (bf16[3,64,1024]{2,1,0:T(8,128)(2,1)}, bf16[3,64,1024]{2,1,0:T(8,128)(2,1)}, u32[]{:S(2)}, u32[]{:S(2)}) collective-permute-start(bf16[3,64,1024]{2,1,0:T(8,128)(2,1)} %slice.19), channel_id=1, source_target_pairs={{0,7},{1,0},{2,1},{3,2},{4,3},{5,4},{6,5},{7,6},{8,15},{9,8},{10,9... | collective-permute-start | bytes 1179656 | tf_op jit(solution)/shard_map/ppermute | solution.py:382
  105.4 7.0 %collective-permute-done.11.refs_4_.refs_6_ = bf16[3,1024,128]{2,1,0:T(8,128)(2,1)S(1)} collective-permute-done((bf16[3,1024,128]{2,1,0:T(8,128)(2,1)S(1)}, bf16[3,1024,128]{2,1,0:T(8,128)(2,1)S(1)}, u32[]{:S(2)}, u32[]{:S(2)}) %collective-permute-start.11) | collective-permute-done | bytes 786464 | tf_op jit(solution)/shard_map/ppermute | solution.py:376
  114.0 2.7 %collective-permute-start.13 = (bf16[3,512,128]{2,1,0:T(8,128)(2,1)}, bf16[3,512,128]{2,1,0:T(8,128)(2,1)}, u32[]{:S(2)}, u32[]{:S(2)}) collective-permute-start(bf16[3,512,128]{2,1,0:T(8,128)(2,1)} %slice.17), channel_id=1, source_target_pairs={{0,7},{1,0},{2,1},{3,2},{4,3},{5,4},{6,5},{7,6},{8,15},{9,8},{10,9... | collective-permute-start | bytes 1179656 | tf_op jit(solution)/shard_map/ppermute | solution.py:382
  116.7 6.9 %bulk.1.part_ref = f32[3,128,1024]{2,1,0:T(8,128)} custom-call(bf16[3,128,1024]{2,1,0:T(8,128)(2,1)} %left_ref.4, bf16[3,1024,128]{2,1,0:T(8,128)(2,1)} %get-tuple-element.18.refs_0_, bf16[3,1024,128]{2,1,0:T(8,128)(2,1)} %copy-done.5, bf16[3,1024,128]{2,1,0:T(8,128)(2,1)} %copy-done.7, bf16[3,1024,128]{2,1,0:T(8,128)(2,1)} %copy-done.1, ...), custom_call_target="tpu_custom_call" | custom-call | flops 1610612736 | bytes 15728640 | tf_op jit(solution)/shard_map/bulk/pallas_call | solution.py:176
  123.6 5.7 %collective-permute-done.12.refs_0_.refs_4_ = bf16[3,512,128]{2,1,0:T(8,128)(2,1)S(1)} collective-permute-done((bf16[3,512,128]{2,1,0:T(8,128)(2,1)}, bf16[3,512,128]{2,1,0:T(8,128)(2,1)S(1)}, u32[]{:S(2)}, u32[]{:S(2)}) %collective-permute-start.12) | collective-permute-done | bytes 393248 | tf_op jit(solution)/shard_map/ppermute | solution.py:381
  130.1 4.5 %precondition.1 = (bf16[400,128]{1,0:T(8,128)(2,1)}, bf16[400,128]{1,0:T(8,128)(2,1)}, bf16[400,128]{1,0:T(8,128)(2,1)}, bf16[400,128]{1,0:T(8,128)(2,1)}, bf16[...) custom-call(s32[1]{0:T(128)} %bitcast.place_ref, ...), custom_call_target="tpu_custom_call" | custom-call | flops 201326592 | bytes 1572864 | tf_op jit(solution)/shard_map/precondition/pallas_call | solution.py:234
  137.4 2.9 %collective-permute-start.19 = (bf16[400,128]{1,0:T(8,128)(2,1)}, bf16[400,128]{1,0:T(8,128)(2,1)S(1)}, u32[]{:S(2)}, u32[]{:S(2)}) collective-permute-start(bf16[400,128]{1,0:T(8,128)(2,1)} %get-tuple-element.23), channel_id=1, source_target_pairs={{0,4},{1,5},{2,6},{3,7},{4,0},{5,1},{6,2},{7,3},{8,12},{9,13},{10,... | collective-permute-start | bytes 307208 | tf_op jit(solution)/shard_map/ppermute | solution.py:402
  140.3 3.6 %collective-permute-start.20 = (bf16[400,128]{1,0:T(8,128)(2,1)}, bf16[400,128]{1,0:T(8,128)(2,1)S(1)}, u32[]{:S(2)}, u32[]{:S(2)}) collective-permute-start(bf16[400,128]{1,0:T(8,128)(2,1)} %get-tuple-element.24), channel_id=1, source_target_pairs={{0,5},{1,6},{2,7},{3,0},{4,1},{5,2},{6,3},{7,4},{8,13},{9,14},{10,... | collective-permute-start | bytes 307208 | tf_op jit(solution)/shard_map/ppermute | solution.py:402
  156.5 15.6 %all-to-all-start.1 = ((bf16[32,112,128]{2,1,0:T(8,128)(2,1)}), bf16[32,112,128]{2,1,0:T(8,128)(2,1)S(1)}, u32[]{:S(2)}, u32[]{:S(2)}) async-start(bf16[32,112,128]{2,1,0:T(8,128)(2,1)} %scale.1), calls=%async_computation.1 | async-start | bytes 1835008 | tf_op jit(solution)/shard_map/all_to_all | solution.py:404
  172.1 7.2 %factors.1 = (f32[3,128,1024]{2,1,0:T(8,128)}, f32[3,128,1024]{2,1,0:T(8,128)}) custom-call(s32[1]{0:T(128)} %bitcast.place_ref, f32[3,128,1024]{2,1,0:T(8,128)} %left_ref.5, f32[3,128,1024]{2,1,0:T(8,128)} %right_ref.1, bf16[3,1024,128]{2,1,0:T(8,128)(2,1)} %get-tuple-element.18.refs_0_, bf16[3,1024,128]{2,1,0:T(8,128)(2,1)} %copy-done.5, ...), custom_call_target="tpu_custom_call" | custom-call | flops 1610612736 | bytes 12582912 | tf_op jit(solution)/shard_map/factors/pallas_call | solution.py:358
  179.3 8.5 %all-to-all-done.1.got_ref = bf16[32,112,128]{2,1,0:T(8,128)(2,1)S(1)} async-done(((bf16[32,112,128]{2,1,0:T(8,128)(2,1)}), bf16[32,112,128]{2,1,0:T(8,128)(2,1)S(1)}, u32[]{:S(2)}, u32[]{:S(2)}) %all-to-all-start.1) | async-done | bytes 917536 | tf_op jit(solution)/shard_map/all_to_all | solution.py:404
  188.8 2.7 %finish.1 = bf16[96,32,128]{2,1,0:T(8,128)(2,1)} custom-call(s32[96]{0:T(128)} %slot_ref.3, bf16[32,112,128]{2,1,0:T(8,128)(2,1)} %copy-done.3), custom_call_target="tpu_custom_call" | custom-call | bytes 1835008 | tf_op jit(solution)/shard_map/finish/pallas_call | solution.py:318
  (73 shorter events, 30.3 us)
Async XLA Ops:
  0.6 23.0 %collective-permute-start = (bf16[3,128,1024]{2,1,0:T(8,128)(2,1)}, bf16[3,128,1024]{2,1,0:T(8,128)(2,1)S(1)}, u32[]{:S(2)}, u32[]{:S(2)}) collective-permute-start(bf16[3,128,1024]{2,1,0:T(8,128)(2,1)} %refs_7_.1), channel_id=1, source_target_pairs={{0,7},{1,0},{2,1},{3,2},{4,3},{5,4},{6,5},{7,6},{8,15},{9,8},{10,9... | collective-permute-start | bytes 2359304 | tf_op jit(solution)/shard_map/ppermute | solution.py:377
  7.1 19.8 %collective-permute-start.3 = (bf16[3,128,1024]{2,1,0:T(8,128)(2,1)}, bf16[3,128,1024]{2,1,0:T(8,128)(2,1)}, u32[]{:S(2)}, u32[]{:S(2)}) collective-permute-start(bf16[3,128,1024]{2,1,0:T(8,128)(2,1)} %refs_7_.1), channel_id=1, source_target_pairs={{0,1},{1,2},{2,3},{3,4},{4,5},{5,6},{6,7},{7,0},{8,9},{9,10},{10,1... | collective-permute-start | bytes 2359304 | tf_op jit(solution)/shard_map/ppermute | solution.py:376
  23.6 18.6 %collective-permute-start.1 = (bf16[3,128,1024]{2,1,0:T(8,128)(2,1)S(1)}, bf16[3,128,1024]{2,1,0:T(8,128)(2,1)}, u32[]{:S(2)}, u32[]{:S(2)}) collective-permute-start(bf16[3,128,1024]{2,1,0:T(8,128)(2,1)S(1)} %collective-permute-done.refs_8_), channel_id=1, source_target_pairs={{0,7},{1,0},{2,1},{3,2},{4,3},{5,4},{6,5},{7,6},{8,15},{9,8},{10,9... | collective-permute-start | bytes 2359304 | tf_op jit(solution)/shard_map/ppermute | solution.py:377
  26.9 18.8 %collective-permute-start.4 = (bf16[3,128,1024]{2,1,0:T(8,128)(2,1)}, bf16[3,128,1024]{2,1,0:T(8,128)(2,1)}, u32[]{:S(2)}, u32[]{:S(2)}) collective-permute-start(bf16[3,128,1024]{2,1,0:T(8,128)(2,1)} %collective-permute-done.3.refs_13_), channel_id=1, source_target_pairs={{0,1},{1,2},{2,3},{3,4},{4,5},{5,6},{6,7},{7,0},{8,9},{9,10},{10,1... | collective-permute-start | bytes 2359304 | tf_op jit(solution)/shard_map/ppermute | solution.py:376
  31.9 24.7 %all-to-all-start = ((bf16[32,112,128]{2,1,0:T(8,128)(2,1)}), bf16[32,112,128]{2,1,0:T(8,128)(2,1)S(1)}, u32[]{:S(2)}, u32[]{:S(2)}) async-start(bf16[32,112,128]{2,1,0:T(8,128)(2,1)} %prepare.1), calls=%async_computation | async-start | bytes 1835008 | tf_op jit(solution)/shard_map/all_to_all | solution.py:394
  42.2 18.2 %collective-permute-start.2 = (bf16[3,128,1024]{2,1,0:T(8,128)(2,1)}, bf16[3,128,1024]{2,1,0:T(8,128)(2,1)S(1)}, u32[]{:S(2)}, u32[]{:S(2)}) collective-permute-start(bf16[3,128,1024]{2,1,0:T(8,128)(2,1)} %collective-permute-done.1.refs_9_), channel_id=1, source_target_pairs={{0,7},{1,0},{2,1},{3,2},{4,3},{5,4},{6,5},{7,6},{8,15},{9,8},{10,9... | collective-permute-start | bytes 2359304 | tf_op jit(solution)/shard_map/ppermute | solution.py:377
  45.8 17.8 %collective-permute-start.5 = (bf16[3,128,1024]{2,1,0:T(8,128)(2,1)}, bf16[3,128,1024]{2,1,0:T(8,128)(2,1)}, u32[]{:S(2)}, u32[]{:S(2)}) collective-permute-start(bf16[3,128,1024]{2,1,0:T(8,128)(2,1)} %collective-permute-done.4.refs_12_), channel_id=1, source_target_pairs={{0,1},{1,2},{2,3},{3,4},{4,5},{5,6},{6,7},{7,0},{8,9},{9,10},{10,1... | collective-permute-start | bytes 2359304 | tf_op jit(solution)/shard_map/ppermute | solution.py:376
  63.6 16.8 %collective-permute-start.9 = (bf16[3,1024,128]{2,1,0:T(8,128)(2,1)}, bf16[3,1024,128]{2,1,0:T(8,128)(2,1)S(1)}, u32[]{:S(2)}, u32[]{:S(2)}) collective-permute-start(bf16[3,1024,128]{2,1,0:T(8,128)(2,1)} %get-tuple-element.18.refs_0_), channel_id=1, source_target_pairs={{0,1},{1,2},{2,3},{3,4},{4,5},{5,6},{6,7},{7,0},{8,9},{9,10},{10,1... | collective-permute-start | bytes 2359304 | tf_op jit(solution)/shard_map/ppermute | solution.py:376
  63.6 16.8 %collective-permute-start.6 = (bf16[3,1024,128]{2,1,0:T(8,128)(2,1)}, bf16[3,1024,128]{2,1,0:T(8,128)(2,1)S(1)}, u32[]{:S(2)}, u32[]{:S(2)}) collective-permute-start(bf16[3,1024,128]{2,1,0:T(8,128)(2,1)} %get-tuple-element.18.refs_0_), channel_id=1, source_target_pairs={{0,7},{1,0},{2,1},{3,2},{4,3},{5,4},{6,5},{7,6},{8,15},{9,8},{10,9... | collective-permute-start | bytes 2359304 | tf_op jit(solution)/shard_map/ppermute | solution.py:377
  80.4 16.0 %collective-permute-start.10 = (bf16[3,1024,128]{2,1,0:T(8,128)(2,1)S(1)}, bf16[3,1024,128]{2,1,0:T(8,128)(2,1)S(1)}, u32[]{:S(2)}, u32[]{:S(2)}) collective-permute-start(bf16[3,1024,128]{2,1,0:T(8,128)(2,1)S(1)} %collective-permute-done.9.refs_6_.refs_8_), channel_id=1, source_target_pairs={{0,1},{1,2},{2,3},{3,4},{4,5},{5,6},{6,7},{7,0},{8,9},{9,10},{10,1... | collective-permute-start | bytes 2359304 | tf_op jit(solution)/shard_map/ppermute | solution.py:376
  80.4 16.0 %collective-permute-start.7 = (bf16[3,1024,128]{2,1,0:T(8,128)(2,1)S(1)}, bf16[3,1024,128]{2,1,0:T(8,128)(2,1)S(1)}, u32[]{:S(2)}, u32[]{:S(2)}) collective-permute-start(bf16[3,1024,128]{2,1,0:T(8,128)(2,1)S(1)} %collective-permute-done.6.refs_1_), channel_id=1, source_target_pairs={{0,7},{1,0},{2,1},{3,2},{4,3},{5,4},{6,5},{7,6},{8,15},{9,8},{10,9... | collective-permute-start | bytes 2359304 | tf_op jit(solution)/shard_map/ppermute | solution.py:377
  96.4 16.0 %collective-permute-start.11 = (bf16[3,1024,128]{2,1,0:T(8,128)(2,1)S(1)}, bf16[3,1024,128]{2,1,0:T(8,128)(2,1)S(1)}, u32[]{:S(2)}, u32[]{:S(2)}) collective-permute-start(bf16[3,1024,128]{2,1,0:T(8,128)(2,1)S(1)} %collective-permute-done.10.refs_5_.refs_7_), channel_id=1, source_target_pairs={{0,1},{1,2},{2,3},{3,4},{4,5},{5,6},{6,7},{7,0},{8,9},{9,10},{10,1... | collective-permute-start | bytes 2359304 | tf_op jit(solution)/shard_map/ppermute | solution.py:376
  96.4 16.8 %collective-permute-start.8 = (bf16[3,1024,128]{2,1,0:T(8,128)(2,1)S(1)}, bf16[3,1024,128]{2,1,0:T(8,128)(2,1)S(1)}, u32[]{:S(2)}, u32[]{:S(2)}) collective-permute-start(bf16[3,1024,128]{2,1,0:T(8,128)(2,1)S(1)} %collective-permute-done.7.refs_2_), channel_id=1, source_target_pairs={{0,7},{1,0},{2,1},{3,2},{4,3},{5,4},{6,5},{7,6},{8,15},{9,8},{10,9... | collective-permute-start | bytes 2359304 | tf_op jit(solution)/shard_map/ppermute | solution.py:377
  100.9 22.7 %collective-permute-start.14 = (bf16[3,64,1024]{2,1,0:T(8,128)(2,1)}, bf16[3,64,1024]{2,1,0:T(8,128)(2,1)}, u32[]{:S(2)}, u32[]{:S(2)}) collective-permute-start(bf16[3,64,1024]{2,1,0:T(8,128)(2,1)} %slice.18), channel_id=1, source_target_pairs={{0,1},{1,2},{2,3},{3,4},{4,5},{5,6},{6,7},{7,0},{8,9},{9,10},{10,1... | collective-permute-start | bytes 1179656 | tf_op jit(solution)/shard_map/ppermute | solution.py:381
  102.7 20.9 %collective-permute-start.15 = (bf16[3,64,1024]{2,1,0:T(8,128)(2,1)}, bf16[3,64,1024]{2,1,0:T(8,128)(2,1)}, u32[]{:S(2)}, u32[]{:S(2)}) collective-permute-start(bf16[3,64,1024]{2,1,0:T(8,128)(2,1)} %slice.19), channel_id=1, source_target_pairs={{0,7},{1,0},{2,1},{3,2},{4,3},{5,4},{6,5},{7,6},{8,15},{9,8},{10,9... | collective-permute-start | bytes 1179656 | tf_op jit(solution)/shard_map/ppermute | solution.py:382
  113.2 16.2 %collective-permute-start.12 = (bf16[3,512,128]{2,1,0:T(8,128)(2,1)}, bf16[3,512,128]{2,1,0:T(8,128)(2,1)S(1)}, u32[]{:S(2)}, u32[]{:S(2)}) collective-permute-start(bf16[3,512,128]{2,1,0:T(8,128)(2,1)} %slice.16), channel_id=1, source_target_pairs={{0,1},{1,2},{2,3},{3,4},{4,5},{5,6},{6,7},{7,0},{8,9},{9,10},{10,1... | collective-permute-start | bytes 1179656 | tf_op jit(solution)/shard_map/ppermute | solution.py:381
  114.0 15.3 %collective-permute-start.13 = (bf16[3,512,128]{2,1,0:T(8,128)(2,1)}, bf16[3,512,128]{2,1,0:T(8,128)(2,1)}, u32[]{:S(2)}, u32[]{:S(2)}) collective-permute-start(bf16[3,512,128]{2,1,0:T(8,128)(2,1)} %slice.17), channel_id=1, source_target_pairs={{0,7},{1,0},{2,1},{3,2},{4,3},{5,4},{6,5},{7,6},{8,15},{9,8},{10,9... | collective-permute-start | bytes 1179656 | tf_op jit(solution)/shard_map/ppermute | solution.py:382
  134.6 9.3 %collective-permute-start.16 = (bf16[400,128]{1,0:T(8,128)(2,1)}, bf16[400,128]{1,0:T(8,128)(2,1)S(1)}, u32[]{:S(2)}, u32[]{:S(2)}) collective-permute-start(bf16[400,128]{1,0:T(8,128)(2,1)} %get-tuple-element.20), channel_id=1, source_target_pairs={{0,1},{1,2},{2,3},{3,4},{4,5},{5,6},{6,7},{7,0},{8,9},{9,10},{10,1... | collective-permute-start | bytes 307208 | tf_op jit(solution)/shard_map/ppermute | solution.py:402
  134.7 10.3 %collective-permute-start.17 = (bf16[400,128]{1,0:T(8,128)(2,1)}, bf16[400,128]{1,0:T(8,128)(2,1)S(1)}, u32[]{:S(2)}, u32[]{:S(2)}) collective-permute-start(bf16[400,128]{1,0:T(8,128)(2,1)} %get-tuple-element.21), channel_id=1, source_target_pairs={{0,2},{1,3},{2,4},{3,5},{4,6},{5,7},{6,0},{7,1},{8,10},{9,11},{10,... | collective-permute-start | bytes 307208 | tf_op jit(solution)/shard_map/ppermute | solution.py:402
  136.2 11.8 %collective-permute-start.18 = (bf16[400,128]{1,0:T(8,128)(2,1)}, bf16[400,128]{1,0:T(8,128)(2,1)S(1)}, u32[]{:S(2)}, u32[]{:S(2)}) collective-permute-start(bf16[400,128]{1,0:T(8,128)(2,1)} %get-tuple-element.22), channel_id=1, source_target_pairs={{0,3},{1,4},{2,5},{3,6},{4,7},{5,0},{6,1},{7,2},{8,11},{9,12},{10,... | collective-permute-start | bytes 307208 | tf_op jit(solution)/shard_map/ppermute | solution.py:402
  137.4 11.1 %collective-permute-start.19 = (bf16[400,128]{1,0:T(8,128)(2,1)}, bf16[400,128]{1,0:T(8,128)(2,1)S(1)}, u32[]{:S(2)}, u32[]{:S(2)}) collective-permute-start(bf16[400,128]{1,0:T(8,128)(2,1)} %get-tuple-element.23), channel_id=1, source_target_pairs={{0,4},{1,5},{2,6},{3,7},{4,0},{5,1},{6,2},{7,3},{8,12},{9,13},{10,... | collective-permute-start | bytes 307208 | tf_op jit(solution)/shard_map/ppermute | solution.py:402
  140.3 8.2 %collective-permute-start.20 = (bf16[400,128]{1,0:T(8,128)(2,1)}, bf16[400,128]{1,0:T(8,128)(2,1)S(1)}, u32[]{:S(2)}, u32[]{:S(2)}) collective-permute-start(bf16[400,128]{1,0:T(8,128)(2,1)} %get-tuple-element.24), channel_id=1, source_target_pairs={{0,5},{1,6},{2,7},{3,0},{4,1},{5,2},{6,3},{7,4},{8,13},{9,14},{10,... | collective-permute-start | bytes 307208 | tf_op jit(solution)/shard_map/ppermute | solution.py:402
  145.0 8.6 %collective-permute-start.22 = (bf16[400,128]{1,0:T(8,128)(2,1)}, bf16[400,128]{1,0:T(8,128)(2,1)S(1)}, u32[]{:S(2)}, u32[]{:S(2)}) collective-permute-start(bf16[400,128]{1,0:T(8,128)(2,1)} %get-tuple-element.26), channel_id=1, source_target_pairs={{0,7},{1,0},{2,1},{3,2},{4,3},{5,4},{6,5},{7,6},{8,15},{9,8},{10,9... | collective-permute-start | bytes 307208 | tf_op jit(solution)/shard_map/ppermute | solution.py:402
  156.5 31.4 %all-to-all-start.1 = ((bf16[32,112,128]{2,1,0:T(8,128)(2,1)}), bf16[32,112,128]{2,1,0:T(8,128)(2,1)S(1)}, u32[]{:S(2)}, u32[]{:S(2)}) async-start(bf16[32,112,128]{2,1,0:T(8,128)(2,1)} %scale.1), calls=%async_computation.1 | async-start | bytes 1835008 | tf_op jit(solution)/shard_map/all_to_all | solution.py:404
  (19 other events, 166.0 us)

commit v3 on v2

--- a/solution.py
+++ b/solution.py
@@ -19,8 +19,8 @@
 SMEM = pltpu.SMEM
 
 
-def params():
-    return pltpu.CompilerParams(vmem_limit_bytes=62 * 1024 * 1024)
+def params(mib):
+    return pltpu.CompilerParams(vmem_limit_bytes=mib * 1024 * 1024)
 
 
 def scalars():
@@ -84,7 +84,7 @@
         grid=(1,),
         in_specs=[scalars()] + [whole(gradient.shape)] * 3,
         out_specs=whole((owners, count * rows + PAD, 128)),
-        compiler_params=params(),
+        compiler_params=params(62),
         cost_estimate=cost(20 * gradient.size, 12 * gradient.size),
         name="prepare",
     )(slot_block, gradient, first_moment, second_moment)
@@ -114,7 +114,7 @@
         grid=(1,),
         in_specs=[whole(got.shape)],
         out_specs=[whole(shape), whole((PAD, 128))],
-        compiler_params=params(),
+        compiler_params=params(16),
         cost_estimate=cost(0, 4 * got.size),
         name="unpack",
     )(got)
@@ -179,7 +179,7 @@
         grid=(count,),
         in_specs=[slot_of(left_root.shape)] + [slot_of(panel.shape) for panel in early],
         out_specs=slot_of(left_root.shape),
-        compiler_params=params(),
+        compiler_params=params(62),
         cost_estimate=cost(count * 4 * rows * order * order, count * 5 * order * order),
         name="bulk",
     )(left_root, *early)
@@ -239,7 +239,7 @@
         + [slot_of(panel.shape) for panel in late],
         out_specs=[whole(out)] * 8,
         scratch_shapes=[pltpu.VMEM((1, 128), F32)],
-        compiler_params=params(),
+        compiler_params=params(16),
         cost_estimate=cost(count * 4 * rows * 128 * order, count * 4 * rows * order),
         name="precondition",
     )(place, left_root, adam, part, *late)
@@ -285,7 +285,7 @@
         grid=(1,),
         in_specs=[scalars()] + [whole(got.shape) for got in gots],
         out_specs=whole(out),
-        compiler_params=params(),
+        compiler_params=params(16),
         cost_estimate=cost(0, 32 * gots[0].size),
         name="scale",
     )(place, *gots)
@@ -321,7 +321,7 @@
         grid=(1,),
         in_specs=[scalars(), whole(got.shape)],
         out_specs=whole(out),
-        compiler_params=params(),
+        compiler_params=params(16),
         cost_estimate=cost(0, 4 * got.size),
         name="finish",
     )(slot_block, got)
@@ -362,7 +362,7 @@
         in_specs=[scalars(), slot_of(left_stat.shape), slot_of(right_stat.shape)]
         + [slot_of(grad.shape) for grad in grads],
         out_specs=[slot_of(left_stat.shape)] * 2,
-        compiler_params=params(),
+        compiler_params=params(62),
         cost_estimate=cost(count * 4 * 128 * order * order, count * 4 * order * order),
         name="factors",
     )(place, left_stat, right_stat, *grads)

time: 192 us -> 188 us (0.979)
  waiting for transfers between devices: 88.6 us -> 96.7 us
  Pallas kernels: 30.8 us -> 25.7 us
  local copies, waits for them, and re-layouts: 8.45 us -> 3.91 us
  starting transfers between devices: 62.9 us -> 60.1 us
    ppermute x7, waiting for transfers between devices: 7.21 us -> 10.2 us  [shards(): gots[k] = lax.ppermute(sents[k], 'mp', [(i, (i + k) % 8) for i in range(8)])]
    ppermute x6, waiting for transfers between devices: 18.8 us -> 21.7 us  [ring(): from_above.append(lax.ppermute(from_above[-1], 'mp', down))]
    all_to_all x2, starting transfers between devices: 24.5 us -> 21.7 us  [shards(): got = lax.all_to_all(sent, 'dp', split_axis=0, concat_axis=0, tiled=True)]
    ppermute x6, waiting for transfers between devices: 37.5 us -> 40 us  [ring(): from_below.append(lax.ppermute(from_below[-1], 'mp', up))]
    pallas_call x1, Pallas kernels: 2.11 us -> 0.09 us  [unpack(): pl.pallas_call(unpack_kernel, out_shape=[jax.ShapeDtypeStruct(shape, BF16...]
  transfers between devices with their start and end apart: 25 -> 25, of which waited for: 14 -> 15; matrix products, arithmetic and copies ran while one was open for 3% -> 1% of each run, Pallas kernels for 11% -> 10%
where the time goes in v3:
time: 188 us; the launch traced here: 187 us
  waiting for transfers between devices  96.7 us (51%)
  starting transfers between devices  60.1 us (32%)
  Pallas kernels  25.7 us (14%)
  local copies, waits for them, and re-layouts  3.91 us (2%)
    ppermute x6, waiting for transfers between devices, ring(): from_below.append(lax.ppermute(from_below[-1], 'mp', up))  40 us
    all_to_all x2, starting transfers between devices, shards(): got = lax.all_to_all(sent, 'dp', split_axis=0, concat_axis=0, tiled=True)  21.7 us
    ppermute x6, waiting for transfers between devices, ring(): from_above.append(lax.ppermute(from_above[-1], 'mp', down))  21.7 us
    ppermute x6, starting transfers between devices, ring(): from_above.append(lax.ppermute(from_above[-1], 'mp', down))  21.3 us
    all_to_all x2, waiting for transfers between devices, shards(): got = lax.all_to_all(sent, 'dp', split_axis=0, concat_axis=0, tiled=True)  19.4 us
    ppermute x7, starting transfers between devices, shards(): gots[k] = lax.ppermute(sents[k], 'mp', [(i, (i + k) % 8) for i in range(8)])  11.7 us
    ppermute x7, waiting for transfers between devices, shards(): gots[k] = lax.ppermute(sents[k], 'mp', [(i, (i + k) % 8) for i in range(8)])  10.2 us
    pallas_call x1, Pallas kernels, factors(): pl.pallas_call(factors_kernel, out_shape=[jax.ShapeDtypeStruct(left_stat....  7.24 us
  transfers between devices with their start and end apart: 25, of which 15 were waited for; matrix products, arithmetic and copies ran while one was open for 1% of the time, Pallas kernels for 10%

profile of v3, /device:TPU:1, one launch (start us, length us, event | category | flops | bytes accessed | tf_op | source)
XLA Modules:
  0.0 187.3 jit_solution(7350545143564147820)
XLA Ops:
  0.6 6.5 %collective-permute-start = (bf16[3,128,1024]{2,1,0:T(8,128)(2,1)}, bf16[3,128,1024]{2,1,0:T(8,128)(2,1)S(1)}, u32[]{:S(2)}, u32[]{:S(2)}) collective-permute-start(bf16[3,128,1024]{2,1,0:T(8,128)(2,1)} %refs_7_.1), channel_id=1, source_target_pairs={{0,7},{1,0},{2,1},{3,2},{4,3},{5,4},{6,5},{7,6},{8,15},{9,8},{10,9... | collective-permute-start | bytes 2359304 | tf_op jit(solution)/shard_map/ppermute | solution.py:377
  7.1 16.5 %collective-permute-done.refs_8_ = bf16[3,128,1024]{2,1,0:T(8,128)(2,1)S(1)} collective-permute-done((bf16[3,128,1024]{2,1,0:T(8,128)(2,1)}, bf16[3,128,1024]{2,1,0:T(8,128)(2,1)S(1)}, u32[]{:S(2)}, u32[]{:S(2)}) %collective-permute-start) | collective-permute-done | bytes 786464 | tf_op jit(solution)/shard_map/ppermute | solution.py:377
  23.6 3.3 %collective-permute-start.1 = (bf16[3,128,1024]{2,1,0:T(8,128)(2,1)S(1)}, bf16[3,128,1024]{2,1,0:T(8,128)(2,1)}, u32[]{:S(2)}, u32[]{:S(2)}) collective-permute-start(bf16[3,128,1024]{2,1,0:T(8,128)(2,1)S(1)} %collective-permute-done.refs_8_), channel_id=1, source_target_pairs={{0,7},{1,0},{2,1},{3,2},{4,3},{5,4},{6,5},{7,6},{8,15},{9,8},{10,9... | collective-permute-start | bytes 2359304 | tf_op jit(solution)/shard_map/ppermute | solution.py:377
  27.0 5.0 %prepare.1 = bf16[32,112,128]{2,1,0:T(8,128)(2,1)} custom-call(s32[96]{0:T(128)} %slot_ref.3, bf16[96,32,128]{2,1,0:T(8,128)(2,1)} %grad_ref.1, f32[96,32,128]{2,1,0:T(8,128)} %one_ref.1, f32[96,32,128]{2,1,0:T(8,128)} %two_ref.1), custom_call_target="tpu_custom_call" | custom-call | flops 7864320 | bytes 4718592 | tf_op jit(solution)/shard_map/prepare/pallas_call | solution.py:81
  31.9 8.9 %all-to-all-start = ((bf16[32,112,128]{2,1,0:T(8,128)(2,1)}), bf16[32,112,128]{2,1,0:T(8,128)(2,1)S(1)}, u32[]{:S(2)}, u32[]{:S(2)}) async-start(bf16[32,112,128]{2,1,0:T(8,128)(2,1)} %prepare.1), calls=%async_computation | async-start | bytes 1835008 | tf_op jit(solution)/shard_map/all_to_all | solution.py:394
  42.2 3.5 %collective-permute-start.2 = (bf16[3,128,1024]{2,1,0:T(8,128)(2,1)}, bf16[3,128,1024]{2,1,0:T(8,128)(2,1)S(1)}, u32[]{:S(2)}, u32[]{:S(2)}) collective-permute-start(bf16[3,128,1024]{2,1,0:T(8,128)(2,1)} %collective-permute-done.1.refs_9_), channel_id=1, source_target_pairs={{0,7},{1,0},{2,1},{3,2},{4,3},{5,4},{6,5},{7,6},{8,15},{9,8},{10,9... | collective-permute-start | bytes 2359304 | tf_op jit(solution)/shard_map/ppermute | solution.py:377
  45.8 10.8 %all-to-all-done.got_ref = bf16[32,112,128]{2,1,0:T(8,128)(2,1)S(1)} async-done(((bf16[32,112,128]{2,1,0:T(8,128)(2,1)}), bf16[32,112,128]{2,1,0:T(8,128)(2,1)S(1)}, u32[]{:S(2)}, u32[]{:S(2)}) %all-to-all-start) | async-done | bytes 917536 | tf_op jit(solution)/shard_map/all_to_all | solution.py:394
  56.7 3.7 %collective-permute-done.2.refs_10_ = bf16[3,128,1024]{2,1,0:T(8,128)(2,1)S(1)} collective-permute-done((bf16[3,128,1024]{2,1,0:T(8,128)(2,1)}, bf16[3,128,1024]{2,1,0:T(8,128)(2,1)S(1)}, u32[]{:S(2)}, u32[]{:S(2)}) %collective-permute-start.2) | collective-permute-done | bytes 786464 | tf_op jit(solution)/shard_map/ppermute | solution.py:377
  60.4 3.0 %collective-permute-done.5.refs_11_ = bf16[3,128,1024]{2,1,0:T(8,128)(2,1)S(1)} collective-permute-done((bf16[3,128,1024]{2,1,0:T(8,128)(2,1)}, bf16[3,128,1024]{2,1,0:T(8,128)(2,1)S(1)}, u32[]{:S(2)}, u32[]{:S(2)}) %collective-permute-start.5) | collective-permute-done | bytes 786464 | tf_op jit(solution)/shard_map/ppermute | solution.py:376
  63.5 2.7 %collective-permute-start.6 = (bf16[3,1024,128]{2,1,0:T(8,128)(2,1)S(1)}, bf16[3,1024,128]{2,1,0:T(8,128)(2,1)S(1)}, u32[]{:S(2)}, u32[]{:S(2)}) collective-permute-start(bf16[3,1024,128]{2,1,0:T(8,128)(2,1)S(1)} %get-tuple-element.18.refs_0_), channel_id=1, source_target_pairs={{0,7},{1,0},{2,1},{3,2},{4,3},{5,4},{6,5},{7,6},{8,15},{9,8},{10,9... | collective-permute-start | bytes 2359304 | tf_op jit(solution)/shard_map/ppermute | solution.py:377
  66.1 13.9 %collective-permute-done.9.refs_6_.refs_8_ = bf16[3,1024,128]{2,1,0:T(8,128)(2,1)S(1)} collective-permute-done((bf16[3,1024,128]{2,1,0:T(8,128)(2,1)S(1)}, bf16[3,1024,128]{2,1,0:T(8,128)(2,1)S(1)}, u32[]{:S(2)}, u32[]{:S(2)}) %collective-permute-start.9) | collective-permute-done | bytes 786464 | tf_op jit(solution)/shard_map/ppermute | solution.py:376
  80.1 2.7 %collective-permute-start.7 = (bf16[3,1024,128]{2,1,0:T(8,128)(2,1)S(1)}, bf16[3,1024,128]{2,1,0:T(8,128)(2,1)S(1)}, u32[]{:S(2)}, u32[]{:S(2)}) collective-permute-start(bf16[3,1024,128]{2,1,0:T(8,128)(2,1)S(1)} %collective-permute-done.6.refs_1_), channel_id=1, source_target_pairs={{0,7},{1,0},{2,1},{3,2},{4,3},{5,4},{6,5},{7,6},{8,15},{9,8},{10,9... | collective-permute-start | bytes 2359304 | tf_op jit(solution)/shard_map/ppermute | solution.py:377
  82.7 13.3 %collective-permute-done.10.refs_5_.refs_7_ = bf16[3,1024,128]{2,1,0:T(8,128)(2,1)S(1)} collective-permute-done((bf16[3,1024,128]{2,1,0:T(8,128)(2,1)S(1)}, bf16[3,1024,128]{2,1,0:T(8,128)(2,1)S(1)}, u32[]{:S(2)}, u32[]{:S(2)}) %collective-permute-start.10) | collective-permute-done | bytes 786464 | tf_op jit(solution)/shard_map/ppermute | solution.py:376
  96.1 2.7 %collective-permute-start.8 = (bf16[3,1024,128]{2,1,0:T(8,128)(2,1)S(1)}, bf16[3,1024,128]{2,1,0:T(8,128)(2,1)S(1)}, u32[]{:S(2)}, u32[]{:S(2)}) collective-permute-start(bf16[3,1024,128]{2,1,0:T(8,128)(2,1)S(1)} %collective-permute-done.7.refs_2_), channel_id=1, source_target_pairs={{0,7},{1,0},{2,1},{3,2},{4,3},{5,4},{6,5},{7,6},{8,15},{9,8},{10,9... | collective-permute-start | bytes 2359304 | tf_op jit(solution)/shard_map/ppermute | solution.py:377
  99.6 2.7 %collective-permute-start.15 = (bf16[3,64,1024]{2,1,0:T(8,128)(2,1)}, bf16[3,64,1024]{2,1,0:T(8,128)(2,1)}, u32[]{:S(2)}, u32[]{:S(2)}) collective-permute-start(bf16[3,64,1024]{2,1,0:T(8,128)(2,1)} %slice.19), channel_id=1, source_target_pairs={{0,7},{1,0},{2,1},{3,2},{4,3},{5,4},{6,5},{7,6},{8,15},{9,8},{10,9... | collective-permute-start | bytes 1179656 | tf_op jit(solution)/shard_map/ppermute | solution.py:382
  102.3 9.7 %collective-permute-done.11.refs_4_.refs_6_ = bf16[3,1024,128]{2,1,0:T(8,128)(2,1)S(1)} collective-permute-done((bf16[3,1024,128]{2,1,0:T(8,128)(2,1)S(1)}, bf16[3,1024,128]{2,1,0:T(8,128)(2,1)S(1)}, u32[]{:S(2)}, u32[]{:S(2)}) %collective-permute-start.11) | collective-permute-done | bytes 786464 | tf_op jit(solution)/shard_map/ppermute | solution.py:376
  116.4 7.0 %bulk.1.part_ref = f32[3,128,1024]{2,1,0:T(8,128)} custom-call(bf16[3,128,1024]{2,1,0:T(8,128)(2,1)} %left_ref.4, bf16[3,1024,128]{2,1,0:T(8,128)(2,1)} %copy-done.1, bf16[3,1024,128]{2,1,0:T(8,128)(2,1)} %copy-done.7, bf16[3,1024,128]{2,1,0:T(8,128)(2,1)} %copy-done.9, bf16[3,1024,128]{2,1,0:T(8,128)(2,1)} %copy-done.5, bf16[3,1024,128]{2,1,0:T(8,128)(2,1)} %copy-done.4, ...), custom_call_target="tpu_custom_call" | custom-call | flops 1610612736 | bytes 15728640 | tf_op jit(solution)/shard_map/bulk/pallas_call | solution.py:176
  123.4 5.6 %collective-permute-done.12.refs_0_.refs_4_ = bf16[3,512,128]{2,1,0:T(8,128)(2,1)} collective-permute-done((bf16[3,512,128]{2,1,0:T(8,128)(2,1)}, bf16[3,512,128]{2,1,0:T(8,128)(2,1)}, u32[]{:S(2)}, u32[]{:S(2)}) %collective-permute-start.12) | collective-permute-done | bytes 393248 | tf_op jit(solution)/shard_map/ppermute | solution.py:381
  130.4 3.2 %precondition.1 = (bf16[400,128]{1,0:T(8,128)(2,1)S(1)}, bf16[400,128]{1,0:T(8,128)(2,1)S(1)}, bf16[400,128]{1,0:T(8,128)(2,1)S(1)}, bf16[400,128]{1,0:T(8,128)(...) custom-call(s32[1]{0:T(128)} %bitcast.place_ref, ...), custom_call_target="tpu_custom_call" | custom-call | flops 201326592 | bytes 1572864 | tf_op jit(solution)/shard_map/precondition/pallas_call | solution.py:234
  139.4 4.4 %collective-permute-start.20 = (bf16[400,128]{1,0:T(8,128)(2,1)S(1)}, bf16[400,128]{1,0:T(8,128)(2,1)S(1)}, u32[]{:S(2)}, u32[]{:S(2)}) collective-permute-start(bf16[400,128]{1,0:T(8,128)(2,1)S(1)} %get-tuple-element.24), channel_id=1, source_target_pairs={{0,5},{1,6},{2,7},{3,0},{4,1},{5,2},{6,3},{7,4},{8,13},{9,14},{10,... | collective-permute-start | bytes 307208 | tf_op jit(solution)/shard_map/ppermute | solution.py:402
  151.2 4.3 %collective-permute-done.22.refs_7_ = bf16[400,128]{1,0:T(8,128)(2,1)S(1)} collective-permute-done((bf16[400,128]{1,0:T(8,128)(2,1)S(1)}, bf16[400,128]{1,0:T(8,128)(2,1)S(1)}, u32[]{:S(2)}, u32[]{:S(2)}) %collective-permute-start.22) | collective-permute-done | bytes 102432 | tf_op jit(solution)/shard_map/ppermute | solution.py:402
  156.7 12.8 %all-to-all-start.1 = ((bf16[32,112,128]{2,1,0:T(8,128)(2,1)}), bf16[32,112,128]{2,1,0:T(8,128)(2,1)S(1)}, u32[]{:S(2)}, u32[]{:S(2)}) async-start(bf16[32,112,128]{2,1,0:T(8,128)(2,1)} %scale.1), calls=%async_computation.1 | async-start | bytes 1835008 | tf_op jit(solution)/shard_map/all_to_all | solution.py:404
  169.5 7.2 %factors.1 = (f32[3,128,1024]{2,1,0:T(8,128)}, f32[3,128,1024]{2,1,0:T(8,128)}) custom-call(s32[1]{0:T(128)} %bitcast.place_ref, f32[3,128,1024]{2,1,0:T(8,128)} %left_ref.5, f32[3,128,1024]{2,1,0:T(8,128)} %right_ref.1, bf16[3,1024,128]{2,1,0:T(8,128)(2,1)} %copy-done.1, bf16[3,1024,128]{2,1,0:T(8,128)(2,1)} %copy-done.7, bf16[3,1024,128]{2,1,0:T(8,128)(2,1)} %copy-done.9, ...), custom_call_target="tpu_custom_call" | custom-call | flops 1610612736 | bytes 12582912 | tf_op jit(solution)/shard_map/factors/pallas_call | solution.py:358
  176.7 8.5 %all-to-all-done.1.got_ref = bf16[32,112,128]{2,1,0:T(8,128)(2,1)S(1)} async-done(((bf16[32,112,128]{2,1,0:T(8,128)(2,1)}), bf16[32,112,128]{2,1,0:T(8,128)(2,1)S(1)}, u32[]{:S(2)}, u32[]{:S(2)}) %all-to-all-start.1) | async-done | bytes 917536 | tf_op jit(solution)/shard_map/all_to_all | solution.py:404
  (63 shorter events, 24.5 us)
Async XLA Ops:
  0.6 23.0 %collective-permute-start = (bf16[3,128,1024]{2,1,0:T(8,128)(2,1)}, bf16[3,128,1024]{2,1,0:T(8,128)(2,1)S(1)}, u32[]{:S(2)}, u32[]{:S(2)}) collective-permute-start(bf16[3,128,1024]{2,1,0:T(8,128)(2,1)} %refs_7_.1), channel_id=1, source_target_pairs={{0,7},{1,0},{2,1},{3,2},{4,3},{5,4},{6,5},{7,6},{8,15},{9,8},{10,9... | collective-permute-start | bytes 2359304 | tf_op jit(solution)/shard_map/ppermute | solution.py:377
  7.1 19.8 %collective-permute-start.3 = (bf16[3,128,1024]{2,1,0:T(8,128)(2,1)}, bf16[3,128,1024]{2,1,0:T(8,128)(2,1)}, u32[]{:S(2)}, u32[]{:S(2)}) collective-permute-start(bf16[3,128,1024]{2,1,0:T(8,128)(2,1)} %refs_7_.1), channel_id=1, source_target_pairs={{0,1},{1,2},{2,3},{3,4},{4,5},{5,6},{6,7},{7,0},{8,9},{9,10},{10,1... | collective-permute-start | bytes 2359304 | tf_op jit(solution)/shard_map/ppermute | solution.py:376
  23.6 18.6 %collective-permute-start.1 = (bf16[3,128,1024]{2,1,0:T(8,128)(2,1)S(1)}, bf16[3,128,1024]{2,1,0:T(8,128)(2,1)}, u32[]{:S(2)}, u32[]{:S(2)}) collective-permute-start(bf16[3,128,1024]{2,1,0:T(8,128)(2,1)S(1)} %collective-permute-done.refs_8_), channel_id=1, source_target_pairs={{0,7},{1,0},{2,1},{3,2},{4,3},{5,4},{6,5},{7,6},{8,15},{9,8},{10,9... | collective-permute-start | bytes 2359304 | tf_op jit(solution)/shard_map/ppermute | solution.py:377
  26.9 18.8 %collective-permute-start.4 = (bf16[3,128,1024]{2,1,0:T(8,128)(2,1)}, bf16[3,128,1024]{2,1,0:T(8,128)(2,1)}, u32[]{:S(2)}, u32[]{:S(2)}) collective-permute-start(bf16[3,128,1024]{2,1,0:T(8,128)(2,1)} %collective-permute-done.3.refs_13_), channel_id=1, source_target_pairs={{0,1},{1,2},{2,3},{3,4},{4,5},{5,6},{6,7},{7,0},{8,9},{9,10},{10,1... | collective-permute-start | bytes 2359304 | tf_op jit(solution)/shard_map/ppermute | solution.py:376
  31.9 24.7 %all-to-all-start = ((bf16[32,112,128]{2,1,0:T(8,128)(2,1)}), bf16[32,112,128]{2,1,0:T(8,128)(2,1)S(1)}, u32[]{:S(2)}, u32[]{:S(2)}) async-start(bf16[32,112,128]{2,1,0:T(8,128)(2,1)} %prepare.1), calls=%async_computation | async-start | bytes 1835008 | tf_op jit(solution)/shard_map/all_to_all | solution.py:394
  42.2 18.2 %collective-permute-start.2 = (bf16[3,128,1024]{2,1,0:T(8,128)(2,1)}, bf16[3,128,1024]{2,1,0:T(8,128)(2,1)S(1)}, u32[]{:S(2)}, u32[]{:S(2)}) collective-permute-start(bf16[3,128,1024]{2,1,0:T(8,128)(2,1)} %collective-permute-done.1.refs_9_), channel_id=1, source_target_pairs={{0,7},{1,0},{2,1},{3,2},{4,3},{5,4},{6,5},{7,6},{8,15},{9,8},{10,9... | collective-permute-start | bytes 2359304 | tf_op jit(solution)/shard_map/ppermute | solution.py:377
  45.8 17.7 %collective-permute-start.5 = (bf16[3,128,1024]{2,1,0:T(8,128)(2,1)}, bf16[3,128,1024]{2,1,0:T(8,128)(2,1)S(1)}, u32[]{:S(2)}, u32[]{:S(2)}) collective-permute-start(bf16[3,128,1024]{2,1,0:T(8,128)(2,1)} %collective-permute-done.4.refs_12_), channel_id=1, source_target_pairs={{0,1},{1,2},{2,3},{3,4},{4,5},{5,6},{6,7},{7,0},{8,9},{9,10},{10,1... | collective-permute-start | bytes 2359304 | tf_op jit(solution)/shard_map/ppermute | solution.py:376
  63.5 16.6 %collective-permute-start.9 = (bf16[3,1024,128]{2,1,0:T(8,128)(2,1)S(1)}, bf16[3,1024,128]{2,1,0:T(8,128)(2,1)S(1)}, u32[]{:S(2)}, u32[]{:S(2)}) collective-permute-start(bf16[3,1024,128]{2,1,0:T(8,128)(2,1)S(1)} %get-tuple-element.18.refs_0_), channel_id=1, source_target_pairs={{0,1},{1,2},{2,3},{3,4},{4,5},{5,6},{6,7},{7,0},{8,9},{9,10},{10,1... | collective-permute-start | bytes 2359304 | tf_op jit(solution)/shard_map/ppermute | solution.py:376
  63.5 16.6 %collective-permute-start.6 = (bf16[3,1024,128]{2,1,0:T(8,128)(2,1)S(1)}, bf16[3,1024,128]{2,1,0:T(8,128)(2,1)S(1)}, u32[]{:S(2)}, u32[]{:S(2)}) collective-permute-start(bf16[3,1024,128]{2,1,0:T(8,128)(2,1)S(1)} %get-tuple-element.18.refs_0_), channel_id=1, source_target_pairs={{0,7},{1,0},{2,1},{3,2},{4,3},{5,4},{6,5},{7,6},{8,15},{9,8},{10,9... | collective-permute-start | bytes 2359304 | tf_op jit(solution)/shard_map/ppermute | solution.py:377
  80.0 16.0 %collective-permute-start.10 = (bf16[3,1024,128]{2,1,0:T(8,128)(2,1)S(1)}, bf16[3,1024,128]{2,1,0:T(8,128)(2,1)S(1)}, u32[]{:S(2)}, u32[]{:S(2)}) collective-permute-start(bf16[3,1024,128]{2,1,0:T(8,128)(2,1)S(1)} %collective-permute-done.9.refs_6_.refs_8_), channel_id=1, source_target_pairs={{0,1},{1,2},{2,3},{3,4},{4,5},{5,6},{6,7},{7,0},{8,9},{9,10},{10,1... | collective-permute-start | bytes 2359304 | tf_op jit(solution)/shard_map/ppermute | solution.py:376
  80.1 16.0 %collective-permute-start.7 = (bf16[3,1024,128]{2,1,0:T(8,128)(2,1)S(1)}, bf16[3,1024,128]{2,1,0:T(8,128)(2,1)S(1)}, u32[]{:S(2)}, u32[]{:S(2)}) collective-permute-start(bf16[3,1024,128]{2,1,0:T(8,128)(2,1)S(1)} %collective-permute-done.6.refs_1_), channel_id=1, source_target_pairs={{0,7},{1,0},{2,1},{3,2},{4,3},{5,4},{6,5},{7,6},{8,15},{9,8},{10,9... | collective-permute-start | bytes 2359304 | tf_op jit(solution)/shard_map/ppermute | solution.py:377
  96.0 16.0 %collective-permute-start.11 = (bf16[3,1024,128]{2,1,0:T(8,128)(2,1)S(1)}, bf16[3,1024,128]{2,1,0:T(8,128)(2,1)S(1)}, u32[]{:S(2)}, u32[]{:S(2)}) collective-permute-start(bf16[3,1024,128]{2,1,0:T(8,128)(2,1)S(1)} %collective-permute-done.10.refs_5_.refs_7_), channel_id=1, source_target_pairs={{0,1},{1,2},{2,3},{3,4},{4,5},{5,6},{6,7},{7,0},{8,9},{9,10},{10,1... | collective-permute-start | bytes 2359304 | tf_op jit(solution)/shard_map/ppermute | solution.py:376
  96.1 16.8 %collective-permute-start.8 = (bf16[3,1024,128]{2,1,0:T(8,128)(2,1)S(1)}, bf16[3,1024,128]{2,1,0:T(8,128)(2,1)S(1)}, u32[]{:S(2)}, u32[]{:S(2)}) collective-permute-start(bf16[3,1024,128]{2,1,0:T(8,128)(2,1)S(1)} %collective-permute-done.7.refs_2_), channel_id=1, source_target_pairs={{0,7},{1,0},{2,1},{3,2},{4,3},{5,4},{6,5},{7,6},{8,15},{9,8},{10,9... | collective-permute-start | bytes 2359304 | tf_op jit(solution)/shard_map/ppermute | solution.py:377
  98.8 24.7 %collective-permute-start.14 = (bf16[3,64,1024]{2,1,0:T(8,128)(2,1)S(1)}, bf16[3,64,1024]{2,1,0:T(8,128)(2,1)}, u32[]{:S(2)}, u32[]{:S(2)}) collective-permute-start(bf16[3,64,1024]{2,1,0:T(8,128)(2,1)S(1)} %slice.18), channel_id=1, source_target_pairs={{0,1},{1,2},{2,3},{3,4},{4,5},{5,6},{6,7},{7,0},{8,9},{9,10},{10,1... | collective-permute-start | bytes 1179656 | tf_op jit(solution)/shard_map/ppermute | solution.py:381
  99.6 23.8 %collective-permute-start.15 = (bf16[3,64,1024]{2,1,0:T(8,128)(2,1)}, bf16[3,64,1024]{2,1,0:T(8,128)(2,1)}, u32[]{:S(2)}, u32[]{:S(2)}) collective-permute-start(bf16[3,64,1024]{2,1,0:T(8,128)(2,1)} %slice.19), channel_id=1, source_target_pairs={{0,7},{1,0},{2,1},{3,2},{4,3},{5,4},{6,5},{7,6},{8,15},{9,8},{10,9... | collective-permute-start | bytes 1179656 | tf_op jit(solution)/shard_map/ppermute | solution.py:382
  112.8 16.1 %collective-permute-start.12 = (bf16[3,512,128]{2,1,0:T(8,128)(2,1)}, bf16[3,512,128]{2,1,0:T(8,128)(2,1)}, u32[]{:S(2)}, u32[]{:S(2)}) collective-permute-start(bf16[3,512,128]{2,1,0:T(8,128)(2,1)} %slice.16), channel_id=1, source_target_pairs={{0,1},{1,2},{2,3},{3,4},{4,5},{5,6},{6,7},{7,0},{8,9},{9,10},{10,1... | collective-permute-start | bytes 1179656 | tf_op jit(solution)/shard_map/ppermute | solution.py:381
  113.7 15.3 %collective-permute-start.13 = (bf16[3,512,128]{2,1,0:T(8,128)(2,1)}, bf16[3,512,128]{2,1,0:T(8,128)(2,1)}, u32[]{:S(2)}, u32[]{:S(2)}) collective-permute-start(bf16[3,512,128]{2,1,0:T(8,128)(2,1)} %slice.17), channel_id=1, source_target_pairs={{0,7},{1,0},{2,1},{3,2},{4,3},{5,4},{6,5},{7,6},{8,15},{9,8},{10,9... | collective-permute-start | bytes 1179656 | tf_op jit(solution)/shard_map/ppermute | solution.py:382
  133.7 10.2 %collective-permute-start.16 = (bf16[400,128]{1,0:T(8,128)(2,1)S(1)}, bf16[400,128]{1,0:T(8,128)(2,1)S(1)}, u32[]{:S(2)}, u32[]{:S(2)}) collective-permute-start(bf16[400,128]{1,0:T(8,128)(2,1)S(1)} %get-tuple-element.20), channel_id=1, source_target_pairs={{0,1},{1,2},{2,3},{3,4},{4,5},{5,6},{6,7},{7,0},{8,9},{9,10},{10,1... | collective-permute-start | bytes 307208 | tf_op jit(solution)/shard_map/ppermute | solution.py:402
  133.7 10.3 %collective-permute-start.17 = (bf16[400,128]{1,0:T(8,128)(2,1)S(1)}, bf16[400,128]{1,0:T(8,128)(2,1)S(1)}, u32[]{:S(2)}, u32[]{:S(2)}) collective-permute-start(bf16[400,128]{1,0:T(8,128)(2,1)S(1)} %get-tuple-element.21), channel_id=1, source_target_pairs={{0,2},{1,3},{2,4},{3,5},{4,6},{5,7},{6,0},{7,1},{8,10},{9,11},{10,... | collective-permute-start | bytes 307208 | tf_op jit(solution)/shard_map/ppermute | solution.py:402
  136.2 11.7 %collective-permute-start.18 = (bf16[400,128]{1,0:T(8,128)(2,1)S(1)}, bf16[400,128]{1,0:T(8,128)(2,1)S(1)}, u32[]{:S(2)}, u32[]{:S(2)}) collective-permute-start(bf16[400,128]{1,0:T(8,128)(2,1)S(1)} %get-tuple-element.22), channel_id=1, source_target_pairs={{0,3},{1,4},{2,5},{3,6},{4,7},{5,0},{6,1},{7,2},{8,11},{9,12},{10,... | collective-permute-start | bytes 307208 | tf_op jit(solution)/shard_map/ppermute | solution.py:402
  137.3 11.6 %collective-permute-start.19 = (bf16[400,128]{1,0:T(8,128)(2,1)S(1)}, bf16[400,128]{1,0:T(8,128)(2,1)S(1)}, u32[]{:S(2)}, u32[]{:S(2)}) collective-permute-start(bf16[400,128]{1,0:T(8,128)(2,1)S(1)} %get-tuple-element.23), channel_id=1, source_target_pairs={{0,4},{1,5},{2,6},{3,7},{4,0},{5,1},{6,2},{7,3},{8,12},{9,13},{10,... | collective-permute-start | bytes 307208 | tf_op jit(solution)/shard_map/ppermute | solution.py:402
  139.4 10.1 %collective-permute-start.20 = (bf16[400,128]{1,0:T(8,128)(2,1)S(1)}, bf16[400,128]{1,0:T(8,128)(2,1)S(1)}, u32[]{:S(2)}, u32[]{:S(2)}) collective-permute-start(bf16[400,128]{1,0:T(8,128)(2,1)S(1)} %get-tuple-element.24), channel_id=1, source_target_pairs={{0,5},{1,6},{2,7},{3,0},{4,1},{5,2},{6,3},{7,4},{8,13},{9,14},{10,... | collective-permute-start | bytes 307208 | tf_op jit(solution)/shard_map/ppermute | solution.py:402
  144.0 11.5 %collective-permute-start.22 = (bf16[400,128]{1,0:T(8,128)(2,1)S(1)}, bf16[400,128]{1,0:T(8,128)(2,1)S(1)}, u32[]{:S(2)}, u32[]{:S(2)}) collective-permute-start(bf16[400,128]{1,0:T(8,128)(2,1)S(1)} %get-tuple-element.26), channel_id=1, source_target_pairs={{0,7},{1,0},{2,1},{3,2},{4,3},{5,4},{6,5},{7,6},{8,15},{9,8},{10,9... | collective-permute-start | bytes 307208 | tf_op jit(solution)/shard_map/ppermute | solution.py:402
  156.7 28.5 %all-to-all-start.1 = ((bf16[32,112,128]{2,1,0:T(8,128)(2,1)}), bf16[32,112,128]{2,1,0:T(8,128)(2,1)S(1)}, u32[]{:S(2)}, u32[]{:S(2)}) async-start(bf16[32,112,128]{2,1,0:T(8,128)(2,1)} %scale.1), calls=%async_computation.1 | async-start | bytes 1835008 | tf_op jit(solution)/shard_map/all_to_all | solution.py:404
  (14 other events, 329.7 us)

commit v4 on v3

--- a/solution.py
+++ b/solution.py
@@ -179,7 +179,7 @@
         grid=(count,),
         in_specs=[slot_of(left_root.shape)] + [slot_of(panel.shape) for panel in early],
         out_specs=slot_of(left_root.shape),
-        compiler_params=params(62),
+        compiler_params=params(56),
         cost_estimate=cost(count * 4 * rows * order * order, count * 5 * order * order),
         name="bulk",
     )(left_root, *early)
@@ -398,7 +398,7 @@
     part = bulk(left_root, grads, roots)
     sents = precondition(place, left_root, adam, part, grads, roots)
     gots = list(sents)
-    for k in (4, 3, 5, 2, 6, 1, 7):
+    for k in (3, 5, 4, 2, 6, 1, 7):
         gots[k] = lax.ppermute(sents[k], "mp", [(i, (i + k) % 8) for i in range(8)])
     sent = scale_up(owners, count, place, gots)
     got = lax.all_to_all(sent, "dp", split_axis=0, concat_axis=0, tiled=True)

time: 188 us -> 186 us (0.989)
  no operation moved by 1% of the time
where the time goes in v4:
time: 186 us
  waiting for transfers between devices  96.5 us (52%)
  starting transfers between devices  60.5 us (33%)
  Pallas kernels  24.1 us (13%)
  local copies, waits for them, and re-layouts  4.19 us (2%)
    ppermute x6, waiting for transfers between devices, ring(): from_below.append(lax.ppermute(from_below[-1], 'mp', up))  40 us
    all_to_all x2, starting transfers between devices, shards(): got = lax.all_to_all(sent, 'dp', split_axis=0, concat_axis=0, tiled=True)  22 us
    ppermute x6, waiting for transfers between devices, ring(): from_above.append(lax.ppermute(from_above[-1], 'mp', down))  21.7 us
    ppermute x6, starting transfers between devices, ring(): from_above.append(lax.ppermute(from_above[-1], 'mp', down))  21.3 us
    all_to_all x2, waiting for transfers between devices, shards(): got = lax.all_to_all(sent, 'dp', split_axis=0, concat_axis=0, tiled=True)  19.4 us
    ppermute x7, starting transfers between devices, shards(): gots[k] = lax.ppermute(sents[k], 'mp', [(i, (i + k) % 8) for i in range(8)])  11.7 us
    ppermute x7, waiting for transfers between devices, shards(): gots[k] = lax.ppermute(sents[k], 'mp', [(i, (i + k) % 8) for i in range(8)])  10 us
    pallas_call x1, Pallas kernels, factors(): pl.pallas_call(factors_kernel, out_shape=[jax.ShapeDtypeStruct(left_stat....  7.22 us
  transfers between devices with their start and end apart: 25, of which 15 were waited for; matrix products, arithmetic and copies ran while one was open for 1% of the time, Pallas kernels for 10%

profile of v4, /device:TPU:1, one launch (start us, length us, event | category | flops | bytes accessed | tf_op | source)
XLA Modules:
  0.0 186.0 jit_solution(8598905196219253648)
XLA Ops:
  0.6 6.5 %collective-permute-start = (bf16[3,128,1024]{2,1,0:T(8,128)(2,1)}, bf16[3,128,1024]{2,1,0:T(8,128)(2,1)S(1)}, u32[]{:S(2)}, u32[]{:S(2)}) collective-permute-start(bf16[3,128,1024]{2,1,0:T(8,128)(2,1)} %refs_7_.1), channel_id=1, source_target_pairs={{0,7},{1,0},{2,1},{3,2},{4,3},{5,4},{6,5},{7,6},{8,15},{9,8},{10,9... | collective-permute-start | bytes 2359304 | tf_op jit(solution)/shard_map/ppermute | solution.py:377
  7.1 16.5 %collective-permute-done.refs_8_ = bf16[3,128,1024]{2,1,0:T(8,128)(2,1)S(1)} collective-permute-done((bf16[3,128,1024]{2,1,0:T(8,128)(2,1)}, bf16[3,128,1024]{2,1,0:T(8,128)(2,1)S(1)}, u32[]{:S(2)}, u32[]{:S(2)}) %collective-permute-start) | collective-permute-done | bytes 786464 | tf_op jit(solution)/shard_map/ppermute | solution.py:377
  23.6 3.3 %collective-permute-start.1 = (bf16[3,128,1024]{2,1,0:T(8,128)(2,1)S(1)}, bf16[3,128,1024]{2,1,0:T(8,128)(2,1)}, u32[]{:S(2)}, u32[]{:S(2)}) collective-permute-start(bf16[3,128,1024]{2,1,0:T(8,128)(2,1)S(1)} %collective-permute-done.refs_8_), channel_id=1, source_target_pairs={{0,7},{1,0},{2,1},{3,2},{4,3},{5,4},{6,5},{7,6},{8,15},{9,8},{10,9... | collective-permute-start | bytes 2359304 | tf_op jit(solution)/shard_map/ppermute | solution.py:377
  27.0 5.0 %prepare.1 = bf16[32,112,128]{2,1,0:T(8,128)(2,1)} custom-call(s32[96]{0:T(128)} %slot_ref.3, bf16[96,32,128]{2,1,0:T(8,128)(2,1)} %grad_ref.1, f32[96,32,128]{2,1,0:T(8,128)} %one_ref.1, f32[96,32,128]{2,1,0:T(8,128)} %two_ref.1), custom_call_target="tpu_custom_call" | custom-call | flops 7864320 | bytes 4718592 | tf_op jit(solution)/shard_map/prepare/pallas_call | solution.py:81
  31.9 8.9 %all-to-all-start = ((bf16[32,112,128]{2,1,0:T(8,128)(2,1)}), bf16[32,112,128]{2,1,0:T(8,128)(2,1)S(1)}, u32[]{:S(2)}, u32[]{:S(2)}) async-start(bf16[32,112,128]{2,1,0:T(8,128)(2,1)} %prepare.1), calls=%async_computation | async-start | bytes 1835008 | tf_op jit(solution)/shard_map/all_to_all | solution.py:394
  42.2 3.5 %collective-permute-start.2 = (bf16[3,128,1024]{2,1,0:T(8,128)(2,1)}, bf16[3,128,1024]{2,1,0:T(8,128)(2,1)S(1)}, u32[]{:S(2)}, u32[]{:S(2)}) collective-permute-start(bf16[3,128,1024]{2,1,0:T(8,128)(2,1)} %collective-permute-done.1.refs_9_), channel_id=1, source_target_pairs={{0,7},{1,0},{2,1},{3,2},{4,3},{5,4},{6,5},{7,6},{8,15},{9,8},{10,9... | collective-permute-start | bytes 2359304 | tf_op jit(solution)/shard_map/ppermute | solution.py:377
  45.8 10.8 %all-to-all-done.got_ref = bf16[32,112,128]{2,1,0:T(8,128)(2,1)S(1)} async-done(((bf16[32,112,128]{2,1,0:T(8,128)(2,1)}), bf16[32,112,128]{2,1,0:T(8,128)(2,1)S(1)}, u32[]{:S(2)}, u32[]{:S(2)}) %all-to-all-start) | async-done | bytes 917536 | tf_op jit(solution)/shard_map/all_to_all | solution.py:394
  56.7 3.7 %collective-permute-done.2.refs_10_ = bf16[3,128,1024]{2,1,0:T(8,128)(2,1)S(1)} collective-permute-done((bf16[3,128,1024]{2,1,0:T(8,128)(2,1)}, bf16[3,128,1024]{2,1,0:T(8,128)(2,1)S(1)}, u32[]{:S(2)}, u32[]{:S(2)}) %collective-permute-start.2) | collective-permute-done | bytes 786464 | tf_op jit(solution)/shard_map/ppermute | solution.py:377
  60.4 3.0 %collective-permute-done.5.refs_11_ = bf16[3,128,1024]{2,1,0:T(8,128)(2,1)S(1)} collective-permute-done((bf16[3,128,1024]{2,1,0:T(8,128)(2,1)}, bf16[3,128,1024]{2,1,0:T(8,128)(2,1)S(1)}, u32[]{:S(2)}, u32[]{:S(2)}) %collective-permute-start.5) | collective-permute-done | bytes 786464 | tf_op jit(solution)/shard_map/ppermute | solution.py:376
  63.5 2.7 %collective-permute-start.6 = (bf16[3,1024,128]{2,1,0:T(8,128)(2,1)S(1)}, bf16[3,1024,128]{2,1,0:T(8,128)(2,1)S(1)}, u32[]{:S(2)}, u32[]{:S(2)}) collective-permute-start(bf16[3,1024,128]{2,1,0:T(8,128)(2,1)S(1)} %get-tuple-element.18.refs_0_), channel_id=1, source_target_pairs={{0,7},{1,0},{2,1},{3,2},{4,3},{5,4},{6,5},{7,6},{8,15},{9,8},{10,9... | collective-permute-start | bytes 2359304 | tf_op jit(solution)/shard_map/ppermute | solution.py:377
  66.1 13.9 %collective-permute-done.9.refs_6_.refs_8_ = bf16[3,1024,128]{2,1,0:T(8,128)(2,1)S(1)} collective-permute-done((bf16[3,1024,128]{2,1,0:T(8,128)(2,1)S(1)}, bf16[3,1024,128]{2,1,0:T(8,128)(2,1)S(1)}, u32[]{:S(2)}, u32[]{:S(2)}) %collective-permute-start.9) | collective-permute-done | bytes 786464 | tf_op jit(solution)/shard_map/ppermute | solution.py:376
  80.1 2.7 %collective-permute-start.7 = (bf16[3,1024,128]{2,1,0:T(8,128)(2,1)S(1)}, bf16[3,1024,128]{2,1,0:T(8,128)(2,1)S(1)}, u32[]{:S(2)}, u32[]{:S(2)}) collective-permute-start(bf16[3,1024,128]{2,1,0:T(8,128)(2,1)S(1)} %collective-permute-done.6.refs_1_), channel_id=1, source_target_pairs={{0,7},{1,0},{2,1},{3,2},{4,3},{5,4},{6,5},{7,6},{8,15},{9,8},{10,9... | collective-permute-start | bytes 2359304 | tf_op jit(solution)/shard_map/ppermute | solution.py:377
  82.7 13.3 %collective-permute-done.10.refs_5_.refs_7_ = bf16[3,1024,128]{2,1,0:T(8,128)(2,1)S(1)} collective-permute-done((bf16[3,1024,128]{2,1,0:T(8,128)(2,1)S(1)}, bf16[3,1024,128]{2,1,0:T(8,128)(2,1)S(1)}, u32[]{:S(2)}, u32[]{:S(2)}) %collective-permute-start.10) | collective-permute-done | bytes 786464 | tf_op jit(solution)/shard_map/ppermute | solution.py:376
  96.1 2.7 %collective-permute-start.8 = (bf16[3,1024,128]{2,1,0:T(8,128)(2,1)S(1)}, bf16[3,1024,128]{2,1,0:T(8,128)(2,1)S(1)}, u32[]{:S(2)}, u32[]{:S(2)}) collective-permute-start(bf16[3,1024,128]{2,1,0:T(8,128)(2,1)S(1)} %collective-permute-done.7.refs_2_), channel_id=1, source_target_pairs={{0,7},{1,0},{2,1},{3,2},{4,3},{5,4},{6,5},{7,6},{8,15},{9,8},{10,9... | collective-permute-start | bytes 2359304 | tf_op jit(solution)/shard_map/ppermute | solution.py:377
  99.6 2.7 %collective-permute-start.15 = (bf16[3,64,1024]{2,1,0:T(8,128)(2,1)}, bf16[3,64,1024]{2,1,0:T(8,128)(2,1)S(1)}, u32[]{:S(2)}, u32[]{:S(2)}) collective-permute-start(bf16[3,64,1024]{2,1,0:T(8,128)(2,1)} %slice.19), channel_id=1, source_target_pairs={{0,7},{1,0},{2,1},{3,2},{4,3},{5,4},{6,5},{7,6},{8,15},{9,8},{10,9... | collective-permute-start | bytes 1179656 | tf_op jit(solution)/shard_map/ppermute | solution.py:382
  102.3 9.7 %collective-permute-done.11.refs_4_.refs_6_ = bf16[3,1024,128]{2,1,0:T(8,128)(2,1)S(1)} collective-permute-done((bf16[3,1024,128]{2,1,0:T(8,128)(2,1)S(1)}, bf16[3,1024,128]{2,1,0:T(8,128)(2,1)S(1)}, u32[]{:S(2)}, u32[]{:S(2)}) %collective-permute-start.11) | collective-permute-done | bytes 786464 | tf_op jit(solution)/shard_map/ppermute | solution.py:376
  113.7 2.7 %collective-permute-start.13 = (bf16[3,512,128]{2,1,0:T(8,128)(2,1)}, bf16[3,512,128]{2,1,0:T(8,128)(2,1)S(1)}, u32[]{:S(2)}, u32[]{:S(2)}) collective-permute-start(bf16[3,512,128]{2,1,0:T(8,128)(2,1)} %slice.17), channel_id=1, source_target_pairs={{0,7},{1,0},{2,1},{3,2},{4,3},{5,4},{6,5},{7,6},{8,15},{9,8},{10,9... | collective-permute-start | bytes 1179656 | tf_op jit(solution)/shard_map/ppermute | solution.py:382
  116.4 7.0 %bulk.1.part_ref = f32[3,128,1024]{2,1,0:T(8,128)} custom-call(bf16[3,128,1024]{2,1,0:T(8,128)(2,1)} %left_ref.4, bf16[3,1024,128]{2,1,0:T(8,128)(2,1)} %copy-done.1, bf16[3,1024,128]{2,1,0:T(8,128)(2,1)} %copy-done.9, bf16[3,1024,128]{2,1,0:T(8,128)(2,1)} %copy-done.11, bf16[3,1024,128]{2,1,0:T(8,128)(2,1)} %copy-done.7, bf16[3,1024,128]{2,1,0:T(8,128)(2,1)} %copy-done.6, ...), custom_call_target="tpu_custom_call" | custom-call | flops 1610612736 | bytes 15728640 | tf_op jit(solution)/shard_map/bulk/pallas_call | solution.py:176
  123.4 5.5 %collective-permute-done.12.refs_0_.refs_4_ = bf16[3,512,128]{2,1,0:T(8,128)(2,1)S(1)} collective-permute-done((bf16[3,512,128]{2,1,0:T(8,128)(2,1)}, bf16[3,512,128]{2,1,0:T(8,128)(2,1)S(1)}, u32[]{:S(2)}, u32[]{:S(2)}) %collective-permute-start.12) | collective-permute-done | bytes 393248 | tf_op jit(solution)/shard_map/ppermute | solution.py:381
  137.9 4.3 %collective-permute-start.20 = (bf16[400,128]{1,0:T(8,128)(2,1)S(1)}, bf16[400,128]{1,0:T(8,128)(2,1)S(1)}, u32[]{:S(2)}, u32[]{:S(2)}) collective-permute-start(bf16[400,128]{1,0:T(8,128)(2,1)S(1)} %get-tuple-element.24), channel_id=1, source_target_pairs={{0,5},{1,6},{2,7},{3,0},{4,1},{5,2},{6,3},{7,4},{8,13},{9,14},{10,... | collective-permute-start | bytes 307208 | tf_op jit(solution)/shard_map/ppermute | solution.py:402
  149.7 4.2 %collective-permute-done.22.refs_7_ = bf16[400,128]{1,0:T(8,128)(2,1)S(1)} collective-permute-done((bf16[400,128]{1,0:T(8,128)(2,1)S(1)}, bf16[400,128]{1,0:T(8,128)(2,1)S(1)}, u32[]{:S(2)}, u32[]{:S(2)}) %collective-permute-start.22) | collective-permute-done | bytes 102432 | tf_op jit(solution)/shard_map/ppermute | solution.py:402
  155.1 13.1 %all-to-all-start.1 = ((bf16[32,112,128]{2,1,0:T(8,128)(2,1)}), bf16[32,112,128]{2,1,0:T(8,128)(2,1)S(1)}, u32[]{:S(2)}, u32[]{:S(2)}) async-start(bf16[32,112,128]{2,1,0:T(8,128)(2,1)} %scale.1), calls=%async_computation.1 | async-start | bytes 1835008 | tf_op jit(solution)/shard_map/all_to_all | solution.py:404
  168.2 7.2 %factors.1 = (f32[3,128,1024]{2,1,0:T(8,128)}, f32[3,128,1024]{2,1,0:T(8,128)}) custom-call(s32[1]{0:T(128)} %bitcast.place_ref, f32[3,128,1024]{2,1,0:T(8,128)} %left_ref.5, f32[3,128,1024]{2,1,0:T(8,128)} %right_ref.1, bf16[3,1024,128]{2,1,0:T(8,128)(2,1)} %copy-done.1, bf16[3,1024,128]{2,1,0:T(8,128)(2,1)} %copy-done.9, bf16[3,1024,128]{2,1,0:T(8,128)(2,1)} %copy-done.11, ...), custom_call_target="tpu_custom_call" | custom-call | flops 1610612736 | bytes 12582912 | tf_op jit(solution)/shard_map/factors/pallas_call | solution.py:358
  175.4 8.5 %all-to-all-done.1.got_ref = bf16[32,112,128]{2,1,0:T(8,128)(2,1)S(1)} async-done(((bf16[32,112,128]{2,1,0:T(8,128)(2,1)}), bf16[32,112,128]{2,1,0:T(8,128)(2,1)S(1)}, u32[]{:S(2)}, u32[]{:S(2)}) %all-to-all-start.1) | async-done | bytes 917536 | tf_op jit(solution)/shard_map/all_to_all | solution.py:404
  (67 shorter events, 23.8 us)
Async XLA Ops:
  0.6 23.0 %collective-permute-start = (bf16[3,128,1024]{2,1,0:T(8,128)(2,1)}, bf16[3,128,1024]{2,1,0:T(8,128)(2,1)S(1)}, u32[]{:S(2)}, u32[]{:S(2)}) collective-permute-start(bf16[3,128,1024]{2,1,0:T(8,128)(2,1)} %refs_7_.1), channel_id=1, source_target_pairs={{0,7},{1,0},{2,1},{3,2},{4,3},{5,4},{6,5},{7,6},{8,15},{9,8},{10,9... | collective-permute-start | bytes 2359304 | tf_op jit(solution)/shard_map/ppermute | solution.py:377
  7.1 19.8 %collective-permute-start.3 = (bf16[3,128,1024]{2,1,0:T(8,128)(2,1)}, bf16[3,128,1024]{2,1,0:T(8,128)(2,1)}, u32[]{:S(2)}, u32[]{:S(2)}) collective-permute-start(bf16[3,128,1024]{2,1,0:T(8,128)(2,1)} %refs_7_.1), channel_id=1, source_target_pairs={{0,1},{1,2},{2,3},{3,4},{4,5},{5,6},{6,7},{7,0},{8,9},{9,10},{10,1... | collective-permute-start | bytes 2359304 | tf_op jit(solution)/shard_map/ppermute | solution.py:376
  23.6 18.6 %collective-permute-start.1 = (bf16[3,128,1024]{2,1,0:T(8,128)(2,1)S(1)}, bf16[3,128,1024]{2,1,0:T(8,128)(2,1)}, u32[]{:S(2)}, u32[]{:S(2)}) collective-permute-start(bf16[3,128,1024]{2,1,0:T(8,128)(2,1)S(1)} %collective-permute-done.refs_8_), channel_id=1, source_target_pairs={{0,7},{1,0},{2,1},{3,2},{4,3},{5,4},{6,5},{7,6},{8,15},{9,8},{10,9... | collective-permute-start | bytes 2359304 | tf_op jit(solution)/shard_map/ppermute | solution.py:377
  26.9 18.8 %collective-permute-start.4 = (bf16[3,128,1024]{2,1,0:T(8,128)(2,1)}, bf16[3,128,1024]{2,1,0:T(8,128)(2,1)}, u32[]{:S(2)}, u32[]{:S(2)}) collective-permute-start(bf16[3,128,1024]{2,1,0:T(8,128)(2,1)} %collective-permute-done.3.refs_13_), channel_id=1, source_target_pairs={{0,1},{1,2},{2,3},{3,4},{4,5},{5,6},{6,7},{7,0},{8,9},{9,10},{10,1... | collective-permute-start | bytes 2359304 | tf_op jit(solution)/shard_map/ppermute | solution.py:376
  31.9 24.7 %all-to-all-start = ((bf16[32,112,128]{2,1,0:T(8,128)(2,1)}), bf16[32,112,128]{2,1,0:T(8,128)(2,1)S(1)}, u32[]{:S(2)}, u32[]{:S(2)}) async-start(bf16[32,112,128]{2,1,0:T(8,128)(2,1)} %prepare.1), calls=%async_computation | async-start | bytes 1835008 | tf_op jit(solution)/shard_map/all_to_all | solution.py:394
  42.2 18.2 %collective-permute-start.2 = (bf16[3,128,1024]{2,1,0:T(8,128)(2,1)}, bf16[3,128,1024]{2,1,0:T(8,128)(2,1)S(1)}, u32[]{:S(2)}, u32[]{:S(2)}) collective-permute-start(bf16[3,128,1024]{2,1,0:T(8,128)(2,1)} %collective-permute-done.1.refs_9_), channel_id=1, source_target_pairs={{0,7},{1,0},{2,1},{3,2},{4,3},{5,4},{6,5},{7,6},{8,15},{9,8},{10,9... | collective-permute-start | bytes 2359304 | tf_op jit(solution)/shard_map/ppermute | solution.py:377
  45.8 17.7 %collective-permute-start.5 = (bf16[3,128,1024]{2,1,0:T(8,128)(2,1)}, bf16[3,128,1024]{2,1,0:T(8,128)(2,1)S(1)}, u32[]{:S(2)}, u32[]{:S(2)}) collective-permute-start(bf16[3,128,1024]{2,1,0:T(8,128)(2,1)} %collective-permute-done.4.refs_12_), channel_id=1, source_target_pairs={{0,1},{1,2},{2,3},{3,4},{4,5},{5,6},{6,7},{7,0},{8,9},{9,10},{10,1... | collective-permute-start | bytes 2359304 | tf_op jit(solution)/shard_map/ppermute | solution.py:376
  63.5 16.6 %collective-permute-start.9 = (bf16[3,1024,128]{2,1,0:T(8,128)(2,1)S(1)}, bf16[3,1024,128]{2,1,0:T(8,128)(2,1)S(1)}, u32[]{:S(2)}, u32[]{:S(2)}) collective-permute-start(bf16[3,1024,128]{2,1,0:T(8,128)(2,1)S(1)} %get-tuple-element.18.refs_0_), channel_id=1, source_target_pairs={{0,1},{1,2},{2,3},{3,4},{4,5},{5,6},{6,7},{7,0},{8,9},{9,10},{10,1... | collective-permute-start | bytes 2359304 | tf_op jit(solution)/shard_map/ppermute | solution.py:376
  63.5 16.6 %collective-permute-start.6 = (bf16[3,1024,128]{2,1,0:T(8,128)(2,1)S(1)}, bf16[3,1024,128]{2,1,0:T(8,128)(2,1)S(1)}, u32[]{:S(2)}, u32[]{:S(2)}) collective-permute-start(bf16[3,1024,128]{2,1,0:T(8,128)(2,1)S(1)} %get-tuple-element.18.refs_0_), channel_id=1, source_target_pairs={{0,7},{1,0},{2,1},{3,2},{4,3},{5,4},{6,5},{7,6},{8,15},{9,8},{10,9... | collective-permute-start | bytes 2359304 | tf_op jit(solution)/shard_map/ppermute | solution.py:377
  80.0 16.0 %collective-permute-start.10 = (bf16[3,1024,128]{2,1,0:T(8,128)(2,1)S(1)}, bf16[3,1024,128]{2,1,0:T(8,128)(2,1)S(1)}, u32[]{:S(2)}, u32[]{:S(2)}) collective-permute-start(bf16[3,1024,128]{2,1,0:T(8,128)(2,1)S(1)} %collective-permute-done.9.refs_6_.refs_8_), channel_id=1, source_target_pairs={{0,1},{1,2},{2,3},{3,4},{4,5},{5,6},{6,7},{7,0},{8,9},{9,10},{10,1... | collective-permute-start | bytes 2359304 | tf_op jit(solution)/shard_map/ppermute | solution.py:376
  80.1 16.0 %collective-permute-start.7 = (bf16[3,1024,128]{2,1,0:T(8,128)(2,1)S(1)}, bf16[3,1024,128]{2,1,0:T(8,128)(2,1)S(1)}, u32[]{:S(2)}, u32[]{:S(2)}) collective-permute-start(bf16[3,1024,128]{2,1,0:T(8,128)(2,1)S(1)} %collective-permute-done.6.refs_1_), channel_id=1, source_target_pairs={{0,7},{1,0},{2,1},{3,2},{4,3},{5,4},{6,5},{7,6},{8,15},{9,8},{10,9... | collective-permute-start | bytes 2359304 | tf_op jit(solution)/shard_map/ppermute | solution.py:377
  96.0 16.0 %collective-permute-start.11 = (bf16[3,1024,128]{2,1,0:T(8,128)(2,1)S(1)}, bf16[3,1024,128]{2,1,0:T(8,128)(2,1)S(1)}, u32[]{:S(2)}, u32[]{:S(2)}) collective-permute-start(bf16[3,1024,128]{2,1,0:T(8,128)(2,1)S(1)} %collective-permute-done.10.refs_5_.refs_7_), channel_id=1, source_target_pairs={{0,1},{1,2},{2,3},{3,4},{4,5},{5,6},{6,7},{7,0},{8,9},{9,10},{10,1... | collective-permute-start | bytes 2359304 | tf_op jit(solution)/shard_map/ppermute | solution.py:376
  96.1 16.8 %collective-permute-start.8 = (bf16[3,1024,128]{2,1,0:T(8,128)(2,1)S(1)}, bf16[3,1024,128]{2,1,0:T(8,128)(2,1)S(1)}, u32[]{:S(2)}, u32[]{:S(2)}) collective-permute-start(bf16[3,1024,128]{2,1,0:T(8,128)(2,1)S(1)} %collective-permute-done.7.refs_2_), channel_id=1, source_target_pairs={{0,7},{1,0},{2,1},{3,2},{4,3},{5,4},{6,5},{7,6},{8,15},{9,8},{10,9... | collective-permute-start | bytes 2359304 | tf_op jit(solution)/shard_map/ppermute | solution.py:377
  98.8 24.6 %collective-permute-start.14 = (bf16[3,64,1024]{2,1,0:T(8,128)(2,1)S(1)}, bf16[3,64,1024]{2,1,0:T(8,128)(2,1)S(1)}, u32[]{:S(2)}, u32[]{:S(2)}) collective-permute-start(bf16[3,64,1024]{2,1,0:T(8,128)(2,1)S(1)} %slice.18), channel_id=1, source_target_pairs={{0,1},{1,2},{2,3},{3,4},{4,5},{5,6},{6,7},{7,0},{8,9},{9,10},{10,1... | collective-permute-start | bytes 1179656 | tf_op jit(solution)/shard_map/ppermute | solution.py:381
  99.6 23.8 %collective-permute-start.15 = (bf16[3,64,1024]{2,1,0:T(8,128)(2,1)}, bf16[3,64,1024]{2,1,0:T(8,128)(2,1)S(1)}, u32[]{:S(2)}, u32[]{:S(2)}) collective-permute-start(bf16[3,64,1024]{2,1,0:T(8,128)(2,1)} %slice.19), channel_id=1, source_target_pairs={{0,7},{1,0},{2,1},{3,2},{4,3},{5,4},{6,5},{7,6},{8,15},{9,8},{10,9... | collective-permute-start | bytes 1179656 | tf_op jit(solution)/shard_map/ppermute | solution.py:382
  112.9 16.0 %collective-permute-start.12 = (bf16[3,512,128]{2,1,0:T(8,128)(2,1)}, bf16[3,512,128]{2,1,0:T(8,128)(2,1)S(1)}, u32[]{:S(2)}, u32[]{:S(2)}) collective-permute-start(bf16[3,512,128]{2,1,0:T(8,128)(2,1)} %slice.16), channel_id=1, source_target_pairs={{0,1},{1,2},{2,3},{3,4},{4,5},{5,6},{6,7},{7,0},{8,9},{9,10},{10,1... | collective-permute-start | bytes 1179656 | tf_op jit(solution)/shard_map/ppermute | solution.py:381
  113.7 15.2 %collective-permute-start.13 = (bf16[3,512,128]{2,1,0:T(8,128)(2,1)}, bf16[3,512,128]{2,1,0:T(8,128)(2,1)S(1)}, u32[]{:S(2)}, u32[]{:S(2)}) collective-permute-start(bf16[3,512,128]{2,1,0:T(8,128)(2,1)} %slice.17), channel_id=1, source_target_pairs={{0,7},{1,0},{2,1},{3,2},{4,3},{5,4},{6,5},{7,6},{8,15},{9,8},{10,9... | collective-permute-start | bytes 1179656 | tf_op jit(solution)/shard_map/ppermute | solution.py:382
  132.2 10.1 %collective-permute-start.16 = (bf16[400,128]{1,0:T(8,128)(2,1)S(1)}, bf16[400,128]{1,0:T(8,128)(2,1)S(1)}, u32[]{:S(2)}, u32[]{:S(2)}) collective-permute-start(bf16[400,128]{1,0:T(8,128)(2,1)S(1)} %get-tuple-element.20), channel_id=1, source_target_pairs={{0,1},{1,2},{2,3},{3,4},{4,5},{5,6},{6,7},{7,0},{8,9},{9,10},{10,1... | collective-permute-start | bytes 307208 | tf_op jit(solution)/shard_map/ppermute | solution.py:402
  132.3 10.3 %collective-permute-start.17 = (bf16[400,128]{1,0:T(8,128)(2,1)S(1)}, bf16[400,128]{1,0:T(8,128)(2,1)S(1)}, u32[]{:S(2)}, u32[]{:S(2)}) collective-permute-start(bf16[400,128]{1,0:T(8,128)(2,1)S(1)} %get-tuple-element.21), channel_id=1, source_target_pairs={{0,2},{1,3},{2,4},{3,5},{4,6},{5,7},{6,0},{7,1},{8,10},{9,11},{10,... | collective-permute-start | bytes 307208 | tf_op jit(solution)/shard_map/ppermute | solution.py:402
  134.5 10.6 %collective-permute-start.18 = (bf16[400,128]{1,0:T(8,128)(2,1)S(1)}, bf16[400,128]{1,0:T(8,128)(2,1)S(1)}, u32[]{:S(2)}, u32[]{:S(2)}) collective-permute-start(bf16[400,128]{1,0:T(8,128)(2,1)S(1)} %get-tuple-element.22), channel_id=1, source_target_pairs={{0,3},{1,4},{2,5},{3,6},{4,7},{5,0},{6,1},{7,2},{8,11},{9,12},{10,... | collective-permute-start | bytes 307208 | tf_op jit(solution)/shard_map/ppermute | solution.py:402
  135.7 11.7 %collective-permute-start.19 = (bf16[400,128]{1,0:T(8,128)(2,1)S(1)}, bf16[400,128]{1,0:T(8,128)(2,1)S(1)}, u32[]{:S(2)}, u32[]{:S(2)}) collective-permute-start(bf16[400,128]{1,0:T(8,128)(2,1)S(1)} %get-tuple-element.23), channel_id=1, source_target_pairs={{0,4},{1,5},{2,6},{3,7},{4,0},{5,1},{6,2},{7,3},{8,12},{9,13},{10,... | collective-permute-start | bytes 307208 | tf_op jit(solution)/shard_map/ppermute | solution.py:402
  137.9 10.1 %collective-permute-start.20 = (bf16[400,128]{1,0:T(8,128)(2,1)S(1)}, bf16[400,128]{1,0:T(8,128)(2,1)S(1)}, u32[]{:S(2)}, u32[]{:S(2)}) collective-permute-start(bf16[400,128]{1,0:T(8,128)(2,1)S(1)} %get-tuple-element.24), channel_id=1, source_target_pairs={{0,5},{1,6},{2,7},{3,0},{4,1},{5,2},{6,3},{7,4},{8,13},{9,14},{10,... | collective-permute-start | bytes 307208 | tf_op jit(solution)/shard_map/ppermute | solution.py:402
  142.6 11.4 %collective-permute-start.22 = (bf16[400,128]{1,0:T(8,128)(2,1)S(1)}, bf16[400,128]{1,0:T(8,128)(2,1)S(1)}, u32[]{:S(2)}, u32[]{:S(2)}) collective-permute-start(bf16[400,128]{1,0:T(8,128)(2,1)S(1)} %get-tuple-element.26), channel_id=1, source_target_pairs={{0,7},{1,0},{2,1},{3,2},{4,3},{5,4},{6,5},{7,6},{8,15},{9,8},{10,9... | collective-permute-start | bytes 307208 | tf_op jit(solution)/shard_map/ppermute | solution.py:402
  155.1 28.8 %all-to-all-start.1 = ((bf16[32,112,128]{2,1,0:T(8,128)(2,1)}), bf16[32,112,128]{2,1,0:T(8,128)(2,1)S(1)}, u32[]{:S(2)}, u32[]{:S(2)}) async-start(bf16[32,112,128]{2,1,0:T(8,128)(2,1)} %scale.1), calls=%async_computation.1 | async-start | bytes 1835008 | tf_op jit(solution)/shard_map/all_to_all | solution.py:404
  (16 other events, 310.3 us)

commit v5 on v4

--- a/solution.py
+++ b/solution.py
@@ -186,18 +186,28 @@
 
 
 def precondition_kernel(place_ref, left_ref, adam_ref, part_ref, *refs):
-    out_refs, sums_ref = refs[4:12], refs[12]
+    out_refs, sums_ref, near_ref, arrived = refs[4:12], refs[12], refs[13], refs[14]
     count = pl.num_programs(0)
     step = pl.program_id(0)
+
+    def fetch(slot):
+        return pltpu.make_async_copy(part_ref.at[slot], near_ref.at[slot], arrived.at[slot])
+
+    @pl.when(step == 0)
+    def _():
+        for slot in range(part_ref.shape[0]):
+            fetch(slot).start()
+
     rows = pl.ds(pl.multiple_of(step * 128, 128), 128)
     panel = jnp.concatenate([refs[0][...], refs[1][...]], axis=0)
     half = jnp.dot(left_ref[...], panel, preferred_element_type=F32).astype(BF16)
+    fetch(step).wait()
     square = jnp.zeros((1, 128), F32)
     largest = jnp.zeros((1, 128), F32)
     for k in range(8):
         column = pl.ds(pl.multiple_of(lax.rem(place_ref[0] + k, 8) * 128, 128), 128)
         root = jnp.concatenate([refs[2][:, column], refs[3][:, column]], axis=0)
-        pre = part_ref[:, column] + jnp.dot(half, root, preferred_element_type=F32)
+        pre = near_ref[step, :, column] + jnp.dot(half, root, preferred_element_type=F32)
         out_refs[k][rows, :] = pre.astype(BF16)
         square = square + jnp.sum(pre * pre, axis=0, keepdims=True)
         largest = jnp.maximum(largest, jnp.max(jnp.abs(pre), axis=0, keepdims=True))
@@ -235,11 +245,16 @@
         precondition_kernel,
         out_shape=[jax.ShapeDtypeStruct(out, BF16)] * 8,
         grid=(count,),
-        in_specs=[scalars(), slot_of(left_root.shape), whole(adam.shape), slot_of(part.shape)]
+        in_specs=[scalars(), slot_of(left_root.shape), whole(adam.shape)]
+        + [pl.BlockSpec(memory_space=pltpu.HBM)]
         + [slot_of(panel.shape) for panel in late],
         out_specs=[whole(out)] * 8,
-        scratch_shapes=[pltpu.VMEM((1, 128), F32)],
-        compiler_params=params(16),
+        scratch_shapes=[
+            pltpu.VMEM((1, 128), F32),
+            pltpu.VMEM(part.shape, F32),
+            pltpu.SemaphoreType.DMA((count,)),
+        ],
+        compiler_params=params(60),
         cost_estimate=cost(count * 4 * rows * 128 * order, count * 4 * rows * order),
         name="precondition",
     )(place, left_root, adam, part, *late)

time: 186 us -> 191 us (1.027)
  waiting for transfers between devices: 96.5 us -> 91.6 us
  local copies, waits for them, and re-layouts: 4.19 us -> 7.81 us
  Pallas kernels: 24.1 us -> 27.6 us
  starting transfers between devices: 60.5 us -> 62.6 us
    pallas_call x1, Pallas kernels: 1.57 us -> 5.21 us  [precondition(): pl.pallas_call(precondition_kernel, out_shape=[jax.ShapeDtypeStruct(out,...]
    ppermute x6, waiting for transfers between devices: 40 us -> 37.3 us  [ring(): from_below.append(lax.ppermute(from_below[-1], 'mp', up))]
    ppermute x7, waiting for transfers between devices: 10 us -> 7.63 us  [shards(): gots[k] = lax.ppermute(sents[k], 'mp', [(i, (i + k) % 8) for i in range(8)])]
    all_to_all x2, starting transfers between devices: 22 us -> 24.2 us  [shards(): got = lax.all_to_all(sent, 'dp', split_axis=0, concat_axis=0, tiled=True)]
  transfers between devices with their start and end apart: 25 -> 25, of which waited for: 15 -> 15; matrix products, arithmetic and copies ran while one was open for 1% -> 3% of each run, Pallas kernels for 10% -> 10%
where the time goes in v5:
time: 191 us; the launch traced here: 190 us
  waiting for transfers between devices  91.6 us (48%)
  starting transfers between devices  62.6 us (33%)
  Pallas kernels  27.6 us (14%)
  local copies, waits for them, and re-layouts  7.81 us (4%)
    ppermute x6, waiting for transfers between devices, ring(): from_below.append(lax.ppermute(from_below[-1], 'mp', up))  37.3 us
    all_to_all x2, starting transfers between devices, shards(): got = lax.all_to_all(sent, 'dp', split_axis=0, concat_axis=0, tiled=True)  24.2 us
    ppermute x6, waiting for transfers between devices, ring(): from_above.append(lax.ppermute(from_above[-1], 'mp', down))  21.6 us
    ppermute x6, starting transfers between devices, ring(): from_above.append(lax.ppermute(from_above[-1], 'mp', down))  21.3 us
    all_to_all x2, waiting for transfers between devices, shards(): got = lax.all_to_all(sent, 'dp', split_axis=0, concat_axis=0, tiled=True)  19.4 us
    ppermute x7, starting transfers between devices, shards(): gots[k] = lax.ppermute(sents[k], 'mp', [(i, (i + k) % 8) for i in range(8)])  11.7 us
    ppermute x7, waiting for transfers between devices, shards(): gots[k] = lax.ppermute(sents[k], 'mp', [(i, (i + k) % 8) for i in range(8)])  7.63 us
    pallas_call x1, Pallas kernels, factors(): pl.pallas_call(factors_kernel, out_shape=[jax.ShapeDtypeStruct(left_stat....  7.21 us
  transfers between devices with their start and end apart: 25, of which 15 were waited for; matrix products, arithmetic and copies ran while one was open for 3% of the time, Pallas kernels for 10%

profile of v5, /device:TPU:1, one launch (start us, length us, event | category | flops | bytes accessed | tf_op | source)
XLA Modules:
  0.0 190.4 jit_solution(2784909494343884812)
XLA Ops:
  0.6 6.5 %collective-permute-start = (bf16[3,128,1024]{2,1,0:T(8,128)(2,1)}, bf16[3,128,1024]{2,1,0:T(8,128)(2,1)S(1)}, u32[]{:S(2)}, u32[]{:S(2)}) collective-permute-start(bf16[3,128,1024]{2,1,0:T(8,128)(2,1)} %refs_7_.1), channel_id=1, source_target_pairs={{0,7},{1,0},{2,1},{3,2},{4,3},{5,4},{6,5},{7,6},{8,15},{9,8},{10,9... | collective-permute-start | bytes 2359304 | tf_op jit(solution)/shard_map/ppermute | solution.py:392
  7.1 16.5 %collective-permute-done.refs_8_ = bf16[3,128,1024]{2,1,0:T(8,128)(2,1)S(1)} collective-permute-done((bf16[3,128,1024]{2,1,0:T(8,128)(2,1)}, bf16[3,128,1024]{2,1,0:T(8,128)(2,1)S(1)}, u32[]{:S(2)}, u32[]{:S(2)}) %collective-permute-start) | collective-permute-done | bytes 786464 | tf_op jit(solution)/shard_map/ppermute | solution.py:392
  23.6 3.3 %collective-permute-start.1 = (bf16[3,128,1024]{2,1,0:T(8,128)(2,1)S(1)}, bf16[3,128,1024]{2,1,0:T(8,128)(2,1)}, u32[]{:S(2)}, u32[]{:S(2)}) collective-permute-start(bf16[3,128,1024]{2,1,0:T(8,128)(2,1)S(1)} %collective-permute-done.refs_8_), channel_id=1, source_target_pairs={{0,7},{1,0},{2,1},{3,2},{4,3},{5,4},{6,5},{7,6},{8,15},{9,8},{10,9... | collective-permute-start | bytes 2359304 | tf_op jit(solution)/shard_map/ppermute | solution.py:392
  27.0 5.0 %prepare.1 = bf16[32,112,128]{2,1,0:T(8,128)(2,1)} custom-call(s32[96]{0:T(128)} %slot_ref.3, bf16[96,32,128]{2,1,0:T(8,128)(2,1)} %grad_ref.1, f32[96,32,128]{2,1,0:T(8,128)} %one_ref.1, f32[96,32,128]{2,1,0:T(8,128)} %two_ref.1), custom_call_target="tpu_custom_call" | custom-call | flops 7864320 | bytes 4718592 | tf_op jit(solution)/shard_map/prepare/pallas_call | solution.py:81
  31.9 8.9 %all-to-all-start = ((bf16[32,112,128]{2,1,0:T(8,128)(2,1)}), bf16[32,112,128]{2,1,0:T(8,128)(2,1)S(1)}, u32[]{:S(2)}, u32[]{:S(2)}) async-start(bf16[32,112,128]{2,1,0:T(8,128)(2,1)} %prepare.1), calls=%async_computation | async-start | bytes 1835008 | tf_op jit(solution)/shard_map/all_to_all | solution.py:409
  42.2 3.5 %collective-permute-start.2 = (bf16[3,128,1024]{2,1,0:T(8,128)(2,1)}, bf16[3,128,1024]{2,1,0:T(8,128)(2,1)S(1)}, u32[]{:S(2)}, u32[]{:S(2)}) collective-permute-start(bf16[3,128,1024]{2,1,0:T(8,128)(2,1)} %collective-permute-done.1.refs_9_), channel_id=1, source_target_pairs={{0,7},{1,0},{2,1},{3,2},{4,3},{5,4},{6,5},{7,6},{8,15},{9,8},{10,9... | collective-permute-start | bytes 2359304 | tf_op jit(solution)/shard_map/ppermute | solution.py:392
  45.8 10.8 %all-to-all-done.got_ref = bf16[32,112,128]{2,1,0:T(8,128)(2,1)S(1)} async-done(((bf16[32,112,128]{2,1,0:T(8,128)(2,1)}), bf16[32,112,128]{2,1,0:T(8,128)(2,1)S(1)}, u32[]{:S(2)}, u32[]{:S(2)}) %all-to-all-start) | async-done | bytes 917536 | tf_op jit(solution)/shard_map/all_to_all | solution.py:409
  56.7 3.7 %collective-permute-done.2.refs_10_ = bf16[3,128,1024]{2,1,0:T(8,128)(2,1)S(1)} collective-permute-done((bf16[3,128,1024]{2,1,0:T(8,128)(2,1)}, bf16[3,128,1024]{2,1,0:T(8,128)(2,1)S(1)}, u32[]{:S(2)}, u32[]{:S(2)}) %collective-permute-start.2) | collective-permute-done | bytes 786464 | tf_op jit(solution)/shard_map/ppermute | solution.py:392
  60.4 3.0 %collective-permute-done.5.refs_11_ = bf16[3,128,1024]{2,1,0:T(8,128)(2,1)S(1)} collective-permute-done((bf16[3,128,1024]{2,1,0:T(8,128)(2,1)}, bf16[3,128,1024]{2,1,0:T(8,128)(2,1)S(1)}, u32[]{:S(2)}, u32[]{:S(2)}) %collective-permute-start.5) | collective-permute-done | bytes 786464 | tf_op jit(solution)/shard_map/ppermute | solution.py:391
  64.4 2.7 %collective-permute-start.6 = (bf16[3,1024,128]{2,1,0:T(8,128)(2,1)S(1)}, bf16[3,1024,128]{2,1,0:T(8,128)(2,1)S(1)}, u32[]{:S(2)}, u32[]{:S(2)}) collective-permute-start(bf16[3,1024,128]{2,1,0:T(8,128)(2,1)S(1)} %get-tuple-element.18.refs_0_), channel_id=1, source_target_pairs={{0,7},{1,0},{2,1},{3,2},{4,3},{5,4},{6,5},{7,6},{8,15},{9,8},{10,9... | collective-permute-start | bytes 2359304 | tf_op jit(solution)/shard_map/ppermute | solution.py:392
  67.1 13.9 %collective-permute-done.9.refs_6_.refs_8_ = bf16[3,1024,128]{2,1,0:T(8,128)(2,1)S(1)} collective-permute-done((bf16[3,1024,128]{2,1,0:T(8,128)(2,1)S(1)}, bf16[3,1024,128]{2,1,0:T(8,128)(2,1)S(1)}, u32[]{:S(2)}, u32[]{:S(2)}) %collective-permute-start.9) | collective-permute-done | bytes 786464 | tf_op jit(solution)/shard_map/ppermute | solution.py:391
  81.0 2.7 %collective-permute-start.7 = (bf16[3,1024,128]{2,1,0:T(8,128)(2,1)S(1)}, bf16[3,1024,128]{2,1,0:T(8,128)(2,1)S(1)}, u32[]{:S(2)}, u32[]{:S(2)}) collective-permute-start(bf16[3,1024,128]{2,1,0:T(8,128)(2,1)S(1)} %collective-permute-done.6.refs_1_), channel_id=1, source_target_pairs={{0,7},{1,0},{2,1},{3,2},{4,3},{5,4},{6,5},{7,6},{8,15},{9,8},{10,9... | collective-permute-start | bytes 2359304 | tf_op jit(solution)/shard_map/ppermute | solution.py:392
  83.6 13.3 %collective-permute-done.10.refs_5_.refs_7_ = bf16[3,1024,128]{2,1,0:T(8,128)(2,1)S(1)} collective-permute-done((bf16[3,1024,128]{2,1,0:T(8,128)(2,1)S(1)}, bf16[3,1024,128]{2,1,0:T(8,128)(2,1)S(1)}, u32[]{:S(2)}, u32[]{:S(2)}) %collective-permute-start.10) | collective-permute-done | bytes 786464 | tf_op jit(solution)/shard_map/ppermute | solution.py:391
  97.0 2.7 %collective-permute-start.8 = (bf16[3,1024,128]{2,1,0:T(8,128)(2,1)S(1)}, bf16[3,1024,128]{2,1,0:T(8,128)(2,1)S(1)}, u32[]{:S(2)}, u32[]{:S(2)}) collective-permute-start(bf16[3,1024,128]{2,1,0:T(8,128)(2,1)S(1)} %collective-permute-done.7.refs_2_), channel_id=1, source_target_pairs={{0,7},{1,0},{2,1},{3,2},{4,3},{5,4},{6,5},{7,6},{8,15},{9,8},{10,9... | collective-permute-start | bytes 2359304 | tf_op jit(solution)/shard_map/ppermute | solution.py:392
  103.2 2.7 %collective-permute-start.15 = (bf16[3,64,1024]{2,1,0:T(8,128)(2,1)}, bf16[3,64,1024]{2,1,0:T(8,128)(2,1)}, u32[]{:S(2)}, u32[]{:S(2)}) collective-permute-start(bf16[3,64,1024]{2,1,0:T(8,128)(2,1)} %slice.19), channel_id=1, source_target_pairs={{0,7},{1,0},{2,1},{3,2},{4,3},{5,4},{6,5},{7,6},{8,15},{9,8},{10,9... | collective-permute-start | bytes 1179656 | tf_op jit(solution)/shard_map/ppermute | solution.py:397
  105.9 7.1 %collective-permute-done.11.refs_4_.refs_6_ = bf16[3,1024,128]{2,1,0:T(8,128)(2,1)S(1)} collective-permute-done((bf16[3,1024,128]{2,1,0:T(8,128)(2,1)S(1)}, bf16[3,1024,128]{2,1,0:T(8,128)(2,1)S(1)}, u32[]{:S(2)}, u32[]{:S(2)}) %collective-permute-start.11) | collective-permute-done | bytes 786464 | tf_op jit(solution)/shard_map/ppermute | solution.py:391
  117.3 6.9 %bulk.1.part_ref = f32[3,128,1024]{2,1,0:T(8,128)} custom-call(bf16[3,128,1024]{2,1,0:T(8,128)(2,1)} %left_ref.4, bf16[3,1024,128]{2,1,0:T(8,128)(2,1)} %copy-done, bf16[3,1024,128]{2,1,0:T(8,128)(2,1)} %copy-done.7, bf16[3,1024,128]{2,1,0:T(8,128)(2,1)} %copy-done.9, bf16[3,1024,128]{2,1,0:T(8,128)(2,1)} %copy-done.5, bf16[3,1024,128]{2,1,0:T(8,128)(2,1)} %copy-done.4, ...), custom_call_target="tpu_custom_call" | custom-call | flops 1610612736 | bytes 15728640 | tf_op jit(solution)/shard_map/bulk/pallas_call | solution.py:176
  124.3 5.6 %collective-permute-done.12.refs_0_.refs_4_ = bf16[3,512,128]{2,1,0:T(8,128)(2,1)S(1)} collective-permute-done((bf16[3,512,128]{2,1,0:T(8,128)(2,1)}, bf16[3,512,128]{2,1,0:T(8,128)(2,1)S(1)}, u32[]{:S(2)}, u32[]{:S(2)}) %collective-permute-start.12) | collective-permute-done | bytes 393248 | tf_op jit(solution)/shard_map/ppermute | solution.py:396
  130.7 5.2 %precondition.1 = (bf16[400,128]{1,0:T(8,128)(2,1)}, bf16[400,128]{1,0:T(8,128)(2,1)}, bf16[400,128]{1,0:T(8,128)(2,1)}, bf16[400,128]{1,0:T(8,128)(2,1)}, bf16[...) custom-call(s32[1]{0:T(128)} %bitcast.place_ref, ...), custom_call_target="tpu_custom_call" | custom-call | flops 201326592 | bytes 1572864 | tf_op jit(solution)/shard_map/precondition/pallas_call | solution.py:244
  138.8 2.9 %collective-permute-start.19 = (bf16[400,128]{1,0:T(8,128)(2,1)}, bf16[400,128]{1,0:T(8,128)(2,1)S(1)}, u32[]{:S(2)}, u32[]{:S(2)}) collective-permute-start(bf16[400,128]{1,0:T(8,128)(2,1)} %get-tuple-element.23), channel_id=1, source_target_pairs={{0,4},{1,5},{2,6},{3,7},{4,0},{5,1},{6,2},{7,3},{8,12},{9,13},{10,... | collective-permute-start | bytes 307208 | tf_op jit(solution)/shard_map/ppermute | solution.py:417
  141.6 3.7 %collective-permute-start.20 = (bf16[400,128]{1,0:T(8,128)(2,1)}, bf16[400,128]{1,0:T(8,128)(2,1)S(1)}, u32[]{:S(2)}, u32[]{:S(2)}) collective-permute-start(bf16[400,128]{1,0:T(8,128)(2,1)} %get-tuple-element.24), channel_id=1, source_target_pairs={{0,5},{1,6},{2,7},{3,0},{4,1},{5,2},{6,3},{7,4},{8,13},{9,14},{10,... | collective-permute-start | bytes 307208 | tf_op jit(solution)/shard_map/ppermute | solution.py:417
  157.3 15.3 %all-to-all-start.1 = ((bf16[32,112,128]{2,1,0:T(8,128)(2,1)}), bf16[32,112,128]{2,1,0:T(8,128)(2,1)S(1)}, u32[]{:S(2)}, u32[]{:S(2)}) async-start(bf16[32,112,128]{2,1,0:T(8,128)(2,1)} %scale.1), calls=%async_computation.1 | async-start | bytes 1835008 | tf_op jit(solution)/shard_map/all_to_all | solution.py:419
  172.6 7.2 %factors.1 = (f32[3,128,1024]{2,1,0:T(8,128)}, f32[3,128,1024]{2,1,0:T(8,128)}) custom-call(s32[1]{0:T(128)} %bitcast.place_ref, f32[3,128,1024]{2,1,0:T(8,128)} %left_ref.5, f32[3,128,1024]{2,1,0:T(8,128)} %right_ref.1, bf16[3,1024,128]{2,1,0:T(8,128)(2,1)} %copy-done, bf16[3,1024,128]{2,1,0:T(8,128)(2,1)} %copy-done.7, bf16[3,1024,128]{2,1,0:T(8,128)(2,1)} %copy-done.9, ...), custom_call_target="tpu_custom_call" | custom-call | flops 1610612736 | bytes 12582912 | tf_op jit(solution)/shard_map/factors/pallas_call | solution.py:373
  179.8 8.5 %all-to-all-done.1.got_ref = bf16[32,112,128]{2,1,0:T(8,128)(2,1)S(1)} async-done(((bf16[32,112,128]{2,1,0:T(8,128)(2,1)}), bf16[32,112,128]{2,1,0:T(8,128)(2,1)S(1)}, u32[]{:S(2)}, u32[]{:S(2)}) %all-to-all-start.1) | async-done | bytes 917536 | tf_op jit(solution)/shard_map/all_to_all | solution.py:419
  (65 shorter events, 28.0 us)
Async XLA Ops:
  0.6 23.0 %collective-permute-start = (bf16[3,128,1024]{2,1,0:T(8,128)(2,1)}, bf16[3,128,1024]{2,1,0:T(8,128)(2,1)S(1)}, u32[]{:S(2)}, u32[]{:S(2)}) collective-permute-start(bf16[3,128,1024]{2,1,0:T(8,128)(2,1)} %refs_7_.1), channel_id=1, source_target_pairs={{0,7},{1,0},{2,1},{3,2},{4,3},{5,4},{6,5},{7,6},{8,15},{9,8},{10,9... | collective-permute-start | bytes 2359304 | tf_op jit(solution)/shard_map/ppermute | solution.py:392
  7.1 19.8 %collective-permute-start.3 = (bf16[3,128,1024]{2,1,0:T(8,128)(2,1)}, bf16[3,128,1024]{2,1,0:T(8,128)(2,1)}, u32[]{:S(2)}, u32[]{:S(2)}) collective-permute-start(bf16[3,128,1024]{2,1,0:T(8,128)(2,1)} %refs_7_.1), channel_id=1, source_target_pairs={{0,1},{1,2},{2,3},{3,4},{4,5},{5,6},{6,7},{7,0},{8,9},{9,10},{10,1... | collective-permute-start | bytes 2359304 | tf_op jit(solution)/shard_map/ppermute | solution.py:391
  23.6 18.6 %collective-permute-start.1 = (bf16[3,128,1024]{2,1,0:T(8,128)(2,1)S(1)}, bf16[3,128,1024]{2,1,0:T(8,128)(2,1)}, u32[]{:S(2)}, u32[]{:S(2)}) collective-permute-start(bf16[3,128,1024]{2,1,0:T(8,128)(2,1)S(1)} %collective-permute-done.refs_8_), channel_id=1, source_target_pairs={{0,7},{1,0},{2,1},{3,2},{4,3},{5,4},{6,5},{7,6},{8,15},{9,8},{10,9... | collective-permute-start | bytes 2359304 | tf_op jit(solution)/shard_map/ppermute | solution.py:392
  26.9 18.8 %collective-permute-start.4 = (bf16[3,128,1024]{2,1,0:T(8,128)(2,1)}, bf16[3,128,1024]{2,1,0:T(8,128)(2,1)}, u32[]{:S(2)}, u32[]{:S(2)}) collective-permute-start(bf16[3,128,1024]{2,1,0:T(8,128)(2,1)} %collective-permute-done.3.refs_13_), channel_id=1, source_target_pairs={{0,1},{1,2},{2,3},{3,4},{4,5},{5,6},{6,7},{7,0},{8,9},{9,10},{10,1... | collective-permute-start | bytes 2359304 | tf_op jit(solution)/shard_map/ppermute | solution.py:391
  31.9 24.7 %all-to-all-start = ((bf16[32,112,128]{2,1,0:T(8,128)(2,1)}), bf16[32,112,128]{2,1,0:T(8,128)(2,1)S(1)}, u32[]{:S(2)}, u32[]{:S(2)}) async-start(bf16[32,112,128]{2,1,0:T(8,128)(2,1)} %prepare.1), calls=%async_computation | async-start | bytes 1835008 | tf_op jit(solution)/shard_map/all_to_all | solution.py:409
  42.2 18.2 %collective-permute-start.2 = (bf16[3,128,1024]{2,1,0:T(8,128)(2,1)}, bf16[3,128,1024]{2,1,0:T(8,128)(2,1)S(1)}, u32[]{:S(2)}, u32[]{:S(2)}) collective-permute-start(bf16[3,128,1024]{2,1,0:T(8,128)(2,1)} %collective-permute-done.1.refs_9_), channel_id=1, source_target_pairs={{0,7},{1,0},{2,1},{3,2},{4,3},{5,4},{6,5},{7,6},{8,15},{9,8},{10,9... | collective-permute-start | bytes 2359304 | tf_op jit(solution)/shard_map/ppermute | solution.py:392
  45.8 17.7 %collective-permute-start.5 = (bf16[3,128,1024]{2,1,0:T(8,128)(2,1)}, bf16[3,128,1024]{2,1,0:T(8,128)(2,1)S(1)}, u32[]{:S(2)}, u32[]{:S(2)}) collective-permute-start(bf16[3,128,1024]{2,1,0:T(8,128)(2,1)} %collective-permute-done.4.refs_12_), channel_id=1, source_target_pairs={{0,1},{1,2},{2,3},{3,4},{4,5},{5,6},{6,7},{7,0},{8,9},{9,10},{10,1... | collective-permute-start | bytes 2359304 | tf_op jit(solution)/shard_map/ppermute | solution.py:391
  64.4 16.6 %collective-permute-start.9 = (bf16[3,1024,128]{2,1,0:T(8,128)(2,1)S(1)}, bf16[3,1024,128]{2,1,0:T(8,128)(2,1)S(1)}, u32[]{:S(2)}, u32[]{:S(2)}) collective-permute-start(bf16[3,1024,128]{2,1,0:T(8,128)(2,1)S(1)} %get-tuple-element.18.refs_0_), channel_id=1, source_target_pairs={{0,1},{1,2},{2,3},{3,4},{4,5},{5,6},{6,7},{7,0},{8,9},{9,10},{10,1... | collective-permute-start | bytes 2359304 | tf_op jit(solution)/shard_map/ppermute | solution.py:391
  64.4 16.6 %collective-permute-start.6 = (bf16[3,1024,128]{2,1,0:T(8,128)(2,1)S(1)}, bf16[3,1024,128]{2,1,0:T(8,128)(2,1)S(1)}, u32[]{:S(2)}, u32[]{:S(2)}) collective-permute-start(bf16[3,1024,128]{2,1,0:T(8,128)(2,1)S(1)} %get-tuple-element.18.refs_0_), channel_id=1, source_target_pairs={{0,7},{1,0},{2,1},{3,2},{4,3},{5,4},{6,5},{7,6},{8,15},{9,8},{10,9... | collective-permute-start | bytes 2359304 | tf_op jit(solution)/shard_map/ppermute | solution.py:392
  81.0 16.0 %collective-permute-start.10 = (bf16[3,1024,128]{2,1,0:T(8,128)(2,1)S(1)}, bf16[3,1024,128]{2,1,0:T(8,128)(2,1)S(1)}, u32[]{:S(2)}, u32[]{:S(2)}) collective-permute-start(bf16[3,1024,128]{2,1,0:T(8,128)(2,1)S(1)} %collective-permute-done.9.refs_6_.refs_8_), channel_id=1, source_target_pairs={{0,1},{1,2},{2,3},{3,4},{4,5},{5,6},{6,7},{7,0},{8,9},{9,10},{10,1... | collective-permute-start | bytes 2359304 | tf_op jit(solution)/shard_map/ppermute | solution.py:391
  81.0 16.0 %collective-permute-start.7 = (bf16[3,1024,128]{2,1,0:T(8,128)(2,1)S(1)}, bf16[3,1024,128]{2,1,0:T(8,128)(2,1)S(1)}, u32[]{:S(2)}, u32[]{:S(2)}) collective-permute-start(bf16[3,1024,128]{2,1,0:T(8,128)(2,1)S(1)} %collective-permute-done.6.refs_1_), channel_id=1, source_target_pairs={{0,7},{1,0},{2,1},{3,2},{4,3},{5,4},{6,5},{7,6},{8,15},{9,8},{10,9... | collective-permute-start | bytes 2359304 | tf_op jit(solution)/shard_map/ppermute | solution.py:392
  97.0 16.0 %collective-permute-start.11 = (bf16[3,1024,128]{2,1,0:T(8,128)(2,1)S(1)}, bf16[3,1024,128]{2,1,0:T(8,128)(2,1)S(1)}, u32[]{:S(2)}, u32[]{:S(2)}) collective-permute-start(bf16[3,1024,128]{2,1,0:T(8,128)(2,1)S(1)} %collective-permute-done.10.refs_5_.refs_7_), channel_id=1, source_target_pairs={{0,1},{1,2},{2,3},{3,4},{4,5},{5,6},{6,7},{7,0},{8,9},{9,10},{10,1... | collective-permute-start | bytes 2359304 | tf_op jit(solution)/shard_map/ppermute | solution.py:391
  97.0 16.8 %collective-permute-start.8 = (bf16[3,1024,128]{2,1,0:T(8,128)(2,1)S(1)}, bf16[3,1024,128]{2,1,0:T(8,128)(2,1)S(1)}, u32[]{:S(2)}, u32[]{:S(2)}) collective-permute-start(bf16[3,1024,128]{2,1,0:T(8,128)(2,1)S(1)} %collective-permute-done.7.refs_2_), channel_id=1, source_target_pairs={{0,7},{1,0},{2,1},{3,2},{4,3},{5,4},{6,5},{7,6},{8,15},{9,8},{10,9... | collective-permute-start | bytes 2359304 | tf_op jit(solution)/shard_map/ppermute | solution.py:392
  101.4 22.8 %collective-permute-start.14 = (bf16[3,64,1024]{2,1,0:T(8,128)(2,1)}, bf16[3,64,1024]{2,1,0:T(8,128)(2,1)}, u32[]{:S(2)}, u32[]{:S(2)}) collective-permute-start(bf16[3,64,1024]{2,1,0:T(8,128)(2,1)} %slice.18), channel_id=1, source_target_pairs={{0,1},{1,2},{2,3},{3,4},{4,5},{5,6},{6,7},{7,0},{8,9},{9,10},{10,1... | collective-permute-start | bytes 1179656 | tf_op jit(solution)/shard_map/ppermute | solution.py:396
  103.2 21.1 %collective-permute-start.15 = (bf16[3,64,1024]{2,1,0:T(8,128)(2,1)}, bf16[3,64,1024]{2,1,0:T(8,128)(2,1)}, u32[]{:S(2)}, u32[]{:S(2)}) collective-permute-start(bf16[3,64,1024]{2,1,0:T(8,128)(2,1)} %slice.19), channel_id=1, source_target_pairs={{0,7},{1,0},{2,1},{3,2},{4,3},{5,4},{6,5},{7,6},{8,15},{9,8},{10,9... | collective-permute-start | bytes 1179656 | tf_op jit(solution)/shard_map/ppermute | solution.py:397
  113.8 16.1 %collective-permute-start.12 = (bf16[3,512,128]{2,1,0:T(8,128)(2,1)}, bf16[3,512,128]{2,1,0:T(8,128)(2,1)S(1)}, u32[]{:S(2)}, u32[]{:S(2)}) collective-permute-start(bf16[3,512,128]{2,1,0:T(8,128)(2,1)} %slice.16), channel_id=1, source_target_pairs={{0,1},{1,2},{2,3},{3,4},{4,5},{5,6},{6,7},{7,0},{8,9},{9,10},{10,1... | collective-permute-start | bytes 1179656 | tf_op jit(solution)/shard_map/ppermute | solution.py:396
  114.6 15.3 %collective-permute-start.13 = (bf16[3,512,128]{2,1,0:T(8,128)(2,1)}, bf16[3,512,128]{2,1,0:T(8,128)(2,1)}, u32[]{:S(2)}, u32[]{:S(2)}) collective-permute-start(bf16[3,512,128]{2,1,0:T(8,128)(2,1)} %slice.17), channel_id=1, source_target_pairs={{0,7},{1,0},{2,1},{3,2},{4,3},{5,4},{6,5},{7,6},{8,15},{9,8},{10,9... | collective-permute-start | bytes 1179656 | tf_op jit(solution)/shard_map/ppermute | solution.py:397
  135.9 9.5 %collective-permute-start.16 = (bf16[400,128]{1,0:T(8,128)(2,1)}, bf16[400,128]{1,0:T(8,128)(2,1)S(1)}, u32[]{:S(2)}, u32[]{:S(2)}) collective-permute-start(bf16[400,128]{1,0:T(8,128)(2,1)} %get-tuple-element.20), channel_id=1, source_target_pairs={{0,1},{1,2},{2,3},{3,4},{4,5},{5,6},{6,7},{7,0},{8,9},{9,10},{10,1... | collective-permute-start | bytes 307208 | tf_op jit(solution)/shard_map/ppermute | solution.py:417
  136.0 10.3 %collective-permute-start.17 = (bf16[400,128]{1,0:T(8,128)(2,1)}, bf16[400,128]{1,0:T(8,128)(2,1)S(1)}, u32[]{:S(2)}, u32[]{:S(2)}) collective-permute-start(bf16[400,128]{1,0:T(8,128)(2,1)} %get-tuple-element.21), channel_id=1, source_target_pairs={{0,2},{1,3},{2,4},{3,5},{4,6},{5,7},{6,0},{7,1},{8,10},{9,11},{10,... | collective-permute-start | bytes 307208 | tf_op jit(solution)/shard_map/ppermute | solution.py:417
  137.6 11.3 %collective-permute-start.18 = (bf16[400,128]{1,0:T(8,128)(2,1)}, bf16[400,128]{1,0:T(8,128)(2,1)S(1)}, u32[]{:S(2)}, u32[]{:S(2)}) collective-permute-start(bf16[400,128]{1,0:T(8,128)(2,1)} %get-tuple-element.22), channel_id=1, source_target_pairs={{0,3},{1,4},{2,5},{3,6},{4,7},{5,0},{6,1},{7,2},{8,11},{9,12},{10,... | collective-permute-start | bytes 307208 | tf_op jit(solution)/shard_map/ppermute | solution.py:417
  138.8 11.3 %collective-permute-start.19 = (bf16[400,128]{1,0:T(8,128)(2,1)}, bf16[400,128]{1,0:T(8,128)(2,1)S(1)}, u32[]{:S(2)}, u32[]{:S(2)}) collective-permute-start(bf16[400,128]{1,0:T(8,128)(2,1)} %get-tuple-element.23), channel_id=1, source_target_pairs={{0,4},{1,5},{2,6},{3,7},{4,0},{5,1},{6,2},{7,3},{8,12},{9,13},{10,... | collective-permute-start | bytes 307208 | tf_op jit(solution)/shard_map/ppermute | solution.py:417
  141.6 9.4 %collective-permute-start.20 = (bf16[400,128]{1,0:T(8,128)(2,1)}, bf16[400,128]{1,0:T(8,128)(2,1)S(1)}, u32[]{:S(2)}, u32[]{:S(2)}) collective-permute-start(bf16[400,128]{1,0:T(8,128)(2,1)} %get-tuple-element.24), channel_id=1, source_target_pairs={{0,5},{1,6},{2,7},{3,0},{4,1},{5,2},{6,3},{7,4},{8,13},{9,14},{10,... | collective-permute-start | bytes 307208 | tf_op jit(solution)/shard_map/ppermute | solution.py:417
  146.3 9.0 %collective-permute-start.22 = (bf16[400,128]{1,0:T(8,128)(2,1)}, bf16[400,128]{1,0:T(8,128)(2,1)S(1)}, u32[]{:S(2)}, u32[]{:S(2)}) collective-permute-start(bf16[400,128]{1,0:T(8,128)(2,1)} %get-tuple-element.26), channel_id=1, source_target_pairs={{0,7},{1,0},{2,1},{3,2},{4,3},{5,4},{6,5},{7,6},{8,15},{9,8},{10,9... | collective-permute-start | bytes 307208 | tf_op jit(solution)/shard_map/ppermute | solution.py:417
  157.3 31.1 %all-to-all-start.1 = ((bf16[32,112,128]{2,1,0:T(8,128)(2,1)}), bf16[32,112,128]{2,1,0:T(8,128)(2,1)S(1)}, u32[]{:S(2)}, u32[]{:S(2)}) async-start(bf16[32,112,128]{2,1,0:T(8,128)(2,1)} %scale.1), calls=%async_computation.1 | async-start | bytes 1835008 | tf_op jit(solution)/shard_map/all_to_all | solution.py:419
  (15 other events, 274.9 us)
